TPU v7x, 256 devices: a whole 4x4x8 slice. The times are simulated.
256 devices in a mesh: half: 4 (over z_lo, core), dev: 64 (over z_hi, x, y).
Axes of the slice: x: 4, y: 4, z: 8 (z_hi: 4, z_lo: 2; z = z_hi * 2 + z_lo), core: 2. Of those that a mesh axis runs over, the one named last changes fastest.
Arguments:
- potential: bfloat16 [1024, 1024], P('dev'), may hold values from 0 to 3
- tilt_ids: int32 [256, 2], P('half'), may hold values from -128 to 128
- beam_index: int32 [256], P('half'), may hold values from 0 to 15
- beam_table: float32 [16, 2], replicated, may hold values from -0.75 to 0.75
- positions: int32 [1024, 2], P('dev'), may hold values from 0 to 1023, as said below
Outputs:
- intensity: float32 [1024, 16, 1024], P('dev', None, 'half')
Inputs may be any that keep to these rules, and one draw needn't show every extreme that they name: `positions`: position p has its row between (p // 16) * 16 and (p // 16) * 16 + 15, the rows of its tile; the second entry is its column.
All inputs are finite; a program needn't handle non-finite values.
Results may differ from a plain program's by a relative error of at most 0.0041.
Values may be sent and summed in bfloat16 or wider, within the bound.
No kernel may reach another device: no remote copies, remote signals or barrier semaphores. Data moves between devices by JAX's collectives and lax.ppermute only.
A program may use at most 128 MiB of HBM per device.

v0:
```python
import math

import jax
import jax.numpy as jnp
from jax import lax
from jax.sharding import PartitionSpec as P

two_pi = 2.0 * math.pi
propagation_rate = 0.6


def split_length(length):
    first_size = 1
    for factor in range(1, math.isqrt(length) + 1):
        if length % factor == 0:
            first_size = factor
    return (first_size, length // first_size)


def phase_table(rows_count, cols_count, modulus, direction):
    product = jnp.mod(
        jnp.arange(rows_count, dtype=jnp.int32)[:, None]
        * jnp.arange(cols_count, dtype=jnp.int32)[None, :],
        modulus,
    )
    angle_table = direction * two_pi * product.astype(jnp.float32) / modulus
    return (jnp.cos(angle_table), jnp.sin(angle_table))


def block_table(cos_part, sin_part):
    return jnp.stack([jnp.stack([cos_part, -sin_part]), jnp.stack([sin_part, cos_part])])


def transform_first(field, direction):
    length = field.shape[1]
    cols_count = field.shape[2]
    first_size, second_size = split_length(length)
    outer_table = block_table(*phase_table(second_size, second_size, second_size, direction))
    twist_re, twist_im = phase_table(second_size, first_size, length, direction)
    inner_table = block_table(*phase_table(first_size, first_size, first_size, direction))
    shaped = field.reshape(2, second_size, first_size, cols_count)
    sectioned = jnp.einsum("ibay,oibc->ocay", shaped, outer_table, precision=lax.Precision.HIGHEST)
    twist_re = twist_re[:, :, None]
    twist_im = twist_im[:, :, None]
    sectioned = jnp.stack(
        [
            sectioned[0] * twist_re - sectioned[1] * twist_im,
            sectioned[0] * twist_im + sectioned[1] * twist_re,
        ]
    )
    result = jnp.einsum("icay,oiad->odcy", sectioned, inner_table, precision=lax.Precision.HIGHEST)
    return result.reshape(2, length, cols_count)


def propagator(grid):
    indices = jnp.arange(grid, dtype=jnp.int32)
    signed = jnp.where(indices < grid // 2, indices, indices - grid)
    squared = signed[:, None] * signed[:, None] + signed[None, :] * signed[None, :]
    kept_mask = 9 * squared < grid * grid
    angle_field = -propagation_rate * squared.astype(jnp.float32) / grid
    return (
        jnp.where(kept_mask, jnp.cos(angle_field), 0.0),
        jnp.where(kept_mask, jnp.sin(angle_field), 0.0),
    )


def mixing_table(tilt_list, beam_list, beam_table, positions, grid):
    levels = beam_table.shape[0]
    selector = (beam_list[:, None] == jnp.arange(levels, dtype=jnp.int32)[None, :]).astype(
        jnp.float32
    )
    weights = jnp.dot(selector, beam_table, precision=lax.Precision.HIGHEST)
    winding = jnp.mod(
        positions[:, 0:1] * tilt_list[None, :, 0] + positions[:, 1:2] * tilt_list[None, :, 1], grid
    )
    coef_angle = two_pi * winding.astype(jnp.float32) / grid
    cosine = jnp.cos(coef_angle)
    sine_part = jnp.sin(coef_angle)
    coef_re = weights[None, :, 0] * cosine + weights[None, :, 1] * sine_part
    coef_im = weights[None, :, 1] * cosine - weights[None, :, 0] * sine_part
    return jnp.stack(
        [jnp.stack([coef_re, -coef_im], 1), jnp.stack([coef_im, coef_re], 1)], 0
    ).astype(jnp.bfloat16)


def local(potential, tilt_ids, beam_index, beam_table, positions):
    grid = potential.shape[1]
    own_tilt = lax.dynamic_slice_in_dim(tilt_ids, lax.axis_index("dev"), 1, 0)[0]
    row_piece = lax.all_gather(potential, "dev", axis=0, tiled=True)
    row_count = row_piece.shape[0]
    row_coord = jnp.arange(row_count, dtype=jnp.int32)
    col_coord = jnp.arange(grid, dtype=jnp.int32)
    winding = jnp.mod(own_tilt[0] * row_coord[:, None] + own_tilt[1] * col_coord[None, :], grid)
    phase_angle = row_piece.astype(jnp.float32) + two_pi * winding.astype(jnp.float32) / grid
    incident = jnp.stack([jnp.cos(phase_angle), jnp.sin(phase_angle)])
    field = transform_first(incident, -1.0)
    field = transform_first(field.transpose(0, 2, 1), -1.0)
    filter_re, filter_im = propagator(grid)
    field = jnp.stack(
        [field[0] * filter_re - field[1] * filter_im, field[0] * filter_im + field[1] * filter_re]
    )
    field = transform_first(field, 1.0)
    field = transform_first(field.transpose(0, 2, 1), 1.0)
    scaling = 1.0 / (grid * grid)
    smatrix = (field * scaling).astype(jnp.bfloat16)[None]
    mixing = mixing_table(tilt_ids, beam_index, beam_table, positions, grid)
    probe = jnp.einsum(
        "opij,jirw->oprw",
        mixing,
        lax.all_to_all(smatrix, "dev", split_axis=2, concat_axis=0, tiled=True),
        preferred_element_type=jnp.float32,
    )
    share_width = grid // lax.axis_size("half")
    summed = lax.psum(probe, "half")
    owned = lax.dynamic_slice_in_dim(summed, lax.axis_index("half") * share_width, share_width, 3)
    return owned[0] * owned[0] + owned[1] * owned[1]


def solution(mesh):
    return jax.shard_map(
        local,
        mesh=mesh,
        in_specs=(P("dev", None), P("half", None), P("half"), P(), P("dev", None)),
        out_specs=P("dev", None, "half"),
        check_vma=False,
    )
```

profile of v0, /device:TPU:1, one launch (start us, length us, event | category | flops | bytes accessed | tf_op | source)
XLA Modules:
  0.0 467.6 jit_solution(10000365001540169459)
XLA Ops:
  10.4 81.1 %all-gather.2.cloned.1.call-done = bf16[1024,1024]{1,0:T(8,128)(2,1)} async-done(((bf16[16,1024]{1,0:T(8,128)(2,1)}), bf16[1024,1024]{1,0:T(8,128)(2,1)}) %all-gather.2.cloned.1.call-update) | async-done | bytes 2097168 | tf_op jit(solution)/shard_map/all_gather | solution.py:89
  91.5 18.4 %fusion.104 = (f32[1024,1024]{1,0:T(8,128)S(1)}, f32[1024,1024]{1,0:T(8,128)S(1)}) fusion(s32[1024]{0:T(1024)S(1)} %get-tuple-element.34, s32[1024]{0:T(1024)S(1)} %get-tuple-element.35, bf16[1024,1024]{1,0:T(8,128)(2,1)} %all-gather.2.cloned.1.call-done), kind=kLoop, calls=%fused_computation.153 | loop fusion | flops 16777216 | bytes 10493952 | tf_op jit(solution)/shard_map/cos | solution.py:95
  109.9 2.4 copy.28
  112.4 2.4 copy.29
  114.8 8.0 %fusion.62 = f32[2,32,32,1024]{3,1,2,0:T(8,128)S(1)} fusion(f32[1,32,32,1024]{3,1,0,2:T(8,128)S(1)} %copy.29, f32[1,32,32,1024]{3,1,0,2:T(8,128)S(1)} %copy.28, f32[1,2,32,32]{2,3,1,0:T(8,128)S(1)} %get-tuple-element.20, f32[1,2,32,32]{2,3,1,0:T(8,128)S(1)} %get-tuple-element.19), kind=kOutput, calls=%fused_computation.72 | convolution fusion | flops 1612713984 | bytes 16793600 | tf_op jit(solution)/shard_map/ibay,oibc->ocay/dot_general | solution.py:42
  125.6 12.1 %fusion.44 = f32[2,32,32,1024]{3,1,2,0:T(8,128)S(1)} fusion(f32[2,32,32,1024]{3,1,2,0:T(8,128)S(1)} %pad_maximum_fusion, f32[1,2,32,32]{2,3,1,0:T(8,128)S(1)} %get-tuple-element.20, f32[1,2,32,32]{2,3,1,0:T(8,128)S(1)} %get-tuple-element.19), kind=kOutput, calls=%fused_computation.66 | convolution fusion | flops 1610616832 | bytes 16793600 | tf_op jit(solution)/shard_map/icay,oiad->odcy/dot_general | solution.py:51
  137.7 8.1 %copy.31 = f32[2,32,32,1024]{3,2,1,0:T(8,128)} copy(f32[2,32,32,1024]{3,1,2,0:T(8,128)S(1)} %fusion.44) | data formatting | bytes 16777216 | tf_op jit(solution)/shard_map/icay,oiad->odcy/dot_general | solution.py:51
  145.9 8.7 %copy.32 = f32[2,1024,1024]{2,1,0:T(8,128)} copy(f32[2,1024,1024]{1,2,0:T(8,128)} %bitcast.140) | data formatting | bytes 16777216 | tf_op jit(solution)/shard_map/transpose | solution.py:97
  154.6 15.8 %fusion.47 = f32[2,32,32,1024]{3,1,2,0:T(8,128)S(1)} fusion(f32[2,32,32,1024]{3,2,1,0:T(8,128)} %bitcast.141, f32[1,2,32,32]{2,3,1,0:T(8,128)S(1)} %get-tuple-element.20, f32[1,2,32,32]{2,3,1,0:T(8,128)S(1)} %get-tuple-element.19), kind=kOutput, calls=%fused_computation.67 | convolution fusion | flops 1610616832 | bytes 16793600 | tf_op jit(solution)/shard_map/ibay,oibc->ocay/dot_general | solution.py:42
  171.9 1.7 pad_maximum_fusion.1
  173.5 12.1 %fusion.50 = f32[2,32,32,1024]{3,1,2,0:T(8,128)S(1)} fusion(f32[2,32,32,1024]{3,1,2,0:T(8,128)S(1)} %pad_maximum_fusion.1, f32[1,2,32,32]{2,3,1,0:T(8,128)S(1)} %get-tuple-element.20, f32[1,2,32,32]{2,3,1,0:T(8,128)S(1)} %get-tuple-element.19), kind=kOutput, calls=%fused_computation.68 | convolution fusion | flops 1610616832 | bytes 16793600 | tf_op jit(solution)/shard_map/icay,oiad->odcy/dot_general | solution.py:51
  185.7 16.8 %fusion.32 = (f32[1,32,32,1024]{3,1,2,0:T(8,128)S(1)}, f32[1,32,32,1024]{3,1,2,0:T(8,128)S(1)}) fusion(f32[2,32,32,1024]{3,1,2,0:T(8,128)S(1)} %fusion.50, s32[1024]{0:T(1024)S(1)} %fusion.92, s32[32,32]{0,1:T(8,128)S(1)} %fusion.75), kind=kLoop, calls=%fused_computation.46 | loop fusion | flops 13631488 | bytes 16785408 | tf_op jit(solution)/shard_map/sub | solution.py:100
  202.5 7.5 %fusion.53 = f32[2,32,32,1024]{3,1,2,0:T(8,128)S(1)} fusion(f32[1,2,32,32]{2,3,1,0:T(8,128)S(1)} %get-tuple-element.18, f32[1,2,32,32]{2,3,1,0:T(8,128)S(1)} %get-tuple-element.17, f32[1,32,32,1024]{3,1,2,0:T(8,128)S(1)} %get-tuple-element.14, f32[1,32,32,1024]{3,1,2,0:T(8,128)S(1)} %get-tuple-element.13), kind=kOutput, calls=%fused_computation.69 | convolution fusion | flops 1612713984 | bytes 16793600 | tf_op jit(solution)/shard_map/ibay,oibc->ocay/dot_general | solution.py:42
  213.2 12.1 %fusion.56 = f32[2,32,32,1024]{3,1,2,0:T(8,128)S(1)} fusion(f32[2,32,32,1024]{3,1,2,0:T(8,128)S(1)} %pad_maximum_fusion.3, f32[1,2,32,32]{2,3,1,0:T(8,128)S(1)} %get-tuple-element.18, f32[1,2,32,32]{2,3,1,0:T(8,128)S(1)} %get-tuple-element.17), kind=kOutput, calls=%fused_computation.70 | convolution fusion | flops 1610616832 | bytes 16793600 | tf_op jit(solution)/shard_map/icay,oiad->odcy/dot_general | solution.py:51
  225.3 8.1 %copy.37 = f32[2,32,32,1024]{3,2,1,0:T(8,128)} copy(f32[2,32,32,1024]{3,1,2,0:T(8,128)S(1)} %fusion.56) | data formatting | bytes 16777216 | tf_op jit(solution)/shard_map/icay,oiad->odcy/dot_general | solution.py:51
  233.5 8.7 %copy.38 = f32[2,1024,1024]{2,1,0:T(8,128)} copy(f32[2,1024,1024]{1,2,0:T(8,128)} %bitcast.142) | data formatting | bytes 16777216 | tf_op jit(solution)/shard_map/transpose | solution.py:103
  242.1 15.8 %fusion.59 = f32[2,32,32,1024]{3,1,2,0:T(8,128)S(1)} fusion(f32[2,32,32,1024]{3,2,1,0:T(8,128)} %bitcast.143, f32[1,2,32,32]{2,3,1,0:T(8,128)S(1)} %get-tuple-element.18, f32[1,2,32,32]{2,3,1,0:T(8,128)S(1)} %get-tuple-element.17), kind=kOutput, calls=%fused_computation.71 | convolution fusion | flops 1610616832 | bytes 16793600 | tf_op jit(solution)/shard_map/ibay,oibc->ocay/dot_general | solution.py:42
  260.7 11.7 %fusion.3 = bf16[2,32,32,1024]{3,1,2,0:T(8,128)(2,1)S(1)} fusion(f32[2,32,32,1024]{3,1,2,0:T(8,128)S(1)} %pad_maximum_fusion.4, f32[1,2,32,32]{2,3,1,0:T(8,128)S(1)} %get-tuple-element.18, f32[1,2,32,32]{2,3,1,0:T(8,128)S(1)} %get-tuple-element.17), kind=kOutput, calls=%fused_computation.10 | convolution fusion | flops 1614811136 | bytes 12599296 | tf_op jit(solution)/shard_map/icay,oiad->odcy/dot_general | solution.py:51
  272.5 2.3 copy.41
  274.8 6.3 %copy.42 = bf16[1,2,1024,1024]{3,1,0,2:T(2,128)(2,1)} copy(bf16[1,2,1024,1024]{3,2,1,0:T(8,128)(2,1)S(1)} %bitcast.146) | data formatting | bytes 8388608 | tf_op jit(solution)/shard_map/convert_element_type | solution.py:105
  281.2 8.7 %all-to-all-start = ((bf16[1,2,1024,1024]{3,1,0,2:T(2,128)(2,1)}), bf16[1,2,1024,1024]{3,1,0,2:T(2,128)(2,1)}, u32[]{:S(2)}, u32[]{:S(2)}) async-start(bf16[1,2,1024,1024]{3,1,0,2:T(2,128)(2,1)} %copy.42), calls=%async_computation | async-start | bytes 8388608 | tf_op jit(solution)/shard_map/all_to_all | solution.py:110
  290.7 89.0 %all-to-all-done = bf16[1,2,1024,1024]{3,1,0,2:T(2,128)(2,1)} async-done(((bf16[1,2,1024,1024]{3,1,0,2:T(2,128)(2,1)}), bf16[1,2,1024,1024]{3,1,0,2:T(2,128)(2,1)}, u32[]{:S(2)}, u32[]{:S(2)}) %all-to-all-start) | async-done | bytes 4194336 | tf_op jit(solution)/shard_map/all_to_all | solution.py:110
  379.6 8.4 %fusion.65 = f32[2,16,16,1024]{3,1,2,0:T(8,128)} fusion(bf16[1,2,64,16,1024]{4,1,3,2,0:T(2,128)(2,1)} %bitcast.55, bf16[1,16,2,64]{3,1,2,0:T(8,128)(2,1)S(1)} %get-tuple-element.22, bf16[1,16,2,64]{3,1,2,0:T(8,128)(2,1)S(1)} %get-tuple-element.21), kind=kOutput, calls=%fused_computation.73 | convolution fusion | flops 134234112 | bytes 6299648 | tf_op jit(solution)/shard_map/opij,jirw->oprw/dot_general | solution.py:107
  388.0 70.3 %all-reduce.2.cloned.1.call-done = f32[2,16,16,1024]{3,1,2,0:T(8,128)} async-done(((f32[2,16,16,1024]{3,1,2,0:T(8,128)}), f32[2,16,16,1024]{3,1,2,0:T(8,128)}) %all-reduce.2.cloned.1.call-update) | async-done | bytes 2097168 | tf_op jit(solution)/shard_map/psum | solution.py:114
  (40 shorter events, 16.7 us)
Async XLA Ops:
  6.5 283.7 %copy-start = (f32[16,2]{0,1:T(2,128)S(1)}, f32[16,2]{0,1:T(2,128)}, u32[]{:S(2)}) copy-start(f32[16,2]{0,1:T(2,128)} %param.8) | copy-start | bytes 388
  6.5 85.0 %all-gather.2.cloned.1.call-start = ((), (), s32[]{:S(2)}) async-start(), calls=%async_computation.1 | async-start | bytes 2129920 | tf_op jit(solution)/shard_map/all_gather | solution.py:89
  281.2 9.1 %copy-start.1 = (s32[64,2]{0,1:T(2,128)S(1)}, s32[64,2]{0,1:T(2,128)}, u32[]{:S(2)}) copy-start(s32[64,2]{0,1:T(2,128)} %param.6) | copy-start | bytes 1540
  281.2 9.1 %copy-start.3 = (s32[64]{0:T(128)S(1)}, s32[64]{0:T(128)}, u32[]{:S(2)}) copy-start(s32[64]{0:T(128)} %param.7) | copy-start | bytes 772
  281.2 9.3 %copy-start.2 = (s32[16,2]{0,1:T(2,128)S(1)}, s32[16,2]{0,1:T(2,128)}, u32[]{:S(2)}) copy-start(s32[16,2]{0,1:T(2,128)} %param.9) | copy-start | bytes 388
  281.2 98.5 %all-to-all-start = ((bf16[1,2,1024,1024]{3,1,0,2:T(2,128)(2,1)}), bf16[1,2,1024,1024]{3,1,0,2:T(2,128)(2,1)}, u32[]{:S(2)}, u32[]{:S(2)}) async-start(bf16[1,2,1024,1024]{3,1,0,2:T(2,128)(2,1)} %copy.42), calls=%async_computation | async-start | bytes 8388608 | tf_op jit(solution)/shard_map/all_to_all | solution.py:110
  289.9 168.4 %all-reduce.2.cloned.1.call-start = ((), (), s32[]{:S(2)}) async-start(), calls=%async_computation.2 | async-start | bytes 4194304 | tf_op jit(solution)/shard_map/psum | solution.py:114
Sparse Core Ops, SparseCore 0:
  10.7 80.7 all-gather.1
  388.1 70.1 all-reduce.1
where the time goes:
time: 471 us; the launch traced here: 468 us
  waiting for transfers between devices  241 us (51%)
  matrix products  104 us (22%)
  other arithmetic  50.2 us (11%)
  local copies, waits for them, and re-layouts  49.4 us (10%)
  between operations  14.2 us (3%)
  starting transfers between devices  9.05 us (2%)
    all_to_all x1, waiting for transfers between devices, local(): lax.all_to_all(smatrix, 'dev', split_axis=2, concat_axis=0, tiled=True)  89 us
    all_gather x1, waiting for transfers between devices, local(): row_piece = lax.all_gather(potential, 'dev', axis=0, tiled=True)  81.1 us
    psum x1, waiting for transfers between devices, local(): summed = lax.psum(probe, 'half')  70.3 us
    dot_general x4, matrix products, transform_first(): jnp.einsum('icay,oiad->odcy', sectioned, inner_table, precision=lax.Preci...  48 us
    dot_general x4, matrix products, transform_first(): jnp.einsum('ibay,oibc->ocay', shaped, outer_table, precision=lax.Precisio...  47.2 us
    cos x1, other arithmetic, local(): incident = jnp.stack([jnp.cos(phase_angle), jnp.sin(phase_angle)])  18.4 us
    sub x1, other arithmetic, local(): field[0] * filter_re - field[1] * filter_im  16.8 us
    dot_general x2, local copies, waits for them, and re-layouts, transform_first(): jnp.einsum('icay,oiad->odcy', sectioned, inner_table, precision=lax.Preci...  16.3 us
  transfers between devices with their start and end apart: 3, of which 3 were waited for; matrix products, arithmetic and copies ran while one was open for 1% of the time, Pallas kernels for 0%

commit v1 on v0

v1 whole, which is shorter than its diff:
```python
import functools
import math

import jax
import jax.numpy as jnp
import ml_dtypes
import numpy as np
from jax import lax
from jax.experimental import pallas as pl
from jax.experimental.pallas import tpu as pltpu
from jax.sharding import PartitionSpec as P

two_pi = 2.0 * math.pi
propagation_rate = 0.6

GRID = 1024
TILTS = 256
REACH = 128
BAND = 341
GROUP = 8
HALVES = 4
TILE = 16
WIDE = 24
PARTS = GROUP * HALVES
ROWS_IN = WIDE + 2 * REACH
HALF_COLS = GROUP * WIDE + 2 * REACH
KU = 768
BATCH = 16
BLOCK = 2 * BATCH * WIDE


def spread_of(count):
    return 2.0 ** np.mod(np.arange(count) * 0.6180339887498949, 1.0)


def angles(product):
    return np.mod(product, GRID).astype(np.float64) * (2.0 * np.pi / GRID)


def two_parts(table):
    high = table.astype(np.float32).astype(ml_dtypes.bfloat16)
    low = (table - high.astype(np.float64)).astype(np.float32).astype(ml_dtypes.bfloat16)
    return high, low


@functools.lru_cache(maxsize=None)
def column_table():
    angle = angles(np.arange(GRID)[:, None] * np.arange(HALF_COLS)[None, :])
    return np.concatenate([np.cos(angle), np.sin(angle)], 1).astype(np.float32)


@functools.lru_cache(maxsize=None)
def row_table():
    source, depth, inner = np.meshgrid(np.arange(16), np.arange(4), np.arange(16), indexing="ij")
    rows = ((depth * 16 + source) * 16 + inner).reshape(-1)
    angle = angles(rows[:, None] * (np.arange(GRID) - BAND - REACH)[None, :])
    table = np.concatenate([np.cos(angle), np.sin(angle)], 1)
    return two_parts(table / spread_of(TILE)[rows % TILE][:, None])


@functools.lru_cache(maxsize=None)
def back_row_table():
    index = np.arange(KU) - BAND
    result = []
    for group in range(8):
        rows = np.arange(GROUP * TILE) + group * GROUP * TILE
        angle = angles(index[:, None] * rows[None, :])
        angle = angle - (propagation_rate / GRID) * (index * index).astype(np.float64)[:, None]
        cosine, sine = np.cos(angle), np.sin(angle)
        result.append(np.concatenate([cosine, sine], 1))
    return np.stack(result).astype(np.float32).astype(ml_dtypes.bfloat16)


@functools.lru_cache(maxsize=None)
def back_column_table():
    index = np.arange(PARTS * WIDE) - BAND
    cols = np.arange(GRID)
    angle = angles(index[:, None] * cols[None, :])
    angle = angle - (propagation_rate / GRID) * (index * index).astype(np.float64)[:, None]
    scale = 1.0 / (GRID * GRID)
    cosine = (np.cos(angle) * scale).reshape(PARTS, WIDE, HALVES, GRID // HALVES)
    sine = (np.sin(angle) * scale).reshape(PARTS, WIDE, HALVES, GRID // HALVES)
    table = np.concatenate(
        [np.concatenate([cosine, sine], 3), np.concatenate([-sine, cosine], 3)], 1
    )
    table = table.reshape(PARTS * 2 * WIDE, HALVES, 2 * GRID // HALVES).transpose(1, 0, 2)
    return two_parts(table)


def field_kernel(
    shift_ref,
    start_ref,
    spread_ref,
    spec_re,
    spec_im,
    back_ref,
    coef_ref,
    level_ref,
    out_ref,
    mask,
    rows,
    field_re,
    field_im,
    sums_re,
    sums_im,
):
    first = start_ref[0]
    row_index = lax.broadcasted_iota(jnp.int32, (WIDE, KU), 0) + first
    lane_index = lax.broadcasted_iota(jnp.int32, (WIDE, KU), 1) - BAND
    inside = 9 * (row_index * row_index + lane_index * lane_index) < GRID * GRID
    inside = jnp.where(inside, 1.0, 0.0)
    mask[...] = jnp.concatenate([inside, inside], 0).astype(jnp.bfloat16)
    chunks = KU // 128

    def shifted(tilt, at):
        row_at = shift_ref[1, tilt]
        lane_at = shift_ref[0, tilt]
        spread = spread_ref[tilt]
        base = jnp.where(lane_at >= 128, 1, 0)
        rest = lane_at - 128 * base
        lanes = lax.broadcasted_iota(jnp.int32, (2 * WIDE, 128), 1)
        keep = lanes < 128 - rest
        turn = jnp.bitwise_and(128 - rest, 127)
        before = None
        for chunk in range(chunks + 1):
            window = jnp.concatenate(
                [ref[base + chunk, pl.ds(row_at, WIDE), :] for ref in (spec_re, spec_im)], 0
            )
            rolled = pltpu.roll((window * spread).astype(jnp.bfloat16), turn, 1)
            if chunk:
                lanes_at = (chunk - 1) * 128
                rows[pl.ds(at, 2 * WIDE), lanes_at : lanes_at + 128] = (
                    jnp.where(keep, before, rolled) * mask[:, lanes_at : lanes_at + 128]
                )
            before = rolled

    def block(step, carry):
        for spot in range(BATCH):
            shifted(step * BATCH + spot, spot * 2 * WIDE)
        at = pl.multiple_of(step * BLOCK, BLOCK)
        result = jnp.dot(rows[...], back_ref[...], preferred_element_type=jnp.float32)
        field_re[pl.ds(at, BLOCK), :] = result[:, :128]
        field_im[pl.ds(at, BLOCK), :] = result[:, 128:]
        return carry

    lax.fori_loop(0, TILTS // BATCH, block, 0)

    count = GROUP * TILE
    for col in range(WIDE):
        values = jnp.concatenate(
            [
                jnp.concatenate(
                    [ref[pl.ds(col + WIDE * part, TILTS, stride=2 * WIDE), :] for part in range(2)], 0
                )
                * level_ref[...]
                for ref in (field_re, field_im)
            ],
            1,
        )
        high = values.astype(jnp.bfloat16)
        low = (values - high.astype(jnp.float32)).astype(jnp.bfloat16)
        mixed = jnp.dot(coef_ref[...], high, preferred_element_type=jnp.float32)
        mixed = mixed + jnp.dot(coef_ref[...], low, preferred_element_type=jnp.float32)
        sums_re[pl.ds(col, count, stride=WIDE), :] = mixed[:count, :count] - mixed[count:, count:]
        sums_im[pl.ds(col, count, stride=WIDE), :] = mixed[count:, :count] + mixed[:count, count:]

    block_of = lax.broadcasted_iota(jnp.int32, (WIDE, 128), 1) // TILE
    for tile in range(GROUP):
        for half in range(2):
            parts = []
            for ref in (sums_re, sums_im):
                total = jnp.zeros((WIDE, 128), jnp.float32)
                for spot in range(8):
                    at = (tile * TILE + half * 8 + spot) * WIDE
                    turned = ref[at : at + WIDE, :]
                    turn = ((spot - tile) * TILE) % 128
                    if turn:
                        turned = pltpu.roll(turned, turn, 1)
                    total = jnp.where(block_of == spot, turned, total)
                parts.append(total)
            out_ref[tile, :, half * 128 : (half + 1) * 128] = jnp.concatenate(parts, 0).astype(
                out_ref.dtype
            )


def field_sums(shifts, start, spec_re, spec_im, back, coef):
    vmem = pl.BlockSpec(memory_space=pltpu.VMEM)
    smem = pl.BlockSpec(memory_space=pltpu.SMEM)
    spread = spread_of(TILTS)
    level = np.tile(np.broadcast_to((1.0 / spread)[:, None], (TILTS, 128)), (2, 1))
    return pl.pallas_call(
        field_kernel,
        out_shape=jax.ShapeDtypeStruct((GROUP, 2 * WIDE, TILE * TILE), jnp.bfloat16),
        in_specs=[smem, smem, smem, vmem, vmem, vmem, vmem, vmem],
        out_specs=vmem,
        scratch_shapes=[
            pltpu.VMEM((2 * WIDE, KU), jnp.bfloat16),
            pltpu.VMEM((BLOCK, KU), jnp.bfloat16),
            pltpu.VMEM((TILTS * 2 * WIDE, 128), jnp.float32),
            pltpu.VMEM((TILTS * 2 * WIDE, 128), jnp.float32),
            pltpu.VMEM((GROUP * TILE * WIDE, 128), jnp.float32),
            pltpu.VMEM((GROUP * TILE * WIDE, 128), jnp.float32),
        ],
        compiler_params=pltpu.CompilerParams(vmem_limit_bytes=48 * 1024 * 1024),
    )(
        shifts,
        start,
        jnp.asarray(spread.astype(np.float32)),
        spec_re,
        spec_im,
        back,
        coef,
        jnp.asarray(level.astype(np.float32)),
    )


def mixing_table(tilt_list, beam_list, beam_table, positions):
    levels = beam_table.shape[0]
    selector = (beam_list[:, None] == jnp.arange(levels, dtype=jnp.int32)[None, :]).astype(
        jnp.float32
    )
    weights = jnp.dot(selector, beam_table, precision=lax.Precision.HIGHEST)
    winding = jnp.bitwise_and(
        positions[:, 0:1] * tilt_list[None, :, 0] + positions[:, 1:2] * tilt_list[None, :, 1],
        GRID - 1,
    )
    coef_angle = two_pi * winding.astype(jnp.float32) / GRID
    cosine = jnp.cos(coef_angle)
    sine_part = jnp.sin(coef_angle)
    coef_re = weights[None, :, 0] * cosine + weights[None, :, 1] * sine_part
    coef_im = weights[None, :, 1] * cosine - weights[None, :, 0] * sine_part
    return jnp.concatenate(
        [jnp.concatenate([coef_re, -coef_im], 1), jnp.concatenate([coef_im, coef_re], 1)], 0
    ).astype(jnp.bfloat16)


def groups(kind):
    flat = np.arange(64).reshape(4, 2, 2, 4)
    if kind == "depth":
        return flat.reshape(4, 16).T.tolist()
    if kind == "plane":
        return flat.reshape(4, 16).tolist()
    return flat.reshape(8, 8).tolist()


def local(potential, tilt_ids, beam_index, beam_table, positions):
    half = lax.axis_index("half")
    dev = lax.axis_index("dev")
    group, member = dev // GROUP, dev % GROUP

    tilt_info = lax.all_gather(
        jnp.concatenate([tilt_ids, beam_index[:, None]], 1), "half", axis=0, tiled=True
    )
    spots = lax.all_gather(
        positions, "dev", axis=0, tiled=True, axis_index_groups=groups("tiles")
    )
    coef = mixing_table(tilt_info[:, :2], tilt_info[:, 2], beam_table, spots)

    first_col = half * (GROUP * WIDE) - BAND - REACH
    turn = jnp.bitwise_and(first_col * jnp.arange(GRID, dtype=jnp.int32), GRID - 1)
    phase = potential.astype(jnp.float32) - (two_pi / GRID) * turn.astype(jnp.float32)[None, :]
    spread = jnp.asarray(spread_of(TILE).astype(np.float32))[:, None]
    wave = jnp.concatenate([jnp.cos(phase) * spread, jnp.sin(phase) * spread], 0)
    mixed = jnp.dot(wave, jnp.asarray(column_table()), precision=lax.Precision.HIGH)
    rows = potential.shape[0]
    cols_re = mixed[:rows, :HALF_COLS] + mixed[rows:, HALF_COLS:]
    cols_im = mixed[rows:, :HALF_COLS] - mixed[:rows, HALF_COLS:]
    piece = jnp.concatenate([cols_re, cols_im], 1).astype(jnp.bfloat16)

    piece = jnp.broadcast_to(piece[None], (4,) + piece.shape)
    piece = lax.all_to_all(
        piece, "dev", 0, 0, tiled=True, axis_index_groups=groups("depth")
    ).reshape(4 * rows, 2 * HALF_COLS)
    windows = jnp.stack(
        [
            jnp.concatenate(
                [
                    piece[:, WIDE * i : WIDE * i + ROWS_IN],
                    piece[:, HALF_COLS + WIDE * i : HALF_COLS + WIDE * i + ROWS_IN],
                ],
                1,
            )
            for i in range(GROUP)
        ]
    )
    windows = jnp.concatenate([windows, windows], 0)
    columns = lax.all_to_all(
        windows, "dev", 0, 0, tiled=True, axis_index_groups=groups("plane")
    ).reshape(GRID, 2 * ROWS_IN)

    high, low = row_table()
    dims = (((0,), (0,)), ((), ()))
    product = lax.dot_general(
        columns, jnp.asarray(high), dims, preferred_element_type=jnp.float32
    ) + lax.dot_general(columns, jnp.asarray(low), dims, preferred_element_type=jnp.float32)
    spec_re = product[:ROWS_IN, :GRID] + product[ROWS_IN:, GRID:]
    spec_im = product[ROWS_IN:, :GRID] - product[:ROWS_IN, GRID:]
    spec_re, spec_im = (
        x.reshape(ROWS_IN, GRID // 128, 128).transpose(1, 0, 2) for x in (spec_re, spec_im)
    )

    back = lax.dynamic_index_in_dim(jnp.asarray(back_row_table()), group, 0, keepdims=False)
    shifts = (REACH - tilt_info[:, :2]).T
    start = (WIDE * (half * GROUP + member) - BAND).reshape(1)
    sums = field_sums(shifts, start, spec_re, spec_im, back, coef)

    sums = lax.all_to_all(sums, "dev", 0, 0, tiled=True, axis_index_groups=groups("tiles"))
    sums = lax.all_gather(sums, "half", axis=0, tiled=True).reshape(PARTS * 2 * WIDE, TILE * TILE)

    high, low = (
        lax.dynamic_index_in_dim(jnp.asarray(t), half, 0, keepdims=False)
        for t in back_column_table()
    )
    probe = lax.dot_general(sums, high, dims, preferred_element_type=jnp.float32) + lax.dot_general(
        sums, low, dims, preferred_element_type=jnp.float32
    )
    share = GRID // HALVES
    real, imag = probe[:, :share], probe[:, share:]
    return (real * real + imag * imag).reshape(TILE, TILE, share)


def solution(mesh):
    return jax.shard_map(
        local,
        mesh=mesh,
        in_specs=(P("dev", None), P("half", None), P("half"), P(), P("dev", None)),
        out_specs=P("dev", None, "half"),
        check_vma=False,
    )
```

time: 471 us -> 126 us (0.27)
  waiting for transfers between devices: 241 us -> 19.5 us
  matrix products: 104 us -> 15 us
  local copies, waits for them, and re-layouts: 49.4 us -> 3.18 us
  blocking collectives: 0 us -> 36.6 us
  other arithmetic: 50.2 us -> 14.6 us
  Pallas kernels: 0 us -> 20.1 us
  between operations: 14.2 us -> 0.2 us
  starting transfers between devices: 9.05 us -> 16.2 us
    dot_general x9 -> x5, matrix products: 104 us -> 14.8 us  [the longest x1 5.01 us: local(): lax.dot_general(columns, jnp.asarray(high), dims, preferred_element_type=...]
    all_gather x1 -> x0, waiting for transfers between devices: 81.1 us -> none  [local(): row_piece = lax.all_gather(potential, 'dev', axis=0, tiled=True)]
    psum x1 -> x0, waiting for transfers between devices: 70.3 us -> none  [local(): summed = lax.psum(probe, 'half')]
    all_to_all x1 -> x3, waiting for transfers between devices: 89 us -> 19.5 us  [the longest x1 13.7 us: local(): lax.all_to_all(windows, 'dev', 0, 0, tiled=True, axis_index_groups=groups...]
    all_gather x0 -> x3, blocking collectives: none -> 36.6 us  [the longest x1 15.3 us: local(): lax.all_gather(sums, 'half', axis=0, tiled=True)]
    sub x5 -> x0, other arithmetic: 22.1 us -> none  [the longest x1 16.8 us: local(): field[0] * filter_re - field[1] * filter_im]
    pallas_call x0 -> x1, Pallas kernels: none -> 20.1 us  [field_sums(): pl.pallas_call(field_kernel, out_shape=jax.ShapeDtypeStruct((GROUP, 2 * W...]
    cos x1 -> x0, other arithmetic: 18.4 us -> none  [local(): incident = jnp.stack([jnp.cos(phase_angle), jnp.sin(phase_angle)])]
  transfers between devices with their start and end apart: 3 -> 3, of which waited for: 3 -> 2; matrix products, arithmetic and copies ran while one was open for 1% -> 2% of each run, Pallas kernels for 0% -> 0%
where the time goes in v1:
time: 126 us; the launch traced here: 125 us
  blocking collectives  36.6 us (29%)
  Pallas kernels  20.1 us (16%)
  waiting for transfers between devices  19.5 us (15%)
  starting transfers between devices  16.2 us (13%)
  matrix products  15 us (12%)
  other arithmetic  14.6 us (12%)
  local copies, waits for them, and re-layouts  3.18 us (3%)
    pallas_call x1, Pallas kernels, field_sums(): pl.pallas_call(field_kernel, out_shape=jax.ShapeDtypeStruct((GROUP, 2 * W...  20.1 us
    all_gather x1, blocking collectives, local(): lax.all_gather(sums, 'half', axis=0, tiled=True)  15.3 us
    all_gather x1, blocking collectives, local(): lax.all_gather(positions, 'dev', axis=0, tiled=True, axis_index_groups=gr...  15.3 us
    all_to_all x1, waiting for transfers between devices, local(): lax.all_to_all(windows, 'dev', 0, 0, tiled=True, axis_index_groups=groups...  13.7 us
    unnamed x17, other arithmetic  11.4 us
    all_to_all x1, starting transfers between devices, local(): lax.all_to_all(piece, 'dev', 0, 0, tiled=True, axis_index_groups=groups('...  9.01 us
    all_gather x1, blocking collectives, local(): lax.all_gather(jnp.concatenate([tilt_ids, beam_index[:, None]], 1), 'half...  5.98 us
    all_to_all x1, waiting for transfers between devices, local(): lax.all_to_all(sums, 'dev', 0, 0, tiled=True, axis_index_groups=groups('t...  5.72 us
  transfers between devices with their start and end apart: 3, of which 2 were waited for; matrix products, arithmetic and copies ran while one was open for 2% of the time, Pallas kernels for 0%

profile of v1, /device:TPU:1, one launch (start us, length us, event | category | flops | bytes accessed | tf_op | source)
XLA Modules:
  0.0 125.3 jit_solution(9307465181332713976)
XLA Ops:
  0.0 1.0 cosine_multiply_fusion
  1.1 3.2 %fusion.15 = f32[32,896]{1,0:T(8,128)S(1)} fusion(f32[1024,896]{1,0:T(8,128)} %constant.88.clone, f32[16,1024]{1,0:T(8,128)S(1)} %get-tuple-element.26, f32[16,1024]{1,0:T(8,128)S(1)} %get-tuple-element.25), kind=kOutput, calls=%fused_computation.28 | convolution fusion | flops 176193536 | bytes 3915776 | tf_op jit(solution)/shard_map/dot_general | solution.py:264
  5.1 9.0 %all-to-all-start = ((bf16[4,16,896]{2,1,0:T(8,128)(2,1)}), bf16[4,16,896]{2,1,0:T(8,128)(2,1)S(1)}, u32[]{:S(2)}, u32[]{:S(2)}) async-start(bf16[4,16,896]{2,1,0:T(8,128)(2,1)} %broadcast_in_dim.5), calls=%async_computation | async-start | bytes 229376 | tf_op jit(solution)/shard_map/all_to_all | solution.py:271
  14.1 6.0 %all-gather = s32[4,64,3]{1,2,0:T(4,128)S(1)} all-gather(s32[1,64,3]{1,2,0:T(4,128)S(1)} %add_bitcast_fusion), channel_id=1, replica_groups=mesh['half'=4,'dev'=64] {'half'}, dimensions={0}, use_global_device_ids=true | all-gather | bytes 3840 | tf_op jit(solution)/shard_map/all_gather | solution.py:251
  20.2 15.3 %all-gather.1 = s32[8,16,2]{1,2,0:T(2,128)S(1)} all-gather(s32[1,16,2]{1,2,0:T(2,128)S(1)} %bitcast.111), channel_id=1, replica_groups={{0,1,2,3,4,5,6,7},{8,9,10,11,12,13,14,15},{16,17,18,19,20,21,22,23},{24..., dimensions={0}, use_global_device_ids=true | all-gather | bytes 1152 | tf_op jit(solution)/shard_map/all_gather | solution.py:254
  36.1 0.7 fusion.32
  37.5 0.7 fusion.28
  38.2 0.7 fusion.26
  41.1 0.7 fusion.18
  43.2 0.7 fusion.29
  44.6 0.7 fusion.25
  47.5 3.8 %all-to-all-start.1 = ((bf16[16,64,560]{2,1,0:T(8,128)(2,1)}), bf16[16,64,560]{2,1,0:T(8,128)(2,1)S(1)}, u32[]{:S(2)}, u32[]{:S(2)}) async-start(bf16[16,64,560]{2,1,0:T(8,128)(2,1)} %fusion.19), calls=%async_computation.1 | async-start | bytes 2621440 | tf_op jit(solution)/shard_map/all_to_all | solution.py:287
  52.0 1.0 dynamic-slice_bitcast_fusion.back_ref
  53.0 13.7 %all-to-all-done.1 = bf16[16,64,560]{2,1,0:T(8,128)(2,1)S(1)} async-done(((bf16[16,64,560]{2,1,0:T(8,128)(2,1)}), bf16[16,64,560]{2,1,0:T(8,128)(2,1)S(1)}, u32[]{:S(2)}, u32[]{:S(2)}) %all-to-all-start.1) | async-done | bytes 1146912 | tf_op jit(solution)/shard_map/all_to_all | solution.py:287
  66.8 5.0 %fusion.43 = f32[560,2048]{1,0:T(8,128)S(1)} fusion(bf16[1024,560]{1,0:T(8,128)(2,1)S(1)} %bitcast.103, bf16[1024,2048]{1,0:T(8,128)(2,1)} %constant.89.clone), kind=kOutput, calls=%fused_computation.75 | convolution fusion | flops 2348810240 | bytes 9928704 | tf_op jit(solution)/shard_map/dot_general | solution.py:293
  71.8 2.6 %convolution_add_fusion = f32[560,2048]{1,0:T(8,128)S(1)} fusion(f32[560,2048]{1,0:T(8,128)S(1)} %fusion.43, bf16[1024,560]{1,0:T(8,128)(2,1)S(1)} %bitcast.104, bf16[1024,2048]{1,0:T(8,128)(2,1)S(1)} %copy-done.3), kind=kOutput, calls=%fused_computation | convolution fusion | flops 2349957120 | bytes 14516224 | tf_op jit(solution)/shard_map/dot_general | solution.py:295
  75.3 0.8 copy-done.1
  76.1 20.1 %shard_map.136 = bf16[8,48,256]{2,1,0:T(8,128)(2,1)} custom-call(s32[2,256]{1,0:T(2,128)S(1)} %fusion.36.shift_ref, s32[1]{0:T(128)} %bitcast.3.start_ref, f32[256]{0:T(256)S(1)} %copy-done.2, f32[8,280,128]{2,1,0:T(8,128)S(1)} %get-tuple-element.38.spec_re, f32[8,280,128]{2,1,0:T(8,128)S(1)} %get-tuple-element.37.spec_im, ...), custom_call_target="tpu_custom_call" | custom-call | tf_op jit(solution)/shard_map/pallas_call | solution.py:191
  96.1 3.4 %all-to-all-start.2 = ((bf16[8,48,256]{2,1,0:T(8,128)(2,1)}), bf16[8,48,256]{2,1,0:T(8,128)(2,1)S(1)}, u32[]{:S(2)}, u32[]{:S(2)}) async-start(bf16[8,48,256]{2,1,0:T(8,128)(2,1)} %shard_map.136), calls=%async_computation.2 | async-start | bytes 393216 | tf_op jit(solution)/shard_map/all_to_all | solution.py:307
  99.5 5.7 %all-to-all-done.2 = bf16[8,48,256]{2,1,0:T(8,128)(2,1)S(1)} async-done(((bf16[8,48,256]{2,1,0:T(8,128)(2,1)}), bf16[8,48,256]{2,1,0:T(8,128)(2,1)S(1)}, u32[]{:S(2)}, u32[]{:S(2)}) %all-to-all-start.2) | async-done | bytes 196640 | tf_op jit(solution)/shard_map/all_to_all | solution.py:307
  105.3 15.3 %all_gather.11 = bf16[32,48,256]{2,1,0:T(8,128)(2,1)S(1)} all-gather(bf16[8,48,256]{2,1,0:T(8,128)(2,1)S(1)} %all-to-all-done.2), channel_id=1, replica_groups=mesh['half'=4,'dev'=64] {'half'}, dimensions={0}, use_global_device_ids=true | all-gather | bytes 983040 | tf_op jit(solution)/shard_map/all_gather | solution.py:308
  120.6 2.0 %fusion = f32[256,512]{1,0:T(8,128)S(1)} fusion(bf16[1536,256]{1,0:T(8,128)(2,1)S(1)} %bitcast.105, bf16[4,1536,512]{2,1,0:T(8,128)(2,1)} %constant.95.clone, s32[]{:T(128)S(6)} %select_n.23), kind=kOutput, calls=%fused_computation.1 | convolution fusion | flops 402653184 | bytes 2883588 | tf_op jit(solution)/shard_map/dot_general | solution.py:314
  122.6 2.0 %fusion.6 = f32[256,512]{1,0:T(8,128)S(1)} fusion(f32[256,512]{1,0:T(8,128)S(1)} %fusion, bf16[1536,256]{1,0:T(8,128)(2,1)S(1)} %bitcast.106, bf16[4,1536,512]{2,1,0:T(8,128)(2,1)} %constant.94.clone, s32[]{:T(128)S(6)} %select_n.23), kind=kOutput, calls=%fused_computation.7 | convolution fusion | flops 402784256 | bytes 3407876 | tf_op jit(solution)/shard_map/dot_general | solution.py:314
  124.6 0.7 fusion.11
  (43 shorter events, 10.1 us)
Async XLA Ops:
  0.0 35.5 %copy-start = (f32[16,2]{0,1:T(2,128)S(1)}, f32[16,2]{0,1:T(2,128)}, u32[]{:S(2)}) copy-start(f32[16,2]{0,1:T(2,128)} %param.17) | copy-start | bytes 388
  1.0 13.0 %copy-start.4 = (s32[64,2]{0,1:T(2,128)S(1)}, s32[64,2]{0,1:T(2,128)}, u32[]{:S(2)}) copy-start(s32[64,2]{0,1:T(2,128)} %param.15) | copy-start | bytes 1540
  1.0 13.0 %copy-start.6 = (s32[64]{0:T(128)S(1)}, s32[64]{0:T(128)}, u32[]{:S(2)}) copy-start(s32[64]{0:T(128)} %param.16) | copy-start | bytes 772
  1.1 19.1 %copy-start.5 = (s32[16,2]{0,1:T(2,128)S(1)}, s32[16,2]{0,1:T(2,128)}, u32[]{:S(2)}) copy-start(s32[16,2]{0,1:T(2,128)} %param.18) | copy-start | bytes 388
  5.1 30.6 %all-to-all-start = ((bf16[4,16,896]{2,1,0:T(8,128)(2,1)}), bf16[4,16,896]{2,1,0:T(8,128)(2,1)S(1)}, u32[]{:S(2)}, u32[]{:S(2)}) async-start(bf16[4,16,896]{2,1,0:T(8,128)(2,1)} %broadcast_in_dim.5), calls=%async_computation | async-start | bytes 229376 | tf_op jit(solution)/shard_map/all_to_all | solution.py:271
  47.5 19.3 %all-to-all-start.1 = ((bf16[16,64,560]{2,1,0:T(8,128)(2,1)}), bf16[16,64,560]{2,1,0:T(8,128)(2,1)S(1)}, u32[]{:S(2)}, u32[]{:S(2)}) async-start(bf16[16,64,560]{2,1,0:T(8,128)(2,1)} %fusion.19), calls=%async_computation.1 | async-start | bytes 2621440 | tf_op jit(solution)/shard_map/all_to_all | solution.py:287
  66.8 5.0 %copy-start.3 = (bf16[1024,2048]{1,0:T(8,128)(2,1)S(1)}, bf16[1024,2048]{1,0:T(8,128)(2,1)}, u32[]{:S(2)}) copy-start(bf16[1024,2048]{1,0:T(8,128)(2,1)} %constant.90.clone) | copy-start | bytes 12582916
  75.1 1.0 copy-start.1
  75.1 0.9 copy-start.2
  96.1 9.1 %all-to-all-start.2 = ((bf16[8,48,256]{2,1,0:T(8,128)(2,1)}), bf16[8,48,256]{2,1,0:T(8,128)(2,1)S(1)}, u32[]{:S(2)}, u32[]{:S(2)}) async-start(bf16[8,48,256]{2,1,0:T(8,128)(2,1)} %shard_map.136), calls=%async_computation.2 | async-start | bytes 393216 | tf_op jit(solution)/shard_map/all_to_all | solution.py:307

commit v2 on v1

--- a/solution.py
+++ b/solution.py
@@ -54,8 +54,10 @@
     source, depth, inner = np.meshgrid(np.arange(16), np.arange(4), np.arange(16), indexing="ij")
     rows = ((depth * 16 + source) * 16 + inner).reshape(-1)
     angle = angles(rows[:, None] * (np.arange(GRID) - BAND - REACH)[None, :])
-    table = np.concatenate([np.cos(angle), np.sin(angle)], 1)
-    return two_parts(table / spread_of(TILE)[rows % TILE][:, None])
+    table = np.stack([np.cos(angle), np.sin(angle)], 1).reshape(GRID, 2, GRID // 128, 128)
+    table = table.transpose(0, 2, 1, 3).reshape(GRID, 2 * GRID)
+    table = table / spread_of(TILE)[rows % TILE][:, None]
+    return table.astype(np.float32).astype(ml_dtypes.bfloat16)
 
 
 @functools.lru_cache(maxsize=None)
@@ -87,23 +89,57 @@
     return two_parts(table)
 
 
+def window_kernel(piece_ref, out_ref):
+    for member in range(GROUP):
+        at = WIDE * member
+        for part in range(2):
+            from_at = part * HALF_COLS + at
+            window = piece_ref[:, from_at : from_at + ROWS_IN]
+            for copy in range(2):
+                out_ref[member + copy * GROUP, :, part * ROWS_IN : (part + 1) * ROWS_IN] = window
+
+
+def windows_of(piece):
+    vmem = pl.BlockSpec(memory_space=pltpu.VMEM)
+    return pl.pallas_call(
+        window_kernel,
+        out_shape=jax.ShapeDtypeStruct((2 * GROUP, piece.shape[0], 2 * ROWS_IN), piece.dtype),
+        in_specs=[vmem],
+        out_specs=vmem,
+    )(piece)
+
+
 def field_kernel(
     shift_ref,
     start_ref,
     spread_ref,
-    spec_re,
-    spec_im,
+    columns_ref,
+    table_ref,
     back_ref,
     coef_ref,
     level_ref,
     out_ref,
+    turned_ref,
+    spec_re,
+    spec_im,
     mask,
-    rows,
+    rows_a,
+    rows_b,
     field_re,
     field_im,
     sums_re,
     sums_im,
 ):
+    turned_ref[...] = columns_ref[...].T
+    for chunk in range(GRID // 128):
+        both = jnp.dot(
+            turned_ref[...],
+            table_ref[:, chunk * 256 : (chunk + 1) * 256],
+            preferred_element_type=jnp.float32,
+        )
+        spec_re[chunk] = both[:ROWS_IN, :128] + both[ROWS_IN:, 128:]
+        spec_im[chunk] = both[ROWS_IN:, :128] - both[:ROWS_IN, 128:]
+
     first = start_ref[0]
     row_index = lax.broadcasted_iota(jnp.int32, (WIDE, KU), 0) + first
     lane_index = lax.broadcasted_iota(jnp.int32, (WIDE, KU), 1) - BAND
@@ -112,7 +148,7 @@
     mask[...] = jnp.concatenate([inside, inside], 0).astype(jnp.bfloat16)
     chunks = KU // 128
 
-    def shifted(tilt, at):
+    def shifted(tilt, rows, at):
         row_at = shift_ref[1, tilt]
         lane_at = shift_ref[0, tilt]
         spread = spread_ref[tilt]
@@ -129,21 +165,32 @@
             rolled = pltpu.roll((window * spread).astype(jnp.bfloat16), turn, 1)
             if chunk:
                 lanes_at = (chunk - 1) * 128
-                rows[pl.ds(at, 2 * WIDE), lanes_at : lanes_at + 128] = (
+                rows[at : at + 2 * WIDE, lanes_at : lanes_at + 128] = (
                     jnp.where(keep, before, rolled) * mask[:, lanes_at : lanes_at + 128]
                 )
             before = rolled
 
-    def block(step, carry):
+    def fill(step, rows):
         for spot in range(BATCH):
-            shifted(step * BATCH + spot, spot * 2 * WIDE)
+            shifted(step * BATCH + spot, rows, spot * 2 * WIDE)
+
+    def multiply(step, rows):
         at = pl.multiple_of(step * BLOCK, BLOCK)
         result = jnp.dot(rows[...], back_ref[...], preferred_element_type=jnp.float32)
         field_re[pl.ds(at, BLOCK), :] = result[:, :128]
         field_im[pl.ds(at, BLOCK), :] = result[:, 128:]
+
+    steps = TILTS // BATCH
+    fill(0, rows_a)
+
+    def block(turn, carry):
+        fill(2 * turn + 1, rows_b)
+        multiply(2 * turn, rows_a)
+        fill(jnp.minimum(2 * turn + 2, steps - 1), rows_a)
+        multiply(2 * turn + 1, rows_b)
         return carry
 
-    lax.fori_loop(0, TILTS // BATCH, block, 0)
+    lax.fori_loop(0, steps // 2, block, 0)
 
     count = GROUP * TILE
     for col in range(WIDE):
@@ -183,7 +230,7 @@
             )
 
 
-def field_sums(shifts, start, spec_re, spec_im, back, coef):
+def field_sums(shifts, start, columns, table, back, coef):
     vmem = pl.BlockSpec(memory_space=pltpu.VMEM)
     smem = pl.BlockSpec(memory_space=pltpu.SMEM)
     spread = spread_of(TILTS)
@@ -194,7 +241,11 @@
         in_specs=[smem, smem, smem, vmem, vmem, vmem, vmem, vmem],
         out_specs=vmem,
         scratch_shapes=[
+            pltpu.VMEM((2 * ROWS_IN, GRID), jnp.bfloat16),
+            pltpu.VMEM((GRID // 128, ROWS_IN, 128), jnp.float32),
+            pltpu.VMEM((GRID // 128, ROWS_IN, 128), jnp.float32),
             pltpu.VMEM((2 * WIDE, KU), jnp.bfloat16),
+            pltpu.VMEM((BLOCK, KU), jnp.bfloat16),
             pltpu.VMEM((BLOCK, KU), jnp.bfloat16),
             pltpu.VMEM((TILTS * 2 * WIDE, 128), jnp.float32),
             pltpu.VMEM((TILTS * 2 * WIDE, 128), jnp.float32),
@@ -206,12 +257,33 @@
         shifts,
         start,
         jnp.asarray(spread.astype(np.float32)),
-        spec_re,
-        spec_im,
+        columns,
+        table,
         back,
         coef,
         jnp.asarray(level.astype(np.float32)),
     )
+
+
+def probe_kernel(sums_ref, high_ref, low_ref, out_ref):
+    sums = sums_ref[...].T
+    probe = jnp.dot(sums, high_ref[...], preferred_element_type=jnp.float32) + jnp.dot(
+        sums, low_ref[...], preferred_element_type=jnp.float32
+    )
+    share = out_ref.shape[1]
+    real, imag = probe[:, :share], probe[:, share:]
+    out_ref[...] = real * real + imag * imag
+
+
+def probe_intensity(sums, high, low):
+    vmem = pl.BlockSpec(memory_space=pltpu.VMEM)
+    return pl.pallas_call(
+        probe_kernel,
+        out_shape=jax.ShapeDtypeStruct((sums.shape[1], high.shape[1] // 2), jnp.float32),
+        in_specs=[vmem] * 3,
+        out_specs=vmem,
+        compiler_params=pltpu.CompilerParams(vmem_limit_bytes=32 * 1024 * 1024),
+    )(sums, high, low)
 
 
 def mixing_table(tilt_list, beam_list, beam_table, positions):
@@ -234,6 +306,16 @@
     ).astype(jnp.bfloat16)
 
 
+def doubled(block, axis, place, strides, size):
+    for stride in strides:
+        other = lax.ppermute(block, axis, [(i, i ^ stride) for i in range(size)])
+        upper = jnp.bitwise_and(place, stride) != 0
+        block = jnp.concatenate(
+            [jnp.where(upper, other, block), jnp.where(upper, block, other)], 0
+        )
+    return block
+
+
 def groups(kind):
     flat = np.arange(64).reshape(4, 2, 2, 4)
     if kind == "depth":
@@ -248,12 +330,10 @@
     dev = lax.axis_index("dev")
     group, member = dev // GROUP, dev % GROUP
 
-    tilt_info = lax.all_gather(
-        jnp.concatenate([tilt_ids, beam_index[:, None]], 1), "half", axis=0, tiled=True
-    )
-    spots = lax.all_gather(
-        positions, "dev", axis=0, tiled=True, axis_index_groups=groups("tiles")
-    )
+    tilt_info = doubled(
+        jnp.concatenate([tilt_ids, beam_index[:, None]], 1), "half", half, (1, 2), HALVES
+    )
+    spots = doubled(positions, "dev", dev, (1, 2, 4), 64)
     coef = mixing_table(tilt_info[:, :2], tilt_info[:, 2], beam_table, spots)
 
     first_col = half * (GROUP * WIDE) - BAND - REACH
@@ -271,38 +351,14 @@
     piece = lax.all_to_all(
         piece, "dev", 0, 0, tiled=True, axis_index_groups=groups("depth")
     ).reshape(4 * rows, 2 * HALF_COLS)
-    windows = jnp.stack(
-        [
-            jnp.concatenate(
-                [
-                    piece[:, WIDE * i : WIDE * i + ROWS_IN],
-                    piece[:, HALF_COLS + WIDE * i : HALF_COLS + WIDE * i + ROWS_IN],
-                ],
-                1,
-            )
-            for i in range(GROUP)
-        ]
-    )
-    windows = jnp.concatenate([windows, windows], 0)
     columns = lax.all_to_all(
-        windows, "dev", 0, 0, tiled=True, axis_index_groups=groups("plane")
+        windows_of(piece), "dev", 0, 0, tiled=True, axis_index_groups=groups("plane")
     ).reshape(GRID, 2 * ROWS_IN)
-
-    high, low = row_table()
-    dims = (((0,), (0,)), ((), ()))
-    product = lax.dot_general(
-        columns, jnp.asarray(high), dims, preferred_element_type=jnp.float32
-    ) + lax.dot_general(columns, jnp.asarray(low), dims, preferred_element_type=jnp.float32)
-    spec_re = product[:ROWS_IN, :GRID] + product[ROWS_IN:, GRID:]
-    spec_im = product[ROWS_IN:, :GRID] - product[:ROWS_IN, GRID:]
-    spec_re, spec_im = (
-        x.reshape(ROWS_IN, GRID // 128, 128).transpose(1, 0, 2) for x in (spec_re, spec_im)
-    )
 
     back = lax.dynamic_index_in_dim(jnp.asarray(back_row_table()), group, 0, keepdims=False)
     shifts = (REACH - tilt_info[:, :2]).T
     start = (WIDE * (half * GROUP + member) - BAND).reshape(1)
-    sums = field_sums(shifts, start, spec_re, spec_im, back, coef)
+    sums = field_sums(shifts, start, columns, jnp.asarray(row_table()), back, coef)
 
     sums = lax.all_to_all(sums, "dev", 0, 0, tiled=True, axis_index_groups=groups("tiles"))
     sums = lax.all_gather(sums, "half", axis=0, tiled=True).reshape(PARTS * 2 * WIDE, TILE * TILE)
@@ -311,12 +367,7 @@
         lax.dynamic_index_in_dim(jnp.asarray(t), half, 0, keepdims=False)
         for t in back_column_table()
     )
-    probe = lax.dot_general(sums, high, dims, preferred_element_type=jnp.float32) + lax.dot_general(
-        sums, low, dims, preferred_element_type=jnp.float32
-    )
-    share = GRID // HALVES
-    real, imag = probe[:, :share], probe[:, share:]
-    return (real * real + imag * imag).reshape(TILE, TILE, share)
+    return probe_intensity(sums, high, low).reshape(TILE, TILE, GRID // HALVES)
 
 
 def solution(mesh):

time: 126 us -> 96.2 us (0.76)
  blocking collectives: 36.6 us -> 12.3 us
  matrix products: 15 us -> 3.34 us
  other arithmetic: 14.6 us -> 3.14 us
  starting transfers between devices: 16.2 us -> 26.1 us
  Pallas kernels: 20.1 us -> 24.1 us
  waiting for transfers between devices: 19.5 us -> 22 us
  local copies, waits for them, and re-layouts: 3.18 us -> 4.47 us
    all_gather x2 -> x0, blocking collectives: 21.2 us -> none  [the longest x1 15.3 us: local(): lax.all_gather(positions, 'dev', axis=0, tiled=True, axis_index_groups=gr...]
    dot_general x4 -> x0, matrix products: 11.6 us -> none  [the longest x1 5.01 us: local(): lax.dot_general(columns, jnp.asarray(high), dims, preferred_element_type=...]
    unnamed x17 -> x0, other arithmetic: 11.4 us -> none
    ppermute x0 -> x5, starting transfers between devices: none -> 7.97 us  [doubled(): other = lax.ppermute(block, axis, [(i, i ^ stride) for i in range(size)])]
    pallas_call x0 -> x2, Pallas kernels: none -> 4 us  [the longest x1 2.3 us: windows_of(): pl.pallas_call(window_kernel, out_shape=jax.ShapeDtypeStruct((2 * GROUP,...]
    all_gather x1, blocking collectives: 15.3 us -> 12.3 us  [local(): lax.all_gather(sums, 'half', axis=0, tiled=True)]
    all_to_all x1, starting transfers between devices: 3.83 us -> 6.76 us  [local(): lax.all_to_all(windows_of(piece), 'dev', 0, 0, tiled=True, axis_index_gro...]
    all_to_all x1, waiting for transfers between devices: 13.7 us -> 16.5 us  [local(): lax.all_to_all(windows_of(piece), 'dev', 0, 0, tiled=True, axis_index_gro...]
  transfers between devices with their start and end apart: 3 -> 8, of which waited for: 2 -> 4; matrix products, arithmetic and copies ran while one was open for 2% -> 11% of each run, Pallas kernels for 0% -> 2%
where the time goes in v2:
time: 96.2 us; the launch traced here: 95.6 us
  starting transfers between devices  26.1 us (27%)
  Pallas kernels  24.1 us (25%)
  waiting for transfers between devices  22 us (23%)
  blocking collectives  12.3 us (13%)
  local copies, waits for them, and re-layouts  4.47 us (5%)
  matrix products  3.34 us (3%)
  other arithmetic  3.14 us (3%)
    pallas_call x1, Pallas kernels, field_sums(): pl.pallas_call(field_kernel, out_shape=jax.ShapeDtypeStruct((GROUP, 2 * W...  20.1 us
    all_to_all x1, waiting for transfers between devices, local(): lax.all_to_all(windows_of(piece), 'dev', 0, 0, tiled=True, axis_index_gro...  16.5 us
    all_gather x1, blocking collectives, local(): lax.all_gather(sums, 'half', axis=0, tiled=True)  12.3 us
    all_to_all x1, starting transfers between devices, local(): lax.all_to_all(piece, 'dev', 0, 0, tiled=True, axis_index_groups=groups('...  8.01 us
    ppermute x5, starting transfers between devices, doubled(): other = lax.ppermute(block, axis, [(i, i ^ stride) for i in range(size)])  7.97 us
    all_to_all x1, starting transfers between devices, local(): lax.all_to_all(windows_of(piece), 'dev', 0, 0, tiled=True, axis_index_gro...  6.76 us
    all_to_all x1, waiting for transfers between devices, local(): lax.all_to_all(sums, 'dev', 0, 0, tiled=True, axis_index_groups=groups('t...  3.62 us
    all_to_all x1, starting transfers between devices, local(): lax.all_to_all(sums, 'dev', 0, 0, tiled=True, axis_index_groups=groups('t...  3.39 us
  transfers between devices with their start and end apart: 8, of which 4 were waited for; matrix products, arithmetic and copies ran while one was open for 11% of the time, Pallas kernels for 2%

profile of v2, /device:TPU:1, one launch (start us, length us, event | category | flops | bytes accessed | tf_op | source)
XLA Modules:
  0.0 95.6 jit_solution(11545299087255060139)
XLA Ops:
  0.0 2.2 %collective-permute-start.2 = (s32[16,2]{0,1:T(2,128)}, s32[16,2]{0,1:T(2,128)S(1)}, u32[]{:S(2)}, u32[]{:S(2)}) collective-permute-start(s32[16,2]{0,1:T(2,128)} %param.17), channel_id=1, source_target_pairs={{0,1},{1,0},{2,3},{3,2},{4,5},{5,4},{6,7},{7,6},{8,9},{9,8},{10,11... | collective-permute-start | bytes 392 | tf_op jit(solution)/shard_map/ppermute | solution.py:311
  2.2 0.7 pad_add_fusion
  2.9 1.1 %collective-permute-start = (s32[64,3]{0,1:T(4,128)S(1)}, s32[64,3]{0,1:T(4,128)S(1)}, u32[]{:S(2)}, u32[]{:S(2)}) collective-permute-start(s32[64,3]{0,1:T(4,128)S(1)} %pad_add_fusion), channel_id=1, source_target_pairs={{0,64},{64,0},{128,192},{192,128},{1,65},{65,1},{129,193},{193,129... | collective-permute-start | bytes 2312 | tf_op jit(solution)/shard_map/ppermute | solution.py:311
  4.1 1.0 %cosine_multiply_fusion = (f32[16,1024]{1,0:T(8,128)S(1)}, f32[16,1024]{1,0:T(8,128)S(1)}) fusion(bf16[16,1024]{1,0:T(8,128)(2,1)} %param.13, f32[16]{0:T(128)} %constant.90.clone, f32[1024]{0:T(1024)S(1)} %convert_multiply_fusion.1), kind=kLoop, calls=%fused_computation.17 | loop fusion | flops 65536 | bytes 168000 | tf_op jit(solution)/shard_map/mul | solution.py:343
  5.1 3.1 %fusion.3 = f32[32,896]{1,0:T(8,128)S(1)} fusion(f32[1024,896]{1,0:T(8,128)} %constant.91.clone, f32[16,1024]{1,0:T(8,128)S(1)} %get-tuple-element.8, f32[16,1024]{1,0:T(8,128)S(1)} %get-tuple-element.7), kind=kOutput, calls=%fused_computation.13 | convolution fusion | flops 176193536 | bytes 3915776 | tf_op jit(solution)/shard_map/dot_general | solution.py:344
  8.4 0.7 broadcast_in_dim.5
  9.1 8.0 %all-to-all-start = ((bf16[4,16,896]{2,1,0:T(8,128)(2,1)}), bf16[4,16,896]{2,1,0:T(8,128)(2,1)S(1)}, u32[]{:S(2)}, u32[]{:S(2)}) async-start(bf16[4,16,896]{2,1,0:T(8,128)(2,1)} %broadcast_in_dim.5), calls=%async_computation | async-start | bytes 229376 | tf_op jit(solution)/shard_map/all_to_all | solution.py:351
  17.1 1.0 %dynamic-slice_bitcast_fusion.2.back_ref = bf16[768,256]{1,0:T(8,128)(2,1)S(1)} fusion(bf16[8,768,256]{2,1,0:T(8,128)(2,1)} %constant.92.clone, s32[]{:T(128)S(6)} %select_n.88), kind=kLoop, calls=%fused_computation.2 | loop fusion | bytes 786436 | tf_op jit(solution)/shard_map/jit(dynamic_index_in_dim)/squeeze | solution.py:358
  18.2 2.6 %collective-permute-start.3 = (s32[32,2]{0,1:T(2,128)S(1)}, s32[32,2]{0,1:T(2,128)S(1)}, u32[]{:S(2)}, u32[]{:S(2)}) collective-permute-start(s32[32,2]{0,1:T(2,128)S(1)} %pad_add_fusion.3), channel_id=1, source_target_pairs={{0,2},{1,3},{2,0},{3,1},{4,6},{5,7},{6,4},{7,5},{8,10},{9,11},{10,... | collective-permute-start | bytes 776 | tf_op jit(solution)/shard_map/ppermute | solution.py:311
  20.9 1.3 %collective-permute-done.3 = s32[32,2]{0,1:T(2,128)S(1)} collective-permute-done((s32[32,2]{0,1:T(2,128)S(1)}, s32[32,2]{0,1:T(2,128)S(1)}, u32[]{:S(2)}, u32[]{:S(2)}) %collective-permute-start.3) | collective-permute-done | bytes 288 | tf_op jit(solution)/shard_map/ppermute | solution.py:311
  22.4 1.2 %collective-permute-start.4 = (s32[64,2]{0,1:T(2,128)S(1)}, s32[64,2]{0,1:T(2,128)S(1)}, u32[]{:S(2)}, u32[]{:S(2)}) collective-permute-start(s32[64,2]{0,1:T(2,128)S(1)} %pad_add_fusion.4), channel_id=1, source_target_pairs={{0,4},{1,5},{2,6},{3,7},{4,0},{5,1},{6,2},{7,3},{8,12},{9,13},{10,... | collective-permute-start | bytes 1544 | tf_op jit(solution)/shard_map/ppermute | solution.py:311
  23.7 0.8 collective-permute-start.1
  24.4 0.6 collective-permute-done.4
  25.2 0.6 copy-done.3
  25.9 2.3 %shard_map.127 = bf16[16,64,560]{2,1,0:T(8,128)(2,1)} custom-call(bf16[64,896]{1,0:T(8,128)(2,1)} %bitcast.27), custom_call_target="tpu_custom_call" | custom-call | tf_op jit(solution)/shard_map/pallas_call | solution.py:104
  28.2 6.8 %all-to-all-start.1 = ((bf16[16,64,560]{2,1,0:T(8,128)(2,1)}), bf16[16,64,560]{2,1,0:T(8,128)(2,1)S(1)}, u32[]{:S(2)}, u32[]{:S(2)}) async-start(bf16[16,64,560]{2,1,0:T(8,128)(2,1)} %shard_map.127), calls=%async_computation.1 | async-start | bytes 2621440 | tf_op jit(solution)/shard_map/all_to_all | solution.py:354
  35.3 0.7 negate_convert_fusion
  36.0 16.5 %all-to-all-done.1 = bf16[16,64,560]{2,1,0:T(8,128)(2,1)S(1)} async-done(((bf16[16,64,560]{2,1,0:T(8,128)(2,1)}), bf16[16,64,560]{2,1,0:T(8,128)(2,1)S(1)}, u32[]{:S(2)}, u32[]{:S(2)}) %all-to-all-start.1) | async-done | bytes 1146912 | tf_op jit(solution)/shard_map/all_to_all | solution.py:354
  52.4 20.1 %shard_map.128 = bf16[8,48,256]{2,1,0:T(8,128)(2,1)} custom-call(s32[2,256]{1,0:T(2,128)S(1)} %fusion.10.shift_ref, s32[1]{0:T(128)} %bitcast.2.start_ref, f32[256]{0:T(256)S(1)} %copy-done.2, bf16[1024,560]{1,0:T(8,128)(2,1)S(1)} %bitcast.25, bf16[1024,2048]{1,0:T(8,128)(2,1)} %constant.93.clone.table_ref, ...), custom_call_target="tpu_custom_call" | custom-call | tf_op jit(solution)/shard_map/pallas_call | solution.py:238
  72.5 3.4 %all-to-all-start.2 = ((bf16[8,48,256]{2,1,0:T(8,128)(2,1)}), bf16[8,48,256]{2,1,0:T(8,128)(2,1)S(1)}, u32[]{:S(2)}, u32[]{:S(2)}) async-start(bf16[8,48,256]{2,1,0:T(8,128)(2,1)} %shard_map.128), calls=%async_computation.2 | async-start | bytes 393216 | tf_op jit(solution)/shard_map/all_to_all | solution.py:363
  75.9 2.1 %dynamic-slice_bitcast_fusion = (bf16[1536,512]{1,0:T(8,128)(2,1)S(1)}, bf16[1536,512]{1,0:T(8,128)(2,1)S(1)}) fusion(bf16[4,1536,512]{2,1,0:T(8,128)(2,1)} %constant.97.clone, s32[]{:T(128)S(6)} %select_n.98, bf16[4,1536,512]{2,1,0:T(8,128)(2,1)} %constant.96.clone), kind=kLoop, calls=%fused_computation | loop fusion | bytes 6291460 | tf_op jit(solution)/shard_map/jit(dynamic_index_in_dim)/squeeze | solution.py:367
  78.0 3.6 %all-to-all-done.2 = bf16[8,48,256]{2,1,0:T(8,128)(2,1)S(1)} async-done(((bf16[8,48,256]{2,1,0:T(8,128)(2,1)}), bf16[8,48,256]{2,1,0:T(8,128)(2,1)S(1)}, u32[]{:S(2)}, u32[]{:S(2)}) %all-to-all-start.2) | async-done | bytes 196640 | tf_op jit(solution)/shard_map/all_to_all | solution.py:363
  81.6 12.3 %all_gather.3 = bf16[32,48,256]{2,1,0:T(8,128)(2,1)S(1)} all-gather(bf16[8,48,256]{2,1,0:T(8,128)(2,1)S(1)} %all-to-all-done.2), channel_id=1, replica_groups=mesh['half'=4,'dev'=64] {'half'}, dimensions={0}, use_global_device_ids=true | all-gather | bytes 983040 | tf_op jit(solution)/shard_map/all_gather | solution.py:364
  93.9 1.7 %shard_map.129 = f32[256,256]{1,0:T(8,128)} custom-call(bf16[1536,256]{1,0:T(8,128)(2,1)S(1)} %bitcast.26, bf16[1536,512]{1,0:T(8,128)(2,1)S(1)} %get-tuple-element.30.high_ref, bf16[1536,512]{1,0:T(8,128)(2,1)S(1)} %get-tuple-element.29.low_ref), custom_call_target="tpu_custom_call" | custom-call | tf_op jit(solution)/shard_map/pallas_call | solution.py:280
  (35 shorter events, 1.0 us)
Async XLA Ops:
  0.0 35.1 %copy-start = (f32[16,2]{0,1:T(2,128)S(1)}, f32[16,2]{0,1:T(2,128)}, u32[]{:S(2)}) copy-start(f32[16,2]{0,1:T(2,128)} %param.16) | copy-start | bytes 388
  0.0 18.1 %copy-start.6 = (s32[16,2]{0,1:T(2,128)S(1)}, s32[16,2]{0,1:T(2,128)}, u32[]{:S(2)}) copy-start(s32[16,2]{0,1:T(2,128)} %param.17) | copy-start | bytes 388
  0.0 23.6 %copy-start.4 = (s32[64,2]{0,1:T(2,128)S(1)}, s32[64,2]{0,1:T(2,128)}, u32[]{:S(2)}) copy-start(s32[64,2]{0,1:T(2,128)} %param.14) | copy-start | bytes 1540
  0.0 23.6 %copy-start.5 = (s32[64]{0:T(128)S(1)}, s32[64]{0:T(128)}, u32[]{:S(2)}) copy-start(s32[64]{0:T(128)} %param.15) | copy-start | bytes 772
  0.0 18.1 %collective-permute-start.2 = (s32[16,2]{0,1:T(2,128)}, s32[16,2]{0,1:T(2,128)S(1)}, u32[]{:S(2)}, u32[]{:S(2)}) collective-permute-start(s32[16,2]{0,1:T(2,128)} %param.17), channel_id=1, source_target_pairs={{0,1},{1,0},{2,3},{3,2},{4,5},{5,4},{6,7},{7,6},{8,9},{9,8},{10,11... | collective-permute-start | bytes 392 | tf_op jit(solution)/shard_map/ppermute | solution.py:311
  2.9 20.6 %collective-permute-start = (s32[64,3]{0,1:T(4,128)S(1)}, s32[64,3]{0,1:T(4,128)S(1)}, u32[]{:S(2)}, u32[]{:S(2)}) collective-permute-start(s32[64,3]{0,1:T(4,128)S(1)} %pad_add_fusion), channel_id=1, source_target_pairs={{0,64},{64,0},{128,192},{192,128},{1,65},{65,1},{129,193},{193,129... | collective-permute-start | bytes 2312 | tf_op jit(solution)/shard_map/ppermute | solution.py:311
  8.2 44.2 %copy-start.1 = (f32[512,128]{1,0:T(8,128)S(1)}, f32[512,128]{1,0:T(8,128)}, u32[]{:S(2)}) copy-start(f32[512,128]{1,0:T(8,128)} %constant.95.clone.level_ref) | copy-start | bytes 786436
  8.2 44.2 %copy-start.2 = (f32[256]{0:T(256)S(1)}, f32[256]{0:T(256)}, u32[]{:S(2)}) copy-start(f32[256]{0:T(256)} %constant.94.clone.spread_ref) | copy-start | bytes 3076
  9.1 16.2 %all-to-all-start = ((bf16[4,16,896]{2,1,0:T(8,128)(2,1)}), bf16[4,16,896]{2,1,0:T(8,128)(2,1)S(1)}, u32[]{:S(2)}, u32[]{:S(2)}) async-start(bf16[4,16,896]{2,1,0:T(8,128)(2,1)} %broadcast_in_dim.5), calls=%async_computation | async-start | bytes 229376 | tf_op jit(solution)/shard_map/all_to_all | solution.py:351
  18.2 4.0 %collective-permute-start.3 = (s32[32,2]{0,1:T(2,128)S(1)}, s32[32,2]{0,1:T(2,128)S(1)}, u32[]{:S(2)}, u32[]{:S(2)}) collective-permute-start(s32[32,2]{0,1:T(2,128)S(1)} %pad_add_fusion.3), channel_id=1, source_target_pairs={{0,2},{1,3},{2,0},{3,1},{4,6},{5,7},{6,4},{7,5},{8,10},{9,11},{10,... | collective-permute-start | bytes 776 | tf_op jit(solution)/shard_map/ppermute | solution.py:311
  22.4 2.7 %collective-permute-start.4 = (s32[64,2]{0,1:T(2,128)S(1)}, s32[64,2]{0,1:T(2,128)S(1)}, u32[]{:S(2)}, u32[]{:S(2)}) collective-permute-start(s32[64,2]{0,1:T(2,128)S(1)} %pad_add_fusion.4), channel_id=1, source_target_pairs={{0,4},{1,5},{2,6},{3,7},{4,0},{5,1},{6,2},{7,3},{8,12},{9,13},{10,... | collective-permute-start | bytes 1544 | tf_op jit(solution)/shard_map/ppermute | solution.py:311
  23.7 11.3 %collective-permute-start.1 = (s32[128,3]{0,1:T(4,128)S(1)}, s32[128,3]{0,1:T(4,128)S(1)}, u32[]{:S(2)}, u32[]{:S(2)}) collective-permute-start(s32[128,3]{0,1:T(4,128)S(1)} %pad_add_fusion.1), channel_id=1, source_target_pairs={{0,128},{64,192},{128,0},{192,64},{1,129},{65,193},{129,1},{193,65... | collective-permute-start | bytes 4616 | tf_op jit(solution)/shard_map/ppermute | solution.py:311
  25.2 0.6 copy-start.3
  28.2 24.3 %all-to-all-start.1 = ((bf16[16,64,560]{2,1,0:T(8,128)(2,1)}), bf16[16,64,560]{2,1,0:T(8,128)(2,1)S(1)}, u32[]{:S(2)}, u32[]{:S(2)}) async-start(bf16[16,64,560]{2,1,0:T(8,128)(2,1)} %shard_map.127), calls=%async_computation.1 | async-start | bytes 2621440 | tf_op jit(solution)/shard_map/all_to_all | solution.py:354
  72.5 9.1 %all-to-all-start.2 = ((bf16[8,48,256]{2,1,0:T(8,128)(2,1)}), bf16[8,48,256]{2,1,0:T(8,128)(2,1)S(1)}, u32[]{:S(2)}, u32[]{:S(2)}) async-start(bf16[8,48,256]{2,1,0:T(8,128)(2,1)} %shard_map.128), calls=%async_computation.2 | async-start | bytes 393216 | tf_op jit(solution)/shard_map/all_to_all | solution.py:363

commit v3 on v2

--- a/solution.py
+++ b/solution.py
@@ -22,8 +22,10 @@
 TILE = 16
 WIDE = 24
 PARTS = GROUP * HALVES
-ROWS_IN = WIDE + 2 * REACH
-HALF_COLS = GROUP * WIDE + 2 * REACH
+ROWS_IN = 2 * WIDE + 2 * REACH
+CHIP_COLS = GROUP * 2 * WIDE + 2 * REACH
+NOTE = 4
+LANES = 2 * ROWS_IN + NOTE
 KU = 768
 BATCH = 16
 BLOCK = 2 * BATCH * WIDE
@@ -45,19 +47,22 @@
 
 @functools.lru_cache(maxsize=None)
 def column_table():
-    angle = angles(np.arange(GRID)[:, None] * np.arange(HALF_COLS)[None, :])
-    return np.concatenate([np.cos(angle), np.sin(angle)], 1).astype(np.float32)
+    angle = angles(np.arange(GRID)[:, None] * np.arange(128)[None, :])
+    return np.stack(two_parts(np.concatenate([np.cos(angle), np.sin(angle)], 1)))
 
 
 @functools.lru_cache(maxsize=None)
 def row_table():
-    source, depth, inner = np.meshgrid(np.arange(16), np.arange(4), np.arange(16), indexing="ij")
-    rows = ((depth * 16 + source) * 16 + inner).reshape(-1)
-    angle = angles(rows[:, None] * (np.arange(GRID) - BAND - REACH)[None, :])
-    table = np.stack([np.cos(angle), np.sin(angle)], 1).reshape(GRID, 2, GRID // 128, 128)
-    table = table.transpose(0, 2, 1, 3).reshape(GRID, 2 * GRID)
-    table = table / spread_of(TILE)[rows % TILE][:, None]
-    return table.astype(np.float32).astype(ml_dtypes.bfloat16)
+    core, pair, source, depth, inner = np.meshgrid(
+        np.arange(2), np.arange(2), np.arange(16), np.arange(4), np.arange(4), indexing="ij"
+    )
+    inner = 4 * inner + 2 * pair + core
+    rows = ((depth * 16 + source) * TILE + inner).reshape(4, GRID // 4)
+    angle = angles(rows[:, :, None] * (np.arange(GRID // 4) - BAND - REACH)[None, None, :])
+    table = np.stack([np.cos(angle), np.sin(angle)], 2)
+    table = table / spread_of(TILE)[rows % TILE][:, :, None, None]
+    table = table.reshape(2, 2, GRID // 4, 2, 2, 128).transpose(0, 1, 2, 4, 3, 5)
+    return table.reshape(2, 2, GRID // 4, 512).astype(np.float32).astype(ml_dtypes.bfloat16)
 
 
 @functools.lru_cache(maxsize=None)
@@ -75,7 +80,9 @@
 
 @functools.lru_cache(maxsize=None)
 def back_column_table():
-    index = np.arange(PARTS * WIDE) - BAND
+    chip, core, member = np.meshgrid(np.arange(2), np.arange(2), np.arange(GROUP), indexing="ij")
+    part = (chip * 2 * GROUP + member * 2 + core).reshape(-1)
+    index = (part[:, None] * WIDE + np.arange(WIDE)[None, :]).reshape(-1) - BAND
     cols = np.arange(GRID)
     angle = angles(index[:, None] * cols[None, :])
     angle = angle - (propagation_rate / GRID) * (index * index).astype(np.float64)[:, None]
@@ -89,36 +96,100 @@
     return two_parts(table)
 
 
-def window_kernel(piece_ref, out_ref):
+def chosen(rows, cols, source):
+    row = lax.broadcasted_iota(jnp.int32, (rows, cols), 0)
+    col = lax.broadcasted_iota(jnp.int32, (rows, cols), 1)
+    return jnp.where(col == source(row), 1.0, 0.0).astype(jnp.bfloat16)
+
+
+def column_kernel(place_ref, field_ref, spread_ref, table_ref, out_ref, table, arrived):
+    copy = pltpu.make_async_copy(table_ref, table, arrived)
+    copy.start()
+    first, core = place_ref[0], place_ref[1]
+    rows = field_ref.shape[0] // 2
+    pick = chosen(rows, 2 * rows, lambda row: 4 * (row % 4) + 2 * (row // 4) + core)
+    field = jnp.dot(pick, field_ref[...], preferred_element_type=jnp.float32)
+    spread = spread_ref[core][:, :1]
+    column = lax.broadcasted_iota(jnp.int32, (rows, GRID), 1)
+    waves = []
+    for chunk in range(CHIP_COLS // 128):
+        turn = jnp.bitwise_and((first + 128 * chunk) * column, GRID - 1)
+        phase = field - (two_pi / GRID) * turn.astype(jnp.float32)
+        waves += [jnp.cos(phase) * spread, jnp.sin(phase) * spread]
+    wave = jnp.concatenate(waves, 0)
+    high = wave.astype(jnp.bfloat16)
+    low = (wave - high.astype(jnp.float32)).astype(jnp.bfloat16)
+    count = wave.shape[0]
+    copy.wait()
+    both = jnp.dot(jnp.concatenate([high, low], 0), table[0], preferred_element_type=jnp.float32)
+    mixed = both[:count] + both[count:]
+    mixed = mixed + jnp.dot(high, table[1], preferred_element_type=jnp.float32)
+    cols_re, cols_im = [], []
+    for chunk in range(CHIP_COLS // 128):
+        cosine = mixed[2 * rows * chunk : 2 * rows * chunk + rows]
+        sine = mixed[2 * rows * chunk + rows : 2 * rows * (chunk + 1)]
+        cols_re.append(cosine[:, :128] + sine[:, 128:])
+        cols_im.append(sine[:, :128] - cosine[:, 128:])
+    piece = jnp.concatenate(cols_re + cols_im, 1).astype(jnp.bfloat16)
+    for copy in range(out_ref.shape[0]):
+        out_ref[copy] = piece
+
+
+def column_piece(place, potential):
+    vmem = pl.BlockSpec(memory_space=pltpu.VMEM)
+    smem = pl.BlockSpec(memory_space=pltpu.SMEM)
+    table = column_table()
+    rows = potential.shape[0]
+    spread = spread_of(TILE).reshape(4, 2, 2).transpose(2, 1, 0).reshape(2, TILE // 2, 1)
+    spread = np.broadcast_to(spread, (2, TILE // 2, 128)).astype(np.float32)
+    return pl.pallas_call(
+        column_kernel,
+        out_shape=jax.ShapeDtypeStruct((4, rows // 2, 2 * CHIP_COLS), jnp.bfloat16),
+        in_specs=[smem, vmem, vmem, pl.BlockSpec(memory_space=pl.ANY)],
+        out_specs=vmem,
+        scratch_shapes=[pltpu.VMEM(table.shape, jnp.bfloat16), pltpu.SemaphoreType.DMA],
+        compiler_params=pltpu.CompilerParams(vmem_limit_bytes=16 * 1024 * 1024),
+    )(place, potential, jnp.asarray(spread), jnp.asarray(table))
+
+
+def window_kernel(piece_ref, note_ref, out_ref):
+    rows = piece_ref.shape[0]
+    pick = chosen(rows, rows, lambda row: 8 * ((row // 4) % 4) + 4 * (row // 16) + row % 4)
+    piece = jnp.dot(pick, piece_ref[...], preferred_element_type=jnp.float32)
+    note = note_ref[...]
     for member in range(GROUP):
-        at = WIDE * member
-        for part in range(2):
-            from_at = part * HALF_COLS + at
-            window = piece_ref[:, from_at : from_at + ROWS_IN]
-            for copy in range(2):
-                out_ref[member + copy * GROUP, :, part * ROWS_IN : (part + 1) * ROWS_IN] = window
-
-
-def windows_of(piece):
+        at = 2 * WIDE * member
+        window = jnp.concatenate(
+            [piece[:, part * CHIP_COLS + at : part * CHIP_COLS + at + ROWS_IN] for part in range(2)]
+            + [note],
+            1,
+        ).astype(jnp.bfloat16)
+        for copy in range(2):
+            out_ref[member + copy * GROUP] = window
+
+
+def windows_of(piece, note):
     vmem = pl.BlockSpec(memory_space=pltpu.VMEM)
     return pl.pallas_call(
         window_kernel,
-        out_shape=jax.ShapeDtypeStruct((2 * GROUP, piece.shape[0], 2 * ROWS_IN), piece.dtype),
-        in_specs=[vmem],
+        out_shape=jax.ShapeDtypeStruct((2 * GROUP, piece.shape[0], LANES), jnp.bfloat16),
+        in_specs=[vmem, vmem],
         out_specs=vmem,
-    )(piece)
+        compiler_params=pltpu.CompilerParams(vmem_limit_bytes=16 * 1024 * 1024),
+    )(piece, note)
 
 
 def field_kernel(
     shift_ref,
     start_ref,
-    spread_ref,
-    columns_ref,
+    own_ref,
+    mate_ref,
     table_ref,
     back_ref,
     coef_ref,
-    level_ref,
     out_ref,
+    table,
+    arrived,
     turned_ref,
     spec_re,
     spec_im,
@@ -130,15 +201,59 @@
     sums_re,
     sums_im,
 ):
-    turned_ref[...] = columns_ref[...].T
+    copy = pltpu.make_async_copy(table_ref, table, arrived)
+    copy.start()
+    core = start_ref[1]
+    for pair in range(2):
+        for place, ref in ((core, own_ref), (1 - core, mate_ref)):
+            block = ref[:, 16 * pair : 16 * pair + 16, :]
+            block = block.reshape(GRID // 4, LANES)[:, : 2 * ROWS_IN]
+            turned_ref[2 * pair + place] = block.T
+    copy.wait()
+    for part in range(2):
+        lanes = slice(256 * part, 256 * (part + 1))
+        each = []
+        for remainder in range(4):
+            both = jnp.dot(
+                turned_ref[remainder],
+                table[remainder % 2, remainder // 2, :, lanes],
+                preferred_element_type=jnp.float32,
+            )
+            each.append(
+                (
+                    both[:ROWS_IN, :128] + both[ROWS_IN:, 128:],
+                    both[ROWS_IN:, :128] - both[:ROWS_IN, 128:],
+                )
+            )
+        (re0, im0), (re1, im1), (re2, im2), (re3, im3) = each
+        even, even_less = (re0 + re2, im0 + im2), (re0 - re2, im0 - im2)
+        odd, odd_less = (re1 + re3, im1 + im3), (im1 - im3, re3 - re1)
+        for quarter, left, right, sign in (
+            (0, even, odd, 1),
+            (1, even_less, odd_less, 1),
+            (2, even, odd, -1),
+            (3, even_less, odd_less, -1),
+        ):
+            for ref, x, y in ((spec_re, left[0], right[0]), (spec_im, left[1], right[1])):
+                ref[2 * quarter + part] = x + y if sign > 0 else x - y
+
+    peak_row = start_ref[2]
+    peak_at = jnp.clip(peak_row, 0, ROWS_IN - 1)
+    peak_lane = BAND + REACH
+    peak_re, peak_im = (
+        ref[peak_lane // 128, pl.ds(peak_at, 1), :][:, peak_lane % 128 : peak_lane % 128 + 1]
+        for ref in (spec_re, spec_im)
+    )
+    power = peak_re * peak_re + peak_im * peak_im
+    held = jnp.logical_and(power > 1e-6, peak_row == peak_at)
+    peak_re = jnp.where(held, peak_re, 1.0)
+    peak_im = jnp.where(held, peak_im, 0.0)
+    inverse = 1.0 / jnp.where(held, power, 1.0)
+    scale_re, scale_im = peak_re * inverse, -peak_im * inverse
     for chunk in range(GRID // 128):
-        both = jnp.dot(
-            turned_ref[...],
-            table_ref[:, chunk * 256 : (chunk + 1) * 256],
-            preferred_element_type=jnp.float32,
-        )
-        spec_re[chunk] = both[:ROWS_IN, :128] + both[ROWS_IN:, 128:]
-        spec_im[chunk] = both[ROWS_IN:, :128] - both[:ROWS_IN, 128:]
+        value_re, value_im = spec_re[chunk], spec_im[chunk]
+        spec_re[chunk] = value_re * scale_re - value_im * scale_im
+        spec_im[chunk] = value_re * scale_im + value_im * scale_re
 
     first = start_ref[0]
     row_index = lax.broadcasted_iota(jnp.int32, (WIDE, KU), 0) + first
@@ -151,7 +266,6 @@
     def shifted(tilt, rows, at):
         row_at = shift_ref[1, tilt]
         lane_at = shift_ref[0, tilt]
-        spread = spread_ref[tilt]
         base = jnp.where(lane_at >= 128, 1, 0)
         rest = lane_at - 128 * base
         lanes = lax.broadcasted_iota(jnp.int32, (2 * WIDE, 128), 1)
@@ -162,7 +276,7 @@
             window = jnp.concatenate(
                 [ref[base + chunk, pl.ds(row_at, WIDE), :] for ref in (spec_re, spec_im)], 0
             )
-            rolled = pltpu.roll((window * spread).astype(jnp.bfloat16), turn, 1)
+            rolled = pltpu.roll(window.astype(jnp.bfloat16), turn, 1)
             if chunk:
                 lanes_at = (chunk - 1) * 128
                 rows[at : at + 2 * WIDE, lanes_at : lanes_at + 128] = (
@@ -198,16 +312,12 @@
             [
                 jnp.concatenate(
                     [ref[pl.ds(col + WIDE * part, TILTS, stride=2 * WIDE), :] for part in range(2)], 0
-                )
-                * level_ref[...]
+                ).astype(jnp.bfloat16)
                 for ref in (field_re, field_im)
             ],
             1,
         )
-        high = values.astype(jnp.bfloat16)
-        low = (values - high.astype(jnp.float32)).astype(jnp.bfloat16)
-        mixed = jnp.dot(coef_ref[...], high, preferred_element_type=jnp.float32)
-        mixed = mixed + jnp.dot(coef_ref[...], low, preferred_element_type=jnp.float32)
+        mixed = jnp.dot(coef_ref[...], values, preferred_element_type=jnp.float32)
         sums_re[pl.ds(col, count, stride=WIDE), :] = mixed[:count, :count] - mixed[count:, count:]
         sums_im[pl.ds(col, count, stride=WIDE), :] = mixed[count:, :count] + mixed[:count, count:]
 
@@ -225,23 +335,24 @@
                         turned = pltpu.roll(turned, turn, 1)
                     total = jnp.where(block_of == spot, turned, total)
                 parts.append(total)
+            parts = [parts[0] * peak_re - parts[1] * peak_im, parts[0] * peak_im + parts[1] * peak_re]
             out_ref[tile, :, half * 128 : (half + 1) * 128] = jnp.concatenate(parts, 0).astype(
                 out_ref.dtype
             )
 
 
-def field_sums(shifts, start, columns, table, back, coef):
+def field_sums(shifts, start, own, mate, table, back, coef):
     vmem = pl.BlockSpec(memory_space=pltpu.VMEM)
     smem = pl.BlockSpec(memory_space=pltpu.SMEM)
-    spread = spread_of(TILTS)
-    level = np.tile(np.broadcast_to((1.0 / spread)[:, None], (TILTS, 128)), (2, 1))
     return pl.pallas_call(
         field_kernel,
         out_shape=jax.ShapeDtypeStruct((GROUP, 2 * WIDE, TILE * TILE), jnp.bfloat16),
-        in_specs=[smem, smem, smem, vmem, vmem, vmem, vmem, vmem],
+        in_specs=[smem, smem, vmem, vmem, pl.BlockSpec(memory_space=pl.ANY), vmem, vmem],
         out_specs=vmem,
         scratch_shapes=[
-            pltpu.VMEM((2 * ROWS_IN, GRID), jnp.bfloat16),
+            pltpu.VMEM((2, 2, GRID // 4, 512), jnp.bfloat16),
+            pltpu.SemaphoreType.DMA,
+            pltpu.VMEM((4, 2 * ROWS_IN, GRID // 4), jnp.bfloat16),
             pltpu.VMEM((GRID // 128, ROWS_IN, 128), jnp.float32),
             pltpu.VMEM((GRID // 128, ROWS_IN, 128), jnp.float32),
             pltpu.VMEM((2 * WIDE, KU), jnp.bfloat16),
@@ -256,12 +367,11 @@
     )(
         shifts,
         start,
-        jnp.asarray(spread.astype(np.float32)),
-        columns,
+        own,
+        mate,
         table,
         back,
         coef,
-        jnp.asarray(level.astype(np.float32)),
     )
 
 
@@ -328,37 +438,40 @@
 def local(potential, tilt_ids, beam_index, beam_table, positions):
     half = lax.axis_index("half")
     dev = lax.axis_index("dev")
+    chip, core = half // 2, half % 2
+    rows = potential.shape[0]
+
+    first_col = chip * (2 * GROUP * WIDE) - BAND - REACH
+    piece = column_piece(jnp.stack([first_col, core]).astype(jnp.int32), potential)
+    piece, tilt_ids, beam_index, positions, dev = lax.optimization_barrier(
+        (piece, tilt_ids, beam_index, positions, dev)
+    )
     group, member = dev // GROUP, dev % GROUP
-
-    tilt_info = doubled(
-        jnp.concatenate([tilt_ids, beam_index[:, None]], 1), "half", half, (1, 2), HALVES
-    )
-    spots = doubled(positions, "dev", dev, (1, 2, 4), 64)
+    info = jnp.concatenate([tilt_ids, beam_index[:, None]], 1)
+    info = doubled(info, "half", half, (1,), HALVES)
+    piece = lax.all_to_all(piece, "dev", 0, 0, tiled=True, axis_index_groups=groups("depth"))
+    piece = piece.reshape(2 * rows, 2 * CHIP_COLS)
+    note = jnp.concatenate([positions >> 7, jnp.bitwise_and(positions, 127)], 1)
+    note = jnp.concatenate([note, jnp.zeros_like(note)], 0).astype(jnp.float32)
+    windows, info = lax.optimization_barrier((windows_of(piece, note), info))
+    tilt_info = doubled(info, "half", half, (2,), HALVES)
+    columns = lax.all_to_all(
+        windows, "dev", 0, 0, tiled=True, axis_index_groups=groups("plane")
+    )
+    mate = lax.ppermute(columns, "half", [(i, i ^ 1) for i in range(HALVES)])
+
+    notes = columns[:, : positions.shape[0], 2 * ROWS_IN :].astype(jnp.int32)
+    notes = lax.dynamic_slice_in_dim(notes, (group % 2) * GROUP, GROUP, 0)
+    notes = notes.reshape(GROUP * positions.shape[0], NOTE)
+    spots = notes[:, :2] * 128 + notes[:, 2:]
     coef = mixing_table(tilt_info[:, :2], tilt_info[:, 2], beam_table, spots)
 
-    first_col = half * (GROUP * WIDE) - BAND - REACH
-    turn = jnp.bitwise_and(first_col * jnp.arange(GRID, dtype=jnp.int32), GRID - 1)
-    phase = potential.astype(jnp.float32) - (two_pi / GRID) * turn.astype(jnp.float32)[None, :]
-    spread = jnp.asarray(spread_of(TILE).astype(np.float32))[:, None]
-    wave = jnp.concatenate([jnp.cos(phase) * spread, jnp.sin(phase) * spread], 0)
-    mixed = jnp.dot(wave, jnp.asarray(column_table()), precision=lax.Precision.HIGH)
-    rows = potential.shape[0]
-    cols_re = mixed[:rows, :HALF_COLS] + mixed[rows:, HALF_COLS:]
-    cols_im = mixed[rows:, :HALF_COLS] - mixed[:rows, HALF_COLS:]
-    piece = jnp.concatenate([cols_re, cols_im], 1).astype(jnp.bfloat16)
-
-    piece = jnp.broadcast_to(piece[None], (4,) + piece.shape)
-    piece = lax.all_to_all(
-        piece, "dev", 0, 0, tiled=True, axis_index_groups=groups("depth")
-    ).reshape(4 * rows, 2 * HALF_COLS)
-    columns = lax.all_to_all(
-        windows_of(piece), "dev", 0, 0, tiled=True, axis_index_groups=groups("plane")
-    ).reshape(GRID, 2 * ROWS_IN)
-
     back = lax.dynamic_index_in_dim(jnp.asarray(back_row_table()), group, 0, keepdims=False)
-    shifts = (REACH - tilt_info[:, :2]).T
-    start = (WIDE * (half * GROUP + member) - BAND).reshape(1)
-    sums = field_sums(shifts, start, columns, jnp.asarray(row_table()), back, coef)
+    shifts = (REACH - tilt_info[:, :2]).T + jnp.stack([jnp.int32(0), WIDE * core])[:, None]
+    first = WIDE * (chip * 2 * GROUP + member * 2 + core) - BAND
+    zero_row = BAND + REACH - 2 * WIDE * (chip * GROUP + member)
+    start = jnp.stack([first, core, zero_row]).astype(jnp.int32)
+    sums = field_sums(shifts, start, columns, mate, jnp.asarray(row_table()), back, coef)
 
     sums = lax.all_to_all(sums, "dev", 0, 0, tiled=True, axis_index_groups=groups("tiles"))
     sums = lax.all_gather(sums, "half", axis=0, tiled=True).reshape(PARTS * 2 * WIDE, TILE * TILE)

time: 96.2 us -> 83.1 us (0.86)
  waiting for transfers between devices: 22 us -> 17.3 us
  matrix products: 3.34 us -> 0.19 us
  Pallas kernels: 24.1 us -> 21.1 us
  blocking collectives: 12.3 us -> 9.67 us
  local copies, waits for them, and re-layouts: 4.47 us -> 6.28 us
  starting transfers between devices: 26.1 us -> 24.7 us
    all_to_all x1, waiting for transfers between devices: 16.5 us -> 10 us  [local(): lax.all_to_all(windows, 'dev', 0, 0, tiled=True, axis_index_groups=groups...]
    ppermute x5 -> x2, starting transfers between devices: 7.97 us -> 1.7 us  [doubled(): other = lax.ppermute(block, axis, [(i, i ^ stride) for i in range(size)])]
    pallas_call x1, Pallas kernels: 20.1 us -> 15.8 us  [field_sums(): pl.pallas_call(field_kernel, out_shape=jax.ShapeDtypeStruct((GROUP, 2 * W...]
    ppermute x0 -> x1, starting transfers between devices: none -> 3.78 us  [local(): mate = lax.ppermute(columns, 'half', [(i, i ^ 1) for i in range(HALVES)])]
    dot_general x1 -> x0, matrix products: 3.15 us -> none  [local(): jnp.dot(wave, jnp.asarray(column_table()), precision=lax.Precision.HIGH)]
    all_to_all x1, waiting for transfers between devices: 0.01 us -> 2.61 us  [local(): lax.all_to_all(piece, 'dev', 0, 0, tiled=True, axis_index_groups=groups('...]
    all_gather x1, blocking collectives: 12.3 us -> 9.67 us  [local(): lax.all_gather(sums, 'half', axis=0, tiled=True)]
    pallas_call x0 -> x1, Pallas kernels: none -> 2.36 us  [column_piece(): pl.pallas_call(column_kernel, out_shape=jax.ShapeDtypeStruct((4, rows //...]
  transfers between devices with their start and end apart: 8 -> 6, of which waited for: 4 -> 4; matrix products, arithmetic and copies ran while one was open for 11% -> 8% of each run, Pallas kernels for 2% -> 0%
where the time goes in v3:
time: 83.1 us; the launch traced here: 82.5 us
  starting transfers between devices  24.7 us (30%)
  Pallas kernels  21.1 us (25%)
  waiting for transfers between devices  17.3 us (21%)
  blocking collectives  9.67 us (12%)
  local copies, waits for them, and re-layouts  6.28 us (8%)
  other arithmetic  3.15 us (4%)
    pallas_call x1, Pallas kernels, field_sums(): pl.pallas_call(field_kernel, out_shape=jax.ShapeDtypeStruct((GROUP, 2 * W...  15.8 us
    all_to_all x1, waiting for transfers between devices, local(): lax.all_to_all(windows, 'dev', 0, 0, tiled=True, axis_index_groups=groups...  10 us
    all_gather x1, blocking collectives, local(): lax.all_gather(sums, 'half', axis=0, tiled=True)  9.67 us
    all_to_all x1, starting transfers between devices, local(): lax.all_to_all(piece, 'dev', 0, 0, tiled=True, axis_index_groups=groups('...  9.02 us
    all_to_all x1, starting transfers between devices, local(): lax.all_to_all(windows, 'dev', 0, 0, tiled=True, axis_index_groups=groups...  6.76 us
    ppermute x1, starting transfers between devices, local(): mate = lax.ppermute(columns, 'half', [(i, i ^ 1) for i in range(HALVES)])  3.78 us
    all_to_all x1, waiting for transfers between devices, local(): lax.all_to_all(sums, 'dev', 0, 0, tiled=True, axis_index_groups=groups('t...  3.62 us
    all_to_all x1, starting transfers between devices, local(): lax.all_to_all(sums, 'dev', 0, 0, tiled=True, axis_index_groups=groups('t...  3.4 us
  transfers between devices with their start and end apart: 6, of which 4 were waited for; matrix products, arithmetic and copies ran while one was open for 8% of the time, Pallas kernels for 0%

profile of v3, /device:TPU:1, one launch (start us, length us, event | category | flops | bytes accessed | tf_op | source)
XLA Modules:
  0.0 82.5 jit_solution(8799866715288272130)
XLA Ops:
  0.1 1.3 %copy-done.2 = bf16[2,1024,256]{2,1,0:T(8,128)(2,1)S(1)} copy-done((bf16[2,1024,256]{2,1,0:T(8,128)(2,1)S(1)}, bf16[2,1024,256]{2,1,0:T(8,128)(2,1)}, u32[]{:S(2)}) %copy-start.2) | copy-done | bytes 1048600
  1.4 0.8 copy-done.3
  2.1 0.7 copy-done.4
  2.8 2.4 %shard_map.109 = bf16[4,8,1280]{2,1,0:T(8,128)(2,1)} custom-call(s32[2]{0:T(128)S(1)} %pad_add_fusion.4.place_ref, bf16[16,1024]{1,0:T(8,128)(2,1)S(1)} %copy-done.3, f32[2,8,128]{2,1,0:T(8,128)S(1)} %copy-done.4, bf16[2,1024,256]{2,1,0:T(8,128)(2,1)S(1)} %copy-done.2), custom_call_target="tpu_custom_call" | custom-call | tf_op jit(solution)/shard_map/pallas_call | solution.py:145
  5.2 9.0 %all-to-all-start = ((bf16[4,8,1280]{2,1,0:T(8,128)(2,1)}), bf16[4,8,1280]{2,1,0:T(8,128)(2,1)S(1)}, u32[]{:S(2)}, u32[]{:S(2)}) async-start(bf16[4,8,1280]{2,1,0:T(8,128)(2,1)} %shard_map.109), calls=%async_computation | async-start | bytes 163840 | tf_op jit(solution)/shard_map/all_to_all | solution.py:452
  14.2 0.7 pad_add_fusion.1
  14.9 1.0 %collective-permute-start = (s32[64,3]{0,1:T(4,128)S(1)}, s32[64,3]{0,1:T(4,128)S(1)}, u32[]{:S(2)}, u32[]{:S(2)}) collective-permute-start(s32[64,3]{0,1:T(4,128)S(1)} %pad_add_fusion.1), channel_id=1, source_target_pairs={{0,64},{64,0},{128,192},{192,128},{1,65},{65,1},{129,193},{193,129... | collective-permute-start | bytes 2312 | tf_op jit(solution)/shard_map/ppermute | solution.py:421
  15.9 0.7 broadcast_shift-right-arithmetic_fusion
  16.7 1.0 %dynamic-slice_bitcast_fusion.2.back_ref = bf16[768,256]{1,0:T(8,128)(2,1)S(1)} fusion(bf16[8,768,256]{2,1,0:T(8,128)(2,1)} %constant.118.clone, s32[]{:T(128)S(6)} %select_n.68), kind=kLoop, calls=%fused_computation.2 | loop fusion | bytes 786436 | tf_op jit(solution)/shard_map/jit(dynamic_index_in_dim)/squeeze | solution.py:469
  17.8 0.7 broadcast_select_fusion.1
  18.6 2.6 %all-to-all-done = bf16[4,8,1280]{2,1,0:T(8,128)(2,1)S(1)} async-done(((bf16[4,8,1280]{2,1,0:T(8,128)(2,1)}), bf16[4,8,1280]{2,1,0:T(8,128)(2,1)S(1)}, u32[]{:S(2)}, u32[]{:S(2)}) %all-to-all-start) | async-done | bytes 81952 | tf_op jit(solution)/shard_map/all_to_all | solution.py:452
  21.2 1.2 %shard_map.110 = bf16[16,32,612]{2,1,0:T(8,128)(2,1)} custom-call(bf16[32,1280]{1,0:T(8,128)(2,1)S(1)} %bitcast.29, f32[32,4]{1,0:T(8,128)S(1)} %pad_convert_fusion.note_ref), custom_call_target="tpu_custom_call" | custom-call | tf_op jit(solution)/shard_map/pallas_call | solution.py:173
  22.4 0.7 collective-permute-start.1
  23.2 6.8 %all-to-all-start.1 = ((bf16[16,32,612]{2,1,0:T(8,128)(2,1)}), bf16[16,32,612]{2,1,0:T(8,128)(2,1)S(1)}, u32[]{:S(2)}, u32[]{:S(2)}) async-start(bf16[16,32,612]{2,1,0:T(8,128)(2,1)} %shard_map.110), calls=%async_computation.1 | async-start | bytes 1310720 | tf_op jit(solution)/shard_map/all_to_all | solution.py:458
  30.3 10.0 %all-to-all-done.1.own_ref = bf16[16,32,612]{2,1,0:T(8,128)(2,1)S(1)} async-done(((bf16[16,32,612]{2,1,0:T(8,128)(2,1)}), bf16[16,32,612]{2,1,0:T(8,128)(2,1)S(1)}, u32[]{:S(2)}, u32[]{:S(2)}) %all-to-all-start.1) | async-done | bytes 626720 | tf_op jit(solution)/shard_map/all_to_all | solution.py:458
  40.6 3.8 %collective-permute-start.2 = (bf16[16,32,612]{2,1,0:T(8,128)(2,1)S(1)}, bf16[16,32,612]{2,1,0:T(8,128)(2,1)S(1)}, u32[]{:S(2)}, u32[]{:S(2)}) collective-permute-start(bf16[16,32,612]{2,1,0:T(8,128)(2,1)S(1)} %all-to-all-done.1.own_ref), channel_id=1, source_target_pairs={{0,64},{64,0},{128,192},{192,128},{1,65},{65,1},{129,193},{193,129... | collective-permute-start | bytes 1880072 | tf_op jit(solution)/shard_map/ppermute | solution.py:461
  44.4 0.6 negate_convert_fusion
  45.0 1.1 %collective-permute-done.2.mate_ref = bf16[16,32,612]{2,1,0:T(8,128)(2,1)S(1)} collective-permute-done((bf16[16,32,612]{2,1,0:T(8,128)(2,1)S(1)}, bf16[16,32,612]{2,1,0:T(8,128)(2,1)S(1)}, u32[]{:S(2)}, u32[]{:S(2)}) %collective-permute-start.2) | collective-permute-done | bytes 626720 | tf_op jit(solution)/shard_map/ppermute | solution.py:461
  46.1 15.8 %shard_map.111 = bf16[8,48,256]{2,1,0:T(8,128)(2,1)} custom-call(s32[2,256]{1,0:T(2,128)S(1)} %fusion.8.shift_ref, s32[3]{0:T(128)S(1)} %pad_add_fusion.6.start_ref, bf16[16,32,612]{2,1,0:T(8,128)(2,1)S(1)} %all-to-all-done.1.own_ref, bf16[16,32,612]{2,1,0:T(8,128)(2,1)S(1)} %collective-permute-done.2.mate_ref, bf16[2,2,256,512]{3,2,1,0:T(8,128)(2,1)S(1)} %copy-done.1, ...), custom_call_target="tpu_custom_call" | custom-call | tf_op jit(solution)/shard_map/pallas_call | solution.py:347
  61.9 3.4 %all-to-all-start.2 = ((bf16[8,48,256]{2,1,0:T(8,128)(2,1)}), bf16[8,48,256]{2,1,0:T(8,128)(2,1)S(1)}, u32[]{:S(2)}, u32[]{:S(2)}) async-start(bf16[8,48,256]{2,1,0:T(8,128)(2,1)} %shard_map.111), calls=%async_computation.2 | async-start | bytes 393216 | tf_op jit(solution)/shard_map/all_to_all | solution.py:476
  65.4 2.1 %dynamic-slice_bitcast_fusion = (bf16[1536,512]{1,0:T(8,128)(2,1)S(1)}, bf16[1536,512]{1,0:T(8,128)(2,1)S(1)}) fusion(bf16[4,1536,512]{2,1,0:T(8,128)(2,1)} %constant.121.clone, s32[]{:T(128)S(6)} %select_n.71, bf16[4,1536,512]{2,1,0:T(8,128)(2,1)} %constant.120.clone), kind=kLoop, calls=%fused_computation | loop fusion | bytes 6291460 | tf_op jit(solution)/shard_map/jit(dynamic_index_in_dim)/squeeze | solution.py:480
  67.5 3.6 %all-to-all-done.2 = bf16[8,48,256]{2,1,0:T(8,128)(2,1)S(1)} async-done(((bf16[8,48,256]{2,1,0:T(8,128)(2,1)}), bf16[8,48,256]{2,1,0:T(8,128)(2,1)S(1)}, u32[]{:S(2)}, u32[]{:S(2)}) %all-to-all-start.2) | async-done | bytes 196640 | tf_op jit(solution)/shard_map/all_to_all | solution.py:476
  71.1 9.7 %all_gather.3 = bf16[32,48,256]{2,1,0:T(8,128)(2,1)S(1)} all-gather(bf16[8,48,256]{2,1,0:T(8,128)(2,1)S(1)} %all-to-all-done.2), channel_id=1, replica_groups=mesh['half'=4,'dev'=64] {'half'}, dimensions={0}, use_global_device_ids=true | all-gather | bytes 983040 | tf_op jit(solution)/shard_map/all_gather | solution.py:477
  80.7 1.7 %shard_map.112 = f32[256,256]{1,0:T(8,128)} custom-call(bf16[1536,256]{1,0:T(8,128)(2,1)S(1)} %bitcast.28, bf16[1536,512]{1,0:T(8,128)(2,1)S(1)} %get-tuple-element.38.high_ref, bf16[1536,512]{1,0:T(8,128)(2,1)S(1)} %get-tuple-element.37.low_ref), custom_call_target="tpu_custom_call" | custom-call | tf_op jit(solution)/shard_map/pallas_call | solution.py:390
  (29 shorter events, 1.1 us)
Async XLA Ops:
  0.0 30.1 %copy-start = (f32[16,2]{0,1:T(2,128)S(1)}, f32[16,2]{0,1:T(2,128)}, u32[]{:S(2)}) copy-start(f32[16,2]{0,1:T(2,128)} %param.14) | copy-start | bytes 388
  0.0 46.1 %copy-start.1 = (bf16[2,2,256,512]{3,2,1,0:T(8,128)(2,1)S(1)}, bf16[2,2,256,512]{3,2,1,0:T(8,128)(2,1)}, u32[]{:S(2)}) copy-start(bf16[2,2,256,512]{3,2,1,0:T(8,128)(2,1)} %constant.119.clone.table_ref) | copy-start | bytes 3145732
  0.1 1.3 %copy-start.2 = (bf16[2,1024,256]{2,1,0:T(8,128)(2,1)S(1)}, bf16[2,1024,256]{2,1,0:T(8,128)(2,1)}, u32[]{:S(2)}) copy-start(bf16[2,1024,256]{2,1,0:T(8,128)(2,1)} %constant.117.clone.table_ref) | copy-start | bytes 3145732
  1.4 0.8 copy-start.3
  2.1 0.7 copy-start.4
  5.2 16.0 %all-to-all-start = ((bf16[4,8,1280]{2,1,0:T(8,128)(2,1)}), bf16[4,8,1280]{2,1,0:T(8,128)(2,1)S(1)}, u32[]{:S(2)}, u32[]{:S(2)}) async-start(bf16[4,8,1280]{2,1,0:T(8,128)(2,1)} %shard_map.109), calls=%async_computation | async-start | bytes 163840 | tf_op jit(solution)/shard_map/all_to_all | solution.py:452
  14.9 2.9 %collective-permute-start = (s32[64,3]{0,1:T(4,128)S(1)}, s32[64,3]{0,1:T(4,128)S(1)}, u32[]{:S(2)}, u32[]{:S(2)}) collective-permute-start(s32[64,3]{0,1:T(4,128)S(1)} %pad_add_fusion.1), channel_id=1, source_target_pairs={{0,64},{64,0},{128,192},{192,128},{1,65},{65,1},{129,193},{193,129... | collective-permute-start | bytes 2312 | tf_op jit(solution)/shard_map/ppermute | solution.py:421
  22.4 7.6 %collective-permute-start.1 = (s32[128,3]{0,1:T(4,128)S(1)}, s32[128,3]{0,1:T(4,128)S(1)}, u32[]{:S(2)}, u32[]{:S(2)}) collective-permute-start(s32[128,3]{0,1:T(4,128)S(1)} %pad_add_fusion.2), channel_id=1, source_target_pairs={{0,128},{64,192},{128,0},{192,64},{1,129},{65,193},{129,1},{193,65... | collective-permute-start | bytes 4616 | tf_op jit(solution)/shard_map/ppermute | solution.py:421
  23.2 17.1 %all-to-all-start.1 = ((bf16[16,32,612]{2,1,0:T(8,128)(2,1)}), bf16[16,32,612]{2,1,0:T(8,128)(2,1)S(1)}, u32[]{:S(2)}, u32[]{:S(2)}) async-start(bf16[16,32,612]{2,1,0:T(8,128)(2,1)} %shard_map.110), calls=%async_computation.1 | async-start | bytes 1310720 | tf_op jit(solution)/shard_map/all_to_all | solution.py:458
  40.6 5.5 %collective-permute-start.2 = (bf16[16,32,612]{2,1,0:T(8,128)(2,1)S(1)}, bf16[16,32,612]{2,1,0:T(8,128)(2,1)S(1)}, u32[]{:S(2)}, u32[]{:S(2)}) collective-permute-start(bf16[16,32,612]{2,1,0:T(8,128)(2,1)S(1)} %all-to-all-done.1.own_ref), channel_id=1, source_target_pairs={{0,64},{64,0},{128,192},{192,128},{1,65},{65,1},{129,193},{193,129... | collective-permute-start | bytes 1880072 | tf_op jit(solution)/shard_map/ppermute | solution.py:461
  61.9 9.1 %all-to-all-start.2 = ((bf16[8,48,256]{2,1,0:T(8,128)(2,1)}), bf16[8,48,256]{2,1,0:T(8,128)(2,1)S(1)}, u32[]{:S(2)}, u32[]{:S(2)}) async-start(bf16[8,48,256]{2,1,0:T(8,128)(2,1)} %shard_map.111), calls=%async_computation.2 | async-start | bytes 393216 | tf_op jit(solution)/shard_map/all_to_all | solution.py:476

commit v4 on v3

--- a/solution.py
+++ b/solution.py
@@ -22,6 +22,7 @@
 TILE = 16
 WIDE = 24
 PARTS = GROUP * HALVES
+PART_ROWS = GROUP * 2 * WIDE
 ROWS_IN = 2 * WIDE + 2 * REACH
 CHIP_COLS = GROUP * 2 * WIDE + 2 * REACH
 NOTE = 4
@@ -29,10 +30,12 @@
 KU = 768
 BATCH = 16
 BLOCK = 2 * BATCH * WIDE
-
-
-def spread_of(count):
-    return 2.0 ** np.mod(np.arange(count) * 0.6180339887498949, 1.0)
+STEP = 2 * WIDE + 1
+
+
+def spread_of(row, xnp=np):
+    turn = row * 0.6180339887498949
+    return xnp.exp2(turn - xnp.floor(turn))
 
 
 def angles(product):
@@ -60,7 +63,7 @@
     rows = ((depth * 16 + source) * TILE + inner).reshape(4, GRID // 4)
     angle = angles(rows[:, :, None] * (np.arange(GRID // 4) - BAND - REACH)[None, None, :])
     table = np.stack([np.cos(angle), np.sin(angle)], 2)
-    table = table / spread_of(TILE)[rows % TILE][:, :, None, None]
+    table = table / spread_of(rows % TILE)[:, :, None, None]
     table = table.reshape(2, 2, GRID // 4, 2, 2, 128).transpose(0, 1, 2, 4, 3, 5)
     return table.reshape(2, 2, GRID // 4, 512).astype(np.float32).astype(ml_dtypes.bfloat16)
 
@@ -83,17 +86,16 @@
     chip, core, member = np.meshgrid(np.arange(2), np.arange(2), np.arange(GROUP), indexing="ij")
     part = (chip * 2 * GROUP + member * 2 + core).reshape(-1)
     index = (part[:, None] * WIDE + np.arange(WIDE)[None, :]).reshape(-1) - BAND
-    cols = np.arange(GRID)
+    cols = np.arange(GRID // HALVES)
     angle = angles(index[:, None] * cols[None, :])
     angle = angle - (propagation_rate / GRID) * (index * index).astype(np.float64)[:, None]
     scale = 1.0 / (GRID * GRID)
-    cosine = (np.cos(angle) * scale).reshape(PARTS, WIDE, HALVES, GRID // HALVES)
-    sine = (np.sin(angle) * scale).reshape(PARTS, WIDE, HALVES, GRID // HALVES)
+    cosine = (np.cos(angle) * scale).reshape(PARTS, WIDE, -1)
+    sine = (np.sin(angle) * scale).reshape(PARTS, WIDE, -1)
     table = np.concatenate(
-        [np.concatenate([cosine, sine], 3), np.concatenate([-sine, cosine], 3)], 1
-    )
-    table = table.reshape(PARTS * 2 * WIDE, HALVES, 2 * GRID // HALVES).transpose(1, 0, 2)
-    return two_parts(table)
+        [np.concatenate([cosine, sine], 2), np.concatenate([-sine, cosine], 2)], 1
+    )
+    return two_parts(table.reshape(HALVES, PART_ROWS, 2 * GRID // HALVES))
 
 
 def chosen(rows, cols, source):
@@ -102,25 +104,39 @@
     return jnp.where(col == source(row), 1.0, 0.0).astype(jnp.bfloat16)
 
 
-def column_kernel(place_ref, field_ref, spread_ref, table_ref, out_ref, table, arrived):
-    copy = pltpu.make_async_copy(table_ref, table, arrived)
-    copy.start()
-    first, core = place_ref[0], place_ref[1]
-    rows = field_ref.shape[0] // 2
+def column_kernel(field_ref, table_ref, out_ref, field_in, table, arrived):
+    copies = [
+        pltpu.make_async_copy(field_ref, field_in, arrived.at[0]),
+        pltpu.make_async_copy(table_ref, table, arrived.at[1]),
+    ]
+    for copy in copies:
+        copy.start()
+    half = lax.axis_index("half")
+    chip, core = half // 2, half % 2
+    first = chip * (2 * GROUP * WIDE) - BAND - REACH
+    rows = field_in.shape[0] // 2
     pick = chosen(rows, 2 * rows, lambda row: 4 * (row % 4) + 2 * (row // 4) + core)
-    field = jnp.dot(pick, field_ref[...], preferred_element_type=jnp.float32)
-    spread = spread_ref[core][:, :1]
+    row = lax.broadcasted_iota(jnp.int32, (rows, 128), 0)
+    spread = spread_of(4 * (row % 4) + 2 * (row // 4) + core, jnp)[:, :1]
+    copies[0].wait()
+    field = jnp.dot(pick, field_in[...], preferred_element_type=jnp.float32)
     column = lax.broadcasted_iota(jnp.int32, (rows, GRID), 1)
-    waves = []
-    for chunk in range(CHIP_COLS // 128):
-        turn = jnp.bitwise_and((first + 128 * chunk) * column, GRID - 1)
-        phase = field - (two_pi / GRID) * turn.astype(jnp.float32)
-        waves += [jnp.cos(phase) * spread, jnp.sin(phase) * spread]
+    turn = jnp.bitwise_and(first * column, GRID - 1)
+    phase = field - (two_pi / GRID) * turn.astype(jnp.float32)
+    cosine, sine = jnp.cos(phase) * spread, jnp.sin(phase) * spread
+    waves = [cosine, sine]
+    column = column[:, :128]
+    for chunk in range(1, CHIP_COLS // 128):
+        eighth = jnp.bitwise_and(chunk * column, 7).astype(jnp.float32) * (two_pi / 8)
+        turn_re, turn_im = (
+            jnp.concatenate([x] * (GRID // 128), 1) for x in (jnp.cos(eighth), jnp.sin(eighth))
+        )
+        waves += [cosine * turn_re + sine * turn_im, sine * turn_re - cosine * turn_im]
     wave = jnp.concatenate(waves, 0)
     high = wave.astype(jnp.bfloat16)
     low = (wave - high.astype(jnp.float32)).astype(jnp.bfloat16)
     count = wave.shape[0]
-    copy.wait()
+    copies[1].wait()
     both = jnp.dot(jnp.concatenate([high, low], 0), table[0], preferred_element_type=jnp.float32)
     mixed = both[:count] + both[count:]
     mixed = mixed + jnp.dot(high, table[1], preferred_element_type=jnp.float32)
@@ -135,28 +151,32 @@
         out_ref[copy] = piece
 
 
-def column_piece(place, potential):
+def column_piece(potential):
     vmem = pl.BlockSpec(memory_space=pltpu.VMEM)
-    smem = pl.BlockSpec(memory_space=pltpu.SMEM)
     table = column_table()
     rows = potential.shape[0]
-    spread = spread_of(TILE).reshape(4, 2, 2).transpose(2, 1, 0).reshape(2, TILE // 2, 1)
-    spread = np.broadcast_to(spread, (2, TILE // 2, 128)).astype(np.float32)
+    anywhere = pl.BlockSpec(memory_space=pltpu.HBM)
     return pl.pallas_call(
         column_kernel,
         out_shape=jax.ShapeDtypeStruct((4, rows // 2, 2 * CHIP_COLS), jnp.bfloat16),
-        in_specs=[smem, vmem, vmem, pl.BlockSpec(memory_space=pl.ANY)],
+        in_specs=[anywhere, anywhere],
         out_specs=vmem,
-        scratch_shapes=[pltpu.VMEM(table.shape, jnp.bfloat16), pltpu.SemaphoreType.DMA],
-        compiler_params=pltpu.CompilerParams(vmem_limit_bytes=16 * 1024 * 1024),
-    )(place, potential, jnp.asarray(spread), jnp.asarray(table))
-
-
-def window_kernel(piece_ref, note_ref, out_ref):
+        scratch_shapes=[
+            pltpu.VMEM(potential.shape, jnp.bfloat16),
+            pltpu.VMEM(table.shape, jnp.bfloat16),
+            pltpu.SemaphoreType.DMA((2,)),
+        ],
+        compiler_params=pltpu.CompilerParams(vmem_limit_bytes=56 * 1024 * 1024),
+    )(potential, jnp.asarray(table))
+
+
+def window_kernel(piece_ref, spot_ref, out_ref):
     rows = piece_ref.shape[0]
     pick = chosen(rows, rows, lambda row: 8 * ((row // 4) % 4) + 4 * (row // 16) + row % 4)
     piece = jnp.dot(pick, piece_ref[...], preferred_element_type=jnp.float32)
-    note = note_ref[...]
+    spots = spot_ref[...]
+    note = jnp.concatenate([spots >> 7, jnp.bitwise_and(spots, 127)], 1).astype(jnp.float32)
+    note = jnp.concatenate([note, jnp.zeros_like(note)], 0)
     for member in range(GROUP):
         at = 2 * WIDE * member
         window = jnp.concatenate(
@@ -168,7 +188,7 @@
             out_ref[member + copy * GROUP] = window
 
 
-def windows_of(piece, note):
+def windows_of(piece, spots):
     vmem = pl.BlockSpec(memory_space=pltpu.VMEM)
     return pl.pallas_call(
         window_kernel,
@@ -176,7 +196,7 @@
         in_specs=[vmem, vmem],
         out_specs=vmem,
         compiler_params=pltpu.CompilerParams(vmem_limit_bytes=16 * 1024 * 1024),
-    )(piece, note)
+    )(piece, spots)
 
 
 def field_kernel(
@@ -184,12 +204,11 @@
     start_ref,
     own_ref,
     mate_ref,
-    table_ref,
+    own_table,
+    mate_table,
     back_ref,
     coef_ref,
     out_ref,
-    table,
-    arrived,
     turned_ref,
     spec_re,
     spec_im,
@@ -201,30 +220,32 @@
     sums_re,
     sums_im,
 ):
-    copy = pltpu.make_async_copy(table_ref, table, arrived)
-    copy.start()
-    core = start_ref[1]
+    first_core = start_ref[1] == 0
     for pair in range(2):
-        for place, ref in ((core, own_ref), (1 - core, mate_ref)):
+        for place, ref in enumerate((own_ref, mate_ref)):
             block = ref[:, 16 * pair : 16 * pair + 16, :]
             block = block.reshape(GRID // 4, LANES)[:, : 2 * ROWS_IN]
-            turned_ref[2 * pair + place] = block.T
-    copy.wait()
+            turned_ref[2 * place + pair] = block.T
     for part in range(2):
         lanes = slice(256 * part, 256 * (part + 1))
         each = []
-        for remainder in range(4):
-            both = jnp.dot(
-                turned_ref[remainder],
-                table[remainder % 2, remainder // 2, :, lanes],
-                preferred_element_type=jnp.float32,
-            )
-            each.append(
-                (
-                    both[:ROWS_IN, :128] + both[ROWS_IN:, 128:],
-                    both[ROWS_IN:, :128] - both[:ROWS_IN, 128:],
+        for place, ref in enumerate((own_table, mate_table)):
+            for pair in range(2):
+                both = jnp.dot(
+                    turned_ref[2 * place + pair],
+                    ref[pair, :, lanes],
+                    preferred_element_type=jnp.float32,
                 )
-            )
+                each.append(
+                    (
+                        both[:ROWS_IN, :128] + both[ROWS_IN:, 128:],
+                        both[ROWS_IN:, :128] - both[:ROWS_IN, 128:],
+                    )
+                )
+        each = [
+            tuple(jnp.where(first_core, x, y) for x, y in zip(each[one], each[two]))
+            for one, two in ((0, 2), (2, 0), (1, 3), (3, 1))
+        ]
         (re0, im0), (re1, im1), (re2, im2), (re3, im3) = each
         even, even_less = (re0 + re2, im0 + im2), (re0 - re2, im0 - im2)
         odd, odd_less = (re1 + re3, im1 + im3), (im1 - im3, re3 - re1)
@@ -289,10 +310,12 @@
             shifted(step * BATCH + spot, rows, spot * 2 * WIDE)
 
     def multiply(step, rows):
-        at = pl.multiple_of(step * BLOCK, BLOCK)
         result = jnp.dot(rows[...], back_ref[...], preferred_element_type=jnp.float32)
-        field_re[pl.ds(at, BLOCK), :] = result[:, :128]
-        field_im[pl.ds(at, BLOCK), :] = result[:, 128:]
+        for spot in range(BATCH):
+            at = step * BATCH * STEP + spot * STEP
+            piece = result[spot * 2 * WIDE : (spot + 1) * 2 * WIDE]
+            field_re[pl.ds(at, 2 * WIDE), :] = piece[:, :128]
+            field_im[pl.ds(at, 2 * WIDE), :] = piece[:, 128:]
 
     steps = TILTS // BATCH
     fill(0, rows_a)
@@ -311,7 +334,7 @@
         values = jnp.concatenate(
             [
                 jnp.concatenate(
-                    [ref[pl.ds(col + WIDE * part, TILTS, stride=2 * WIDE), :] for part in range(2)], 0
+                    [ref[pl.ds(col + WIDE * part, TILTS, stride=STEP), :] for part in range(2)], 0
                 ).astype(jnp.bfloat16)
                 for ref in (field_re, field_im)
             ],
@@ -336,64 +359,75 @@
                     total = jnp.where(block_of == spot, turned, total)
                 parts.append(total)
             parts = [parts[0] * peak_re - parts[1] * peak_im, parts[0] * peak_im + parts[1] * peak_re]
-            out_ref[tile, :, half * 128 : (half + 1) * 128] = jnp.concatenate(parts, 0).astype(
-                out_ref.dtype
-            )
-
-
-def field_sums(shifts, start, own, mate, table, back, coef):
+            parts = jnp.concatenate(parts, 0).astype(out_ref.dtype)
+            for copy in range(2):
+                out_ref[tile + copy * GROUP, :, half * 128 : (half + 1) * 128] = parts
+
+
+def field_sums(shifts, start, own, mate, own_table, mate_table, back, coef):
     vmem = pl.BlockSpec(memory_space=pltpu.VMEM)
     smem = pl.BlockSpec(memory_space=pltpu.SMEM)
     return pl.pallas_call(
         field_kernel,
-        out_shape=jax.ShapeDtypeStruct((GROUP, 2 * WIDE, TILE * TILE), jnp.bfloat16),
-        in_specs=[smem, smem, vmem, vmem, pl.BlockSpec(memory_space=pl.ANY), vmem, vmem],
+        out_shape=jax.ShapeDtypeStruct((2 * GROUP, 2 * WIDE, TILE * TILE), jnp.bfloat16),
+        in_specs=[smem, smem] + [vmem] * 6,
         out_specs=vmem,
         scratch_shapes=[
-            pltpu.VMEM((2, 2, GRID // 4, 512), jnp.bfloat16),
-            pltpu.SemaphoreType.DMA,
             pltpu.VMEM((4, 2 * ROWS_IN, GRID // 4), jnp.bfloat16),
             pltpu.VMEM((GRID // 128, ROWS_IN, 128), jnp.float32),
             pltpu.VMEM((GRID // 128, ROWS_IN, 128), jnp.float32),
             pltpu.VMEM((2 * WIDE, KU), jnp.bfloat16),
             pltpu.VMEM((BLOCK, KU), jnp.bfloat16),
             pltpu.VMEM((BLOCK, KU), jnp.bfloat16),
-            pltpu.VMEM((TILTS * 2 * WIDE, 128), jnp.float32),
-            pltpu.VMEM((TILTS * 2 * WIDE, 128), jnp.float32),
+            pltpu.VMEM((TILTS * STEP, 128), jnp.float32),
+            pltpu.VMEM((TILTS * STEP, 128), jnp.float32),
             pltpu.VMEM((GROUP * TILE * WIDE, 128), jnp.float32),
             pltpu.VMEM((GROUP * TILE * WIDE, 128), jnp.float32),
         ],
-        compiler_params=pltpu.CompilerParams(vmem_limit_bytes=48 * 1024 * 1024),
+        compiler_params=pltpu.CompilerParams(vmem_limit_bytes=30 * 1024 * 1024),
     )(
         shifts,
         start,
         own,
         mate,
-        table,
+        own_table,
+        mate_table,
         back,
         coef,
     )
 
 
-def probe_kernel(sums_ref, high_ref, low_ref, out_ref):
-    sums = sums_ref[...].T
-    probe = jnp.dot(sums, high_ref[...], preferred_element_type=jnp.float32) + jnp.dot(
-        sums, low_ref[...], preferred_element_type=jnp.float32
-    )
+def probe_kernel(half_ref, own_ref, mate_ref, high_ref, low_ref, out_ref):
+    half = half_ref[0]
+    index = lax.broadcasted_iota(jnp.int32, (1, WIDE, TILE * TILE), 1) + (3 * BAND)
+    turns = jnp.bitwise_and(index * half, 3)
+    cosine = jnp.where(turns == 0, 1.0, jnp.where(turns == 2, -1.0, 0.0))
+    sine = jnp.where(turns == 1, 1.0, jnp.where(turns == 3, -1.0, 0.0))
+    probe = 0.0
+    for ref, core in ((own_ref, half % 2), (mate_ref, 1 - half % 2)):
+        for chip in range(2):
+            sums = ref[chip].astype(jnp.float32)
+            real, imag = sums[:, :WIDE], sums[:, WIDE:]
+            sums = jnp.concatenate([real * cosine - imag * sine, real * sine + imag * cosine], 1)
+            sums = sums.reshape(PART_ROWS, TILE * TILE).T.astype(jnp.bfloat16)
+            part = 2 * chip + core
+            probe = probe + jnp.dot(sums, high_ref[part], preferred_element_type=jnp.float32)
+            probe = probe + jnp.dot(sums, low_ref[part], preferred_element_type=jnp.float32)
     share = out_ref.shape[1]
     real, imag = probe[:, :share], probe[:, share:]
     out_ref[...] = real * real + imag * imag
 
 
-def probe_intensity(sums, high, low):
+def probe_all(half, own, mate, high, low):
     vmem = pl.BlockSpec(memory_space=pltpu.VMEM)
+    smem = pl.BlockSpec(memory_space=pltpu.SMEM)
     return pl.pallas_call(
         probe_kernel,
-        out_shape=jax.ShapeDtypeStruct((sums.shape[1], high.shape[1] // 2), jnp.float32),
-        in_specs=[vmem] * 3,
+        out_shape=jax.ShapeDtypeStruct((TILE * TILE, GRID // HALVES), jnp.float32),
+        in_specs=[smem] + [vmem] * 4,
         out_specs=vmem,
-        compiler_params=pltpu.CompilerParams(vmem_limit_bytes=32 * 1024 * 1024),
-    )(sums, high, low)
+        compiler_params=pltpu.CompilerParams(vmem_limit_bytes=24 * 1024 * 1024),
+    )(half, own, mate, high, low)
 
 
 def mixing_table(tilt_list, beam_list, beam_table, positions):
@@ -435,26 +469,26 @@
     return flat.reshape(8, 8).tolist()
 
 
+def joint_groups():
+    flat = np.arange(256).reshape(2, 2, 8, 8)
+    return flat.transpose(2, 1, 0, 3).reshape(16, 16).tolist()
+
+
 def local(potential, tilt_ids, beam_index, beam_table, positions):
     half = lax.axis_index("half")
     dev = lax.axis_index("dev")
     chip, core = half // 2, half % 2
     rows = potential.shape[0]
 
-    first_col = chip * (2 * GROUP * WIDE) - BAND - REACH
-    piece = column_piece(jnp.stack([first_col, core]).astype(jnp.int32), potential)
-    piece, tilt_ids, beam_index, positions, dev = lax.optimization_barrier(
-        (piece, tilt_ids, beam_index, positions, dev)
+    piece = column_piece(potential)
+    piece = lax.all_to_all(piece, "dev", 0, 0, tiled=True, axis_index_groups=groups("depth"))
+    windows = windows_of(piece.reshape(2 * rows, 2 * CHIP_COLS), positions)
+    windows, tilt_ids, beam_index, dev, core_late = lax.optimization_barrier(
+        (windows, tilt_ids, beam_index, dev, core)
     )
     group, member = dev // GROUP, dev % GROUP
     info = jnp.concatenate([tilt_ids, beam_index[:, None]], 1)
-    info = doubled(info, "half", half, (1,), HALVES)
-    piece = lax.all_to_all(piece, "dev", 0, 0, tiled=True, axis_index_groups=groups("depth"))
-    piece = piece.reshape(2 * rows, 2 * CHIP_COLS)
-    note = jnp.concatenate([positions >> 7, jnp.bitwise_and(positions, 127)], 1)
-    note = jnp.concatenate([note, jnp.zeros_like(note)], 0).astype(jnp.float32)
-    windows, info = lax.optimization_barrier((windows_of(piece, note), info))
-    tilt_info = doubled(info, "half", half, (2,), HALVES)
+    tilt_info = doubled(info, "half", half, (1, 2), HALVES)
     columns = lax.all_to_all(
         windows, "dev", 0, 0, tiled=True, axis_index_groups=groups("plane")
     )
@@ -466,21 +500,28 @@
     spots = notes[:, :2] * 128 + notes[:, 2:]
     coef = mixing_table(tilt_info[:, :2], tilt_info[:, 2], beam_table, spots)
 
+    row_tables = [
+        lax.dynamic_index_in_dim(jnp.asarray(row_table()), place, 0, keepdims=False)
+        for place in (core_late, 1 - core_late)
+    ]
     back = lax.dynamic_index_in_dim(jnp.asarray(back_row_table()), group, 0, keepdims=False)
     shifts = (REACH - tilt_info[:, :2]).T + jnp.stack([jnp.int32(0), WIDE * core])[:, None]
     first = WIDE * (chip * 2 * GROUP + member * 2 + core) - BAND
     zero_row = BAND + REACH - 2 * WIDE * (chip * GROUP + member)
     start = jnp.stack([first, core, zero_row]).astype(jnp.int32)
-    sums = field_sums(shifts, start, columns, mate, jnp.asarray(row_table()), back, coef)
-
-    sums = lax.all_to_all(sums, "dev", 0, 0, tiled=True, axis_index_groups=groups("tiles"))
-    sums = lax.all_gather(sums, "half", axis=0, tiled=True).reshape(PARTS * 2 * WIDE, TILE * TILE)
-
-    high, low = (
-        lax.dynamic_index_in_dim(jnp.asarray(t), half, 0, keepdims=False)
-        for t in back_column_table()
-    )
-    return probe_intensity(sums, high, low).reshape(TILE, TILE, GRID // HALVES)
+    sums = field_sums(shifts, start, columns, mate, *row_tables, back, coef)
+
+    sums = lax.all_to_all(
+        sums,
+        ("half", "dev"), 0, 0, tiled=True, axis_index_groups=joint_groups(),
+    )
+    mates = lax.ppermute(sums, "half", [(i, i ^ 1) for i in range(HALVES)])
+    sums, mates = (x.reshape(2, GROUP, 2 * WIDE, TILE * TILE) for x in (sums, mates))
+
+    high, low = (jnp.asarray(t) for t in back_column_table())
+    place = half.reshape(1)
+    probe = probe_all(place, sums, mates, high, low)
+    return probe.reshape(TILE, TILE, GRID // HALVES)
 
 
 def solution(mesh):

time: 83.1 us -> 72.9 us (0.88)
  waiting for transfers between devices: 17.3 us -> 12.9 us
  Pallas kernels: 21.1 us -> 18 us
  local copies, waits for them, and re-layouts: 6.28 us -> 4.06 us
  other arithmetic: 3.15 us -> 1.05 us
  blocking collectives: 9.67 us -> 11.7 us
    all_to_all x0 -> x1, blocking collectives: none -> 11.7 us  [local(): lax.all_to_all(sums, ('half', 'dev'), 0, 0, tiled=True, axis_index_groups...]
    all_gather x1 -> x0, blocking collectives: 9.67 us -> none  [local(): lax.all_gather(sums, 'half', axis=0, tiled=True)]
    all_to_all x1, waiting for transfers between devices: 10 us -> 2.4 us  [local(): lax.all_to_all(windows, 'dev', 0, 0, tiled=True, axis_index_groups=groups...]
    all_to_all x1 -> x0, waiting for transfers between devices: 3.62 us -> none  [local(): lax.all_to_all(sums, 'dev', 0, 0, tiled=True, axis_index_groups=groups('t...]
    all_to_all x1, waiting for transfers between devices: 2.61 us -> 6.15 us  [local(): lax.all_to_all(piece, 'dev', 0, 0, tiled=True, axis_index_groups=groups('...]
    all_to_all x1 -> x0, starting transfers between devices: 3.4 us -> none  [local(): lax.all_to_all(sums, 'dev', 0, 0, tiled=True, axis_index_groups=groups('t...]
    pallas_call x2, Pallas kernels: 17.5 us -> 14.5 us  [the longest x1 12.5 us: field_sums(): pl.pallas_call(field_kernel, out_shape=jax.ShapeDtypeStruct((2 * GROUP, 2...]
    squeeze x1, local copies, waits for them, and re-layouts: 2.09 us -> 0.07 us  [local(): lax.dynamic_index_in_dim(jnp.asarray(row_table()), place, 0, keepdims=False)]
  transfers between devices with their start and end apart: 6 -> 6, of which waited for: 4 -> 5; matrix products, arithmetic and copies ran while one was open for 8% -> 5% of each run, Pallas kernels for 0% -> 0%
where the time goes in v4:
time: 72.9 us; the launch traced here: 72.5 us
  starting transfers between devices  24.5 us (34%)
  Pallas kernels  18 us (25%)
  waiting for transfers between devices  12.9 us (18%)
  blocking collectives  11.7 us (16%)
  local copies, waits for them, and re-layouts  4.06 us (6%)
  other arithmetic  1.05 us (1%)
    pallas_call x1, Pallas kernels, field_sums(): pl.pallas_call(field_kernel, out_shape=jax.ShapeDtypeStruct((2 * GROUP, 2...  12.5 us
    all_to_all x1, blocking collectives, local(): lax.all_to_all(sums, ('half', 'dev'), 0, 0, tiled=True, axis_index_groups...  11.7 us
    all_to_all x1, starting transfers between devices, local(): lax.all_to_all(piece, 'dev', 0, 0, tiled=True, axis_index_groups=groups('...  9.02 us
    all_to_all x1, starting transfers between devices, local(): lax.all_to_all(windows, 'dev', 0, 0, tiled=True, axis_index_groups=groups...  6.75 us
    all_to_all x1, waiting for transfers between devices, local(): lax.all_to_all(piece, 'dev', 0, 0, tiled=True, axis_index_groups=groups('...  6.15 us
    ppermute x1, starting transfers between devices, local(): mate = lax.ppermute(columns, 'half', [(i, i ^ 1) for i in range(HALVES)])  3.61 us
    ppermute x2, starting transfers between devices, doubled(): other = lax.ppermute(block, axis, [(i, i ^ stride) for i in range(size)])  3.45 us
    all_to_all x1, waiting for transfers between devices, local(): lax.all_to_all(windows, 'dev', 0, 0, tiled=True, axis_index_groups=groups...  2.4 us
  transfers between devices with their start and end apart: 6, of which 5 were waited for; matrix products, arithmetic and copies ran while one was open for 5% of the time, Pallas kernels for 0%

profile of v4, /device:TPU:1, one launch (start us, length us, event | category | flops | bytes accessed | tf_op | source)
XLA Modules:
  0.0 72.5 jit_solution(15786517169241919439)
XLA Ops:
  0.0 2.3 %shard_map.100 = bf16[4,8,1280]{2,1,0:T(8,128)(2,1)} custom-call(bf16[16,1024]{1,0:T(8,128)(2,1)} %field_ref.1, bf16[2,1024,256]{2,1,0:T(8,128)(2,1)} %constant.103.clone.table_ref), custom_call_target="tpu_custom_call" | custom-call | tf_op jit(solution)/shard_map/pallas_call | solution.py:159
  2.3 9.0 %all-to-all-start = ((bf16[4,8,1280]{2,1,0:T(8,128)(2,1)}), bf16[4,8,1280]{2,1,0:T(8,128)(2,1)S(1)}, u32[]{:S(2)}, u32[]{:S(2)}) async-start(bf16[4,8,1280]{2,1,0:T(8,128)(2,1)} %shard_map.100), calls=%async_computation | async-start | bytes 163840 | tf_op jit(solution)/shard_map/all_to_all | solution.py:484
  11.4 0.8 %copy.12.spot_ref = s32[16,2]{1,0:T(8,128)S(1)} copy(s32[16,2]{0,1:T(2,128)} %param.14) | data formatting | bytes 256 | tf_op args[4]
  12.2 6.1 %all-to-all-done = bf16[4,8,1280]{2,1,0:T(8,128)(2,1)S(1)} async-done(((bf16[4,8,1280]{2,1,0:T(8,128)(2,1)}), bf16[4,8,1280]{2,1,0:T(8,128)(2,1)S(1)}, u32[]{:S(2)}, u32[]{:S(2)}) %all-to-all-start) | async-done | bytes 81952 | tf_op jit(solution)/shard_map/all_to_all | solution.py:484
  18.3 1.2 %shard_map.101 = bf16[16,32,612]{2,1,0:T(8,128)(2,1)} custom-call(bf16[32,1280]{1,0:T(8,128)(2,1)S(1)} %bitcast.31, s32[16,2]{1,0:T(8,128)S(1)} %copy.12.spot_ref), custom_call_target="tpu_custom_call" | custom-call | tf_op jit(solution)/shard_map/pallas_call | solution.py:193
  19.5 6.8 %all-to-all-start.1 = ((bf16[16,32,612]{2,1,0:T(8,128)(2,1)}), bf16[16,32,612]{2,1,0:T(8,128)(2,1)S(1)}, u32[]{:S(2)}, u32[]{:S(2)}) async-start(bf16[16,32,612]{2,1,0:T(8,128)(2,1)} %shard_map.101), calls=%async_computation.1 | async-start | bytes 1310720 | tf_op jit(solution)/shard_map/all_to_all | solution.py:492
  26.3 2.7 %collective-permute-start = (s32[64,3]{0,1:T(4,128)S(1)}, s32[64,3]{0,1:T(4,128)S(1)}, u32[]{:S(2)}, u32[]{:S(2)}) collective-permute-start(s32[64,3]{0,1:T(4,128)S(1)} %pad_add_fusion), channel_id=1, source_target_pairs={{0,64},{64,0},{128,192},{192,128},{1,65},{65,1},{129,193},{193,129... | collective-permute-start | bytes 2312 | tf_op jit(solution)/shard_map/ppermute | solution.py:455
  29.1 1.9 %dynamic-slice_bitcast_fusion.2.back_ref = bf16[768,256]{1,0:T(8,128)(2,1)} fusion(bf16[8,768,256]{2,1,0:T(8,128)(2,1)} %constant.105.clone, s32[]{:T(128)S(6)} %select_n.72), kind=kLoop, calls=%fused_computation.2 | loop fusion | bytes 786436 | tf_op jit(solution)/shard_map/jit(dynamic_index_in_dim)/squeeze | solution.py:507
  31.1 0.8 %collective-permute-start.1 = (s32[128,3]{0,1:T(4,128)S(1)}, s32[128,3]{0,1:T(4,128)S(1)}, u32[]{:S(2)}, u32[]{:S(2)}) collective-permute-start(s32[128,3]{0,1:T(4,128)S(1)} %pad_add_fusion.1), channel_id=1, source_target_pairs={{0,128},{64,192},{128,0},{192,64},{1,129},{65,193},{129,1},{193,65... | collective-permute-start | bytes 4616 | tf_op jit(solution)/shard_map/ppermute | solution.py:455
  31.9 1.9 %collective-permute-done.1 = s32[128,3]{0,1:T(4,128)S(1)} collective-permute-done((s32[128,3]{0,1:T(4,128)S(1)}, s32[128,3]{0,1:T(4,128)S(1)}, u32[]{:S(2)}, u32[]{:S(2)}) %collective-permute-start.1) | collective-permute-done | bytes 1568 | tf_op jit(solution)/shard_map/ppermute | solution.py:455
  34.0 0.2 fusion.2
  34.2 2.4 %all-to-all-done.1.own_ref = bf16[16,32,612]{2,1,0:T(8,128)(2,1)S(1)} async-done(((bf16[16,32,612]{2,1,0:T(8,128)(2,1)}), bf16[16,32,612]{2,1,0:T(8,128)(2,1)S(1)}, u32[]{:S(2)}, u32[]{:S(2)}) %all-to-all-start.1) | async-done | bytes 626720 | tf_op jit(solution)/shard_map/all_to_all | solution.py:492
  36.6 0.1 slice.54
  36.7 0.1 fusion.11
  36.8 0.1 copy.16
  36.9 3.6 %collective-permute-start.2 = (bf16[16,32,612]{2,1,0:T(8,128)(2,1)S(1)}, bf16[16,32,612]{2,1,0:T(8,128)(2,1)S(1)}, u32[]{:S(2)}, u32[]{:S(2)}) collective-permute-start(bf16[16,32,612]{2,1,0:T(8,128)(2,1)S(1)} %all-to-all-done.1.own_ref), channel_id=1, source_target_pairs={{0,64},{64,0},{128,192},{192,128},{1,65},{65,1},{129,193},{193,129... | collective-permute-start | bytes 1880072 | tf_op jit(solution)/shard_map/ppermute | solution.py:495
  40.5 0.6 negate_convert_fusion
  41.2 1.1 %collective-permute-done.2.mate_ref = bf16[16,32,612]{2,1,0:T(8,128)(2,1)S(1)} collective-permute-done((bf16[16,32,612]{2,1,0:T(8,128)(2,1)S(1)}, bf16[16,32,612]{2,1,0:T(8,128)(2,1)S(1)}, u32[]{:S(2)}, u32[]{:S(2)}) %collective-permute-start.2) | collective-permute-done | bytes 626720 | tf_op jit(solution)/shard_map/ppermute | solution.py:495
  42.3 1.0 %copy-done.3 = bf16[768,256]{1,0:T(8,128)(2,1)S(1)} copy-done((bf16[768,256]{1,0:T(8,128)(2,1)S(1)}, bf16[768,256]{1,0:T(8,128)(2,1)}, u32[]{:S(2)}) %copy-start.3) | copy-done | bytes 393240
  43.3 12.5 %shard_map.102 = bf16[16,48,256]{2,1,0:T(8,128)(2,1)S(1)} custom-call(s32[2,256]{1,0:T(2,128)S(1)} %fusion.8.shift_ref, s32[3]{0:T(128)S(1)} %pad_add_fusion.4.start_ref, bf16[16,32,612]{2,1,0:T(8,128)(2,1)S(1)} %all-to-all-done.1.own_ref, bf16[16,32,612]{2,1,0:T(8,128)(2,1)S(1)} %collective-permute-done.2.mate_ref, ...), custom_call_target="tpu_custom_call" | custom-call | tf_op jit(solution)/shard_map/pallas_call | solution.py:370
  55.8 11.7 %all_to_all.15 = bf16[16,48,256]{2,1,0:T(8,128)(2,1)S(1)} all-to-all(bf16[16,48,256]{2,1,0:T(8,128)(2,1)S(1)} %shard_map.102), channel_id=1, replica_groups={{0,1,2,3,4,5,6,7,128,129,130,131,132,133,134,135},{64,65,66,67,68,69,70..., dimensions={0} | all-to-all | bytes 786432 | tf_op jit(solution)/shard_map/all_to_all | solution.py:514
  67.4 1.6 %collective-permute-start.3 = (bf16[16,48,256]{2,1,0:T(8,128)(2,1)S(1)}, bf16[16,48,256]{2,1,0:T(8,128)(2,1)S(1)}, u32[]{:S(2)}, u32[]{:S(2)}) collective-permute-start(bf16[16,48,256]{2,1,0:T(8,128)(2,1)S(1)} %all_to_all.15), channel_id=1, source_target_pairs={{0,64},{64,0},{128,192},{192,128},{1,65},{65,1},{129,193},{193,129... | collective-permute-start | bytes 1179656 | tf_op jit(solution)/shard_map/ppermute | solution.py:518
  69.1 1.3 %collective-permute-done.3 = bf16[16,48,256]{2,1,0:T(8,128)(2,1)S(1)} collective-permute-done((bf16[16,48,256]{2,1,0:T(8,128)(2,1)S(1)}, bf16[16,48,256]{2,1,0:T(8,128)(2,1)S(1)}, u32[]{:S(2)}, u32[]{:S(2)}) %collective-permute-start.3) | collective-permute-done | bytes 393248 | tf_op jit(solution)/shard_map/ppermute | solution.py:518
  70.5 2.0 %shard_map.103 = f32[256,256]{1,0:T(8,128)} custom-call(s32[1]{0:T(128)} %bitcast.half_ref, bf16[2,8,48,256]{3,2,1,0:T(8,128)(2,1)S(1)} %bitcast.29, bf16[2,8,48,256]{3,2,1,0:T(8,128)(2,1)S(1)} %bitcast.30, bf16[4,384,512]{2,1,0:T(8,128)(2,1)S(1)} %copy-done.2, bf16[4,384,512]{2,1,0:T(8,128)(2,1)S(1)} %copy-done.1), custom_call_target="tpu_custom_call" | custom-call | tf_op jit(solution)/shard_map/pallas_call | solution.py:424
  (29 shorter events, 0.6 us)
Async XLA Ops:
  0.0 34.0 %copy-start = (f32[16,2]{0,1:T(2,128)S(1)}, f32[16,2]{0,1:T(2,128)}, u32[]{:S(2)}) copy-start(f32[16,2]{0,1:T(2,128)} %param.13) | copy-start | bytes 388
  0.0 29.0 %copy-start.4 = (bf16[2,2,256,512]{3,2,1,0:T(8,128)(2,1)S(1)}, bf16[2,2,256,512]{3,2,1,0:T(8,128)(2,1)}, u32[]{:S(2)}) copy-start(bf16[2,2,256,512]{3,2,1,0:T(8,128)(2,1)} %constant.104.clone) | copy-start | bytes 3145732
  0.0 26.3 %copy-start.6 = (s32[64]{0:T(128)S(1)}, s32[64]{0:T(128)}, u32[]{:S(2)}) copy-start(s32[64]{0:T(128)} %param.12) | copy-start | bytes 772
  0.0 26.3 %copy-start.5 = (s32[64,2]{0,1:T(2,128)S(1)}, s32[64,2]{0,1:T(2,128)}, u32[]{:S(2)}) copy-start(s32[64,2]{0,1:T(2,128)} %param.11) | copy-start | bytes 1540
  2.3 16.0 %all-to-all-start = ((bf16[4,8,1280]{2,1,0:T(8,128)(2,1)}), bf16[4,8,1280]{2,1,0:T(8,128)(2,1)S(1)}, u32[]{:S(2)}, u32[]{:S(2)}) async-start(bf16[4,8,1280]{2,1,0:T(8,128)(2,1)} %shard_map.100), calls=%async_computation | async-start | bytes 163840 | tf_op jit(solution)/shard_map/all_to_all | solution.py:484
  19.5 17.1 %all-to-all-start.1 = ((bf16[16,32,612]{2,1,0:T(8,128)(2,1)}), bf16[16,32,612]{2,1,0:T(8,128)(2,1)S(1)}, u32[]{:S(2)}, u32[]{:S(2)}) async-start(bf16[16,32,612]{2,1,0:T(8,128)(2,1)} %shard_map.101), calls=%async_computation.1 | async-start | bytes 1310720 | tf_op jit(solution)/shard_map/all_to_all | solution.py:492
  26.3 4.7 %collective-permute-start = (s32[64,3]{0,1:T(4,128)S(1)}, s32[64,3]{0,1:T(4,128)S(1)}, u32[]{:S(2)}, u32[]{:S(2)}) collective-permute-start(s32[64,3]{0,1:T(4,128)S(1)} %pad_add_fusion), channel_id=1, source_target_pairs={{0,64},{64,0},{128,192},{192,128},{1,65},{65,1},{129,193},{193,129... | collective-permute-start | bytes 2312 | tf_op jit(solution)/shard_map/ppermute | solution.py:455
  29.1 41.4 %copy-start.1 = (bf16[4,384,512]{2,1,0:T(8,128)(2,1)S(1)}, bf16[4,384,512]{2,1,0:T(8,128)(2,1)}, u32[]{:S(2)}) copy-start(bf16[4,384,512]{2,1,0:T(8,128)(2,1)} %constant.107.clone.low_ref) | copy-start | bytes 4718596
  31.1 2.8 %collective-permute-start.1 = (s32[128,3]{0,1:T(4,128)S(1)}, s32[128,3]{0,1:T(4,128)S(1)}, u32[]{:S(2)}, u32[]{:S(2)}) collective-permute-start(s32[128,3]{0,1:T(4,128)S(1)} %pad_add_fusion.1), channel_id=1, source_target_pairs={{0,128},{64,192},{128,0},{192,64},{1,129},{65,193},{129,1},{193,65... | collective-permute-start | bytes 4616 | tf_op jit(solution)/shard_map/ppermute | solution.py:455
  36.9 33.5 %copy-start.2 = (bf16[4,384,512]{2,1,0:T(8,128)(2,1)S(1)}, bf16[4,384,512]{2,1,0:T(8,128)(2,1)}, u32[]{:S(2)}) copy-start(bf16[4,384,512]{2,1,0:T(8,128)(2,1)} %constant.106.clone.high_ref) | copy-start | bytes 4718596
  36.9 5.3 %collective-permute-start.2 = (bf16[16,32,612]{2,1,0:T(8,128)(2,1)S(1)}, bf16[16,32,612]{2,1,0:T(8,128)(2,1)S(1)}, u32[]{:S(2)}, u32[]{:S(2)}) collective-permute-start(bf16[16,32,612]{2,1,0:T(8,128)(2,1)S(1)} %all-to-all-done.1.own_ref), channel_id=1, source_target_pairs={{0,64},{64,0},{128,192},{192,128},{1,65},{65,1},{129,193},{193,129... | collective-permute-start | bytes 1880072 | tf_op jit(solution)/shard_map/ppermute | solution.py:495
  42.3 1.0 %copy-start.3 = (bf16[768,256]{1,0:T(8,128)(2,1)S(1)}, bf16[768,256]{1,0:T(8,128)(2,1)}, u32[]{:S(2)}) copy-start(bf16[768,256]{1,0:T(8,128)(2,1)} %dynamic-slice_bitcast_fusion.2.back_ref) | copy-start | bytes 1179652
  67.4 3.0 %collective-permute-start.3 = (bf16[16,48,256]{2,1,0:T(8,128)(2,1)S(1)}, bf16[16,48,256]{2,1,0:T(8,128)(2,1)S(1)}, u32[]{:S(2)}, u32[]{:S(2)}) collective-permute-start(bf16[16,48,256]{2,1,0:T(8,128)(2,1)S(1)} %all_to_all.15), channel_id=1, source_target_pairs={{0,64},{64,0},{128,192},{192,128},{1,65},{65,1},{129,193},{193,129... | collective-permute-start | bytes 1179656 | tf_op jit(solution)/shard_map/ppermute | solution.py:518

commit v5 on v4

--- a/solution.py
+++ b/solution.py
@@ -83,19 +83,14 @@
 
 @functools.lru_cache(maxsize=None)
 def back_column_table():
-    chip, core, member = np.meshgrid(np.arange(2), np.arange(2), np.arange(GROUP), indexing="ij")
+    core, chip, member = np.meshgrid(np.arange(2), np.arange(2), np.arange(GROUP), indexing="ij")
     part = (chip * 2 * GROUP + member * 2 + core).reshape(-1)
     index = (part[:, None] * WIDE + np.arange(WIDE)[None, :]).reshape(-1) - BAND
     cols = np.arange(GRID // HALVES)
     angle = angles(index[:, None] * cols[None, :])
     angle = angle - (propagation_rate / GRID) * (index * index).astype(np.float64)[:, None]
     scale = 1.0 / (GRID * GRID)
-    cosine = (np.cos(angle) * scale).reshape(PARTS, WIDE, -1)
-    sine = (np.sin(angle) * scale).reshape(PARTS, WIDE, -1)
-    table = np.concatenate(
-        [np.concatenate([cosine, sine], 2), np.concatenate([-sine, cosine], 2)], 1
-    )
-    return two_parts(table.reshape(HALVES, PART_ROWS, 2 * GRID // HALVES))
+    return two_parts(np.concatenate([np.cos(angle), np.sin(angle)], 1) * scale)
 
 
 def chosen(rows, cols, source):
@@ -379,10 +374,10 @@
             pltpu.VMEM((2 * WIDE, KU), jnp.bfloat16),
             pltpu.VMEM((BLOCK, KU), jnp.bfloat16),
             pltpu.VMEM((BLOCK, KU), jnp.bfloat16),
-            pltpu.VMEM((TILTS * STEP, 128), jnp.float32),
-            pltpu.VMEM((TILTS * STEP, 128), jnp.float32),
-            pltpu.VMEM((GROUP * TILE * WIDE, 128), jnp.float32),
-            pltpu.VMEM((GROUP * TILE * WIDE, 128), jnp.float32),
+            pltpu.VMEM(((TILTS + 1) * STEP, 128), jnp.float32),
+            pltpu.VMEM(((TILTS + 1) * STEP, 128), jnp.float32),
+            pltpu.VMEM(((GROUP * TILE + 1) * WIDE, 128), jnp.float32),
+            pltpu.VMEM(((GROUP * TILE + 1) * WIDE, 128), jnp.float32),
         ],
         compiler_params=pltpu.CompilerParams(vmem_limit_bytes=30 * 1024 * 1024),
     )(
@@ -397,24 +392,27 @@
     )
 
 
-def probe_kernel(half_ref, own_ref, mate_ref, high_ref, low_ref, out_ref):
+def probe_kernel(half_ref, own_ref, mate_ref, high_ref, low_ref, out_ref, turned):
     half = half_ref[0]
-    index = lax.broadcasted_iota(jnp.int32, (1, WIDE, TILE * TILE), 1) + (3 * BAND)
+    core = half % 2
+    spots = TILE * TILE
+    index = lax.broadcasted_iota(jnp.int32, (1, 1, WIDE, spots), 2) + (3 * BAND)
     turns = jnp.bitwise_and(index * half, 3)
     cosine = jnp.where(turns == 0, 1.0, jnp.where(turns == 2, -1.0, 0.0))
     sine = jnp.where(turns == 1, 1.0, jnp.where(turns == 3, -1.0, 0.0))
-    probe = 0.0
-    for ref, core in ((own_ref, half % 2), (mate_ref, 1 - half % 2)):
-        for chip in range(2):
-            sums = ref[chip].astype(jnp.float32)
-            real, imag = sums[:, :WIDE], sums[:, WIDE:]
-            sums = jnp.concatenate([real * cosine - imag * sine, real * sine + imag * cosine], 1)
-            sums = sums.reshape(PART_ROWS, TILE * TILE).T.astype(jnp.bfloat16)
-            part = 2 * chip + core
-            probe = probe + jnp.dot(sums, high_ref[part], preferred_element_type=jnp.float32)
-            probe = probe + jnp.dot(sums, low_ref[part], preferred_element_type=jnp.float32)
+    for ref, place in ((own_ref, core), (mate_ref, 1 - core)):
+        sums = ref[...].astype(jnp.float32)
+        real, imag = sums[:, :, :WIDE], sums[:, :, WIDE:]
+        at = pl.multiple_of(place * PART_ROWS, 128)
+        for part, value in enumerate((real * cosine - imag * sine, real * sine + imag * cosine)):
+            turned[part * spots : (part + 1) * spots, pl.ds(at, PART_ROWS)] = (
+                value.astype(jnp.bfloat16).reshape(PART_ROWS, spots).T
+            )
+    both = jnp.dot(turned[...], high_ref[...], preferred_element_type=jnp.float32)
+    both = both + jnp.dot(turned[...], low_ref[...], preferred_element_type=jnp.float32)
     share = out_ref.shape[1]
-    real, imag = probe[:, :share], probe[:, share:]
+    real = both[:spots, :share] - both[spots:, share:]
+    imag = both[:spots, share:] + both[spots:, :share]
     out_ref[...] = real * real + imag * imag
 
 
@@ -426,6 +424,7 @@
         out_shape=jax.ShapeDtypeStruct((TILE * TILE, GRID // HALVES), jnp.float32),
         in_specs=[smem] + [vmem] * 4,
         out_specs=vmem,
+        scratch_shapes=[pltpu.VMEM((2 * TILE * TILE, 2 * PART_ROWS), jnp.bfloat16)],
         compiler_params=pltpu.CompilerParams(vmem_limit_bytes=24 * 1024 * 1024),
     )(half, own, mate, high, low)
 
@@ -492,6 +491,7 @@
     columns = lax.all_to_all(
         windows, "dev", 0, 0, tiled=True, axis_index_groups=groups("plane")
     )
+    columns, group_late = lax.optimization_barrier((columns, group))
     mate = lax.ppermute(columns, "half", [(i, i ^ 1) for i in range(HALVES)])
 
     notes = columns[:, : positions.shape[0], 2 * ROWS_IN :].astype(jnp.int32)
@@ -504,7 +504,7 @@
         lax.dynamic_index_in_dim(jnp.asarray(row_table()), place, 0, keepdims=False)
         for place in (core_late, 1 - core_late)
     ]
-    back = lax.dynamic_index_in_dim(jnp.asarray(back_row_table()), group, 0, keepdims=False)
+    back = lax.dynamic_index_in_dim(jnp.asarray(back_row_table()), group_late, 0, keepdims=False)
     shifts = (REACH - tilt_info[:, :2]).T + jnp.stack([jnp.int32(0), WIDE * core])[:, None]
     first = WIDE * (chip * 2 * GROUP + member * 2 + core) - BAND
     zero_row = BAND + REACH - 2 * WIDE * (chip * GROUP + member)

time: 72.9 us -> 72.6 us (level)
  local copies, waits for them, and re-layouts: 4.06 us -> 2.2 us
  waiting for transfers between devices: 12.9 us -> 13.7 us
    all_to_all x1, waiting for transfers between devices: 2.4 us -> 3.57 us  [local(): lax.all_to_all(windows, 'dev', 0, 0, tiled=True, axis_index_groups=groups...]
    ppermute x1, waiting for transfers between devices: 1.07 us -> 0.01 us  [local(): mate = lax.ppermute(columns, 'half', [(i, i ^ 1) for i in range(HALVES)])]
    unnamed x17 -> x15, local copies, waits for them, and re-layouts: 1.92 us -> 0.92 us
    squeeze x1, local copies, waits for them, and re-layouts: 1.9 us -> 1.03 us  [local(): lax.dynamic_index_in_dim(jnp.asarray(back_row_table()), group_late, 0, ke...]
    pallas_call x1, Pallas kernels: 12.5 us -> 13.3 us  [field_sums(): pl.pallas_call(field_kernel, out_shape=jax.ShapeDtypeStruct((2 * GROUP, 2...]
where the time goes in v5:
time: 72.6 us; the launch traced here: 72.2 us
  starting transfers between devices  24.3 us (33%)
  Pallas kernels  18.7 us (26%)
  waiting for transfers between devices  13.7 us (19%)
  blocking collectives  11.9 us (16%)
  local copies, waits for them, and re-layouts  2.2 us (3%)
  other arithmetic  1.06 us (1%)
    pallas_call x1, Pallas kernels, field_sums(): pl.pallas_call(field_kernel, out_shape=jax.ShapeDtypeStruct((2 * GROUP, 2...  13.3 us
    all_to_all x1, blocking collectives, local(): lax.all_to_all(sums, ('half', 'dev'), 0, 0, tiled=True, axis_index_groups...  11.9 us
    all_to_all x1, starting transfers between devices, local(): lax.all_to_all(piece, 'dev', 0, 0, tiled=True, axis_index_groups=groups('...  9.02 us
    all_to_all x1, starting transfers between devices, local(): lax.all_to_all(windows, 'dev', 0, 0, tiled=True, axis_index_groups=groups...  6.75 us
    all_to_all x1, waiting for transfers between devices, local(): lax.all_to_all(piece, 'dev', 0, 0, tiled=True, axis_index_groups=groups('...  6.15 us
    ppermute x1, starting transfers between devices, local(): mate = lax.ppermute(columns, 'half', [(i, i ^ 1) for i in range(HALVES)])  3.63 us
    all_to_all x1, waiting for transfers between devices, local(): lax.all_to_all(windows, 'dev', 0, 0, tiled=True, axis_index_groups=groups...  3.57 us
    ppermute x2, starting transfers between devices, doubled(): other = lax.ppermute(block, axis, [(i, i ^ stride) for i in range(size)])  3.44 us
  transfers between devices with their start and end apart: 6, of which 5 were waited for; matrix products, arithmetic and copies ran while one was open for 5% of the time, Pallas kernels for 0%

profile of v5, /device:TPU:1, one launch (start us, length us, event | category | flops | bytes accessed | tf_op | source)
XLA Modules:
  0.0 72.2 jit_solution(12209035217880866417)
XLA Ops:
  0.0 2.3 %shard_map.100 = bf16[4,8,1280]{2,1,0:T(8,128)(2,1)} custom-call(bf16[16,1024]{1,0:T(8,128)(2,1)} %field_ref.1, bf16[2,1024,256]{2,1,0:T(8,128)(2,1)} %constant.103.clone.table_ref), custom_call_target="tpu_custom_call" | custom-call | tf_op jit(solution)/shard_map/pallas_call | solution.py:154
  2.3 9.0 %all-to-all-start = ((bf16[4,8,1280]{2,1,0:T(8,128)(2,1)}), bf16[4,8,1280]{2,1,0:T(8,128)(2,1)S(1)}, u32[]{:S(2)}, u32[]{:S(2)}) async-start(bf16[4,8,1280]{2,1,0:T(8,128)(2,1)} %shard_map.100), calls=%async_computation | async-start | bytes 163840 | tf_op jit(solution)/shard_map/all_to_all | solution.py:483
  11.4 0.8 %copy.12.spot_ref = s32[16,2]{1,0:T(8,128)S(1)} copy(s32[16,2]{0,1:T(2,128)} %param.14) | data formatting | bytes 256 | tf_op args[4]
  12.2 6.1 %all-to-all-done = bf16[4,8,1280]{2,1,0:T(8,128)(2,1)S(1)} async-done(((bf16[4,8,1280]{2,1,0:T(8,128)(2,1)}), bf16[4,8,1280]{2,1,0:T(8,128)(2,1)S(1)}, u32[]{:S(2)}, u32[]{:S(2)}) %all-to-all-start) | async-done | bytes 81952 | tf_op jit(solution)/shard_map/all_to_all | solution.py:483
  18.3 1.2 %shard_map.101 = bf16[16,32,612]{2,1,0:T(8,128)(2,1)} custom-call(bf16[32,1280]{1,0:T(8,128)(2,1)S(1)} %bitcast.31, s32[16,2]{1,0:T(8,128)S(1)} %copy.12.spot_ref), custom_call_target="tpu_custom_call" | custom-call | tf_op jit(solution)/shard_map/pallas_call | solution.py:188
  19.5 6.8 %all-to-all-start.1 = ((bf16[16,32,612]{2,1,0:T(8,128)(2,1)}), bf16[16,32,612]{2,1,0:T(8,128)(2,1)S(1)}, u32[]{:S(2)}, u32[]{:S(2)}) async-start(bf16[16,32,612]{2,1,0:T(8,128)(2,1)} %shard_map.101), calls=%async_computation.1 | async-start | bytes 1310720 | tf_op jit(solution)/shard_map/all_to_all | solution.py:491
  26.3 2.7 %collective-permute-start = (s32[64,3]{0,1:T(4,128)S(1)}, s32[64,3]{0,1:T(4,128)S(1)}, u32[]{:S(2)}, u32[]{:S(2)}) collective-permute-start(s32[64,3]{0,1:T(4,128)S(1)} %pad_add_fusion), channel_id=1, source_target_pairs={{0,64},{64,0},{128,192},{192,128},{1,65},{65,1},{129,193},{193,129... | collective-permute-start | bytes 2312 | tf_op jit(solution)/shard_map/ppermute | solution.py:454
  29.1 0.7 collective-permute-done
  29.8 0.1 pad_add_fusion.1
  29.9 0.8 %collective-permute-start.1 = (s32[128,3]{0,1:T(4,128)S(1)}, s32[128,3]{0,1:T(4,128)S(1)}, u32[]{:S(2)}, u32[]{:S(2)}) collective-permute-start(s32[128,3]{0,1:T(4,128)S(1)} %pad_add_fusion.1), channel_id=1, source_target_pairs={{0,128},{64,192},{128,0},{192,64},{1,129},{65,193},{129,1},{193,65... | collective-permute-start | bytes 4616 | tf_op jit(solution)/shard_map/ppermute | solution.py:454
  30.7 1.9 %collective-permute-done.1 = s32[128,3]{0,1:T(4,128)S(1)} collective-permute-done((s32[128,3]{0,1:T(4,128)S(1)}, s32[128,3]{0,1:T(4,128)S(1)}, u32[]{:S(2)}, u32[]{:S(2)}) %collective-permute-start.1) | collective-permute-done | bytes 1568 | tf_op jit(solution)/shard_map/ppermute | solution.py:454
  32.8 0.2 fusion.2
  33.0 3.6 %all-to-all-done.1.own_ref = bf16[16,32,612]{2,1,0:T(8,128)(2,1)S(1)} async-done(((bf16[16,32,612]{2,1,0:T(8,128)(2,1)}), bf16[16,32,612]{2,1,0:T(8,128)(2,1)S(1)}, u32[]{:S(2)}, u32[]{:S(2)}) %all-to-all-start.1) | async-done | bytes 626720 | tf_op jit(solution)/shard_map/all_to_all | solution.py:491
  36.6 0.1 slice.41
  36.7 3.6 %collective-permute-start.2 = (bf16[16,32,612]{2,1,0:T(8,128)(2,1)S(1)}, bf16[16,32,612]{2,1,0:T(8,128)(2,1)}, u32[]{:S(2)}, u32[]{:S(2)}) collective-permute-start(bf16[16,32,612]{2,1,0:T(8,128)(2,1)S(1)} %all-to-all-done.1.own_ref), channel_id=1, source_target_pairs={{0,64},{64,0},{128,192},{192,128},{1,65},{65,1},{129,193},{193,129... | collective-permute-start | bytes 1880072 | tf_op jit(solution)/shard_map/ppermute | solution.py:495
  40.3 0.1 fusion.11
  40.5 0.1 copy.16
  40.6 0.6 negate_convert_fusion
  41.2 1.0 %dynamic-slice_bitcast_fusion.2.back_ref = bf16[768,256]{1,0:T(8,128)(2,1)S(1)} fusion(bf16[8,768,256]{2,1,0:T(8,128)(2,1)} %constant.105.clone, s32[]{:T(128)S(6)} %select_n.72), kind=kLoop, calls=%fused_computation.2 | loop fusion | bytes 786436 | tf_op jit(solution)/shard_map/jit(dynamic_index_in_dim)/squeeze | solution.py:507
  42.3 13.3 %shard_map.102 = bf16[16,48,256]{2,1,0:T(8,128)(2,1)S(1)} custom-call(s32[2,256]{1,0:T(2,128)S(1)} %fusion.8.shift_ref, s32[3]{0:T(128)S(1)} %pad_add_fusion.4.start_ref, bf16[16,32,612]{2,1,0:T(8,128)(2,1)S(1)} %all-to-all-done.1.own_ref, bf16[16,32,612]{2,1,0:T(8,128)(2,1)} %collective-permute-done.2.mate_ref, ...), custom_call_target="tpu_custom_call" | custom-call | tf_op jit(solution)/shard_map/pallas_call | solution.py:365
  55.5 11.9 %all_to_all.15 = bf16[16,48,256]{2,1,0:T(8,128)(2,1)S(1)} all-to-all(bf16[16,48,256]{2,1,0:T(8,128)(2,1)S(1)} %shard_map.102), channel_id=1, replica_groups={{0,1,2,3,4,5,6,7,128,129,130,131,132,133,134,135},{64,65,66,67,68,69,70..., dimensions={0} | all-to-all | bytes 786432 | tf_op jit(solution)/shard_map/all_to_all | solution.py:514
  67.4 1.4 %collective-permute-start.3 = (bf16[16,48,256]{2,1,0:T(8,128)(2,1)S(1)}, bf16[16,48,256]{2,1,0:T(8,128)(2,1)S(1)}, u32[]{:S(2)}, u32[]{:S(2)}) collective-permute-start(bf16[16,48,256]{2,1,0:T(8,128)(2,1)S(1)} %all_to_all.15), channel_id=1, source_target_pairs={{0,64},{64,0},{128,192},{192,128},{1,65},{65,1},{129,193},{193,129... | collective-permute-start | bytes 1179656 | tf_op jit(solution)/shard_map/ppermute | solution.py:518
  68.9 1.3 %collective-permute-done.3 = bf16[16,48,256]{2,1,0:T(8,128)(2,1)S(1)} collective-permute-done((bf16[16,48,256]{2,1,0:T(8,128)(2,1)S(1)}, bf16[16,48,256]{2,1,0:T(8,128)(2,1)S(1)}, u32[]{:S(2)}, u32[]{:S(2)}) %collective-permute-start.3) | collective-permute-done | bytes 393248 | tf_op jit(solution)/shard_map/ppermute | solution.py:518
  70.2 2.0 %shard_map.103 = f32[256,256]{1,0:T(8,128)} custom-call(s32[1]{0:T(128)} %bitcast.half_ref, bf16[2,8,48,256]{3,2,1,0:T(8,128)(2,1)S(1)} %bitcast.29, bf16[2,8,48,256]{3,2,1,0:T(8,128)(2,1)S(1)} %bitcast.30, bf16[768,512]{1,0:T(8,128)(2,1)S(1)} %copy-done.2, bf16[768,512]{1,0:T(8,128)(2,1)S(1)} %copy-done.1), custom_call_target="tpu_custom_call" | custom-call | tf_op jit(solution)/shard_map/pallas_call | solution.py:422
  (27 shorter events, 0.5 us)
Async XLA Ops:
  0.0 32.8 %copy-start = (f32[16,2]{0,1:T(2,128)S(1)}, f32[16,2]{0,1:T(2,128)}, u32[]{:S(2)}) copy-start(f32[16,2]{0,1:T(2,128)} %param.13) | copy-start | bytes 388
  0.0 29.0 %copy-start.3 = (bf16[2,2,256,512]{3,2,1,0:T(8,128)(2,1)S(1)}, bf16[2,2,256,512]{3,2,1,0:T(8,128)(2,1)}, u32[]{:S(2)}) copy-start(bf16[2,2,256,512]{3,2,1,0:T(8,128)(2,1)} %constant.104.clone) | copy-start | bytes 3145732
  0.0 26.3 %copy-start.5 = (s32[64]{0:T(128)S(1)}, s32[64]{0:T(128)}, u32[]{:S(2)}) copy-start(s32[64]{0:T(128)} %param.12) | copy-start | bytes 772
  0.0 26.3 %copy-start.4 = (s32[64,2]{0,1:T(2,128)S(1)}, s32[64,2]{0,1:T(2,128)}, u32[]{:S(2)}) copy-start(s32[64,2]{0,1:T(2,128)} %param.11) | copy-start | bytes 1540
  2.3 16.0 %all-to-all-start = ((bf16[4,8,1280]{2,1,0:T(8,128)(2,1)}), bf16[4,8,1280]{2,1,0:T(8,128)(2,1)S(1)}, u32[]{:S(2)}, u32[]{:S(2)}) async-start(bf16[4,8,1280]{2,1,0:T(8,128)(2,1)} %shard_map.100), calls=%async_computation | async-start | bytes 163840 | tf_op jit(solution)/shard_map/all_to_all | solution.py:483
  19.5 17.1 %all-to-all-start.1 = ((bf16[16,32,612]{2,1,0:T(8,128)(2,1)}), bf16[16,32,612]{2,1,0:T(8,128)(2,1)S(1)}, u32[]{:S(2)}, u32[]{:S(2)}) async-start(bf16[16,32,612]{2,1,0:T(8,128)(2,1)} %shard_map.101), calls=%async_computation.1 | async-start | bytes 1310720 | tf_op jit(solution)/shard_map/all_to_all | solution.py:491
  26.3 3.5 %collective-permute-start = (s32[64,3]{0,1:T(4,128)S(1)}, s32[64,3]{0,1:T(4,128)S(1)}, u32[]{:S(2)}, u32[]{:S(2)}) collective-permute-start(s32[64,3]{0,1:T(4,128)S(1)} %pad_add_fusion), channel_id=1, source_target_pairs={{0,64},{64,0},{128,192},{192,128},{1,65},{65,1},{129,193},{193,129... | collective-permute-start | bytes 2312 | tf_op jit(solution)/shard_map/ppermute | solution.py:454
  29.9 2.8 %collective-permute-start.1 = (s32[128,3]{0,1:T(4,128)S(1)}, s32[128,3]{0,1:T(4,128)S(1)}, u32[]{:S(2)}, u32[]{:S(2)}) collective-permute-start(s32[128,3]{0,1:T(4,128)S(1)} %pad_add_fusion.1), channel_id=1, source_target_pairs={{0,128},{64,192},{128,0},{192,64},{1,129},{65,193},{129,1},{193,65... | collective-permute-start | bytes 4616 | tf_op jit(solution)/shard_map/ppermute | solution.py:454
  36.6 33.7 %copy-start.1 = (bf16[768,512]{1,0:T(8,128)(2,1)S(1)}, bf16[768,512]{1,0:T(8,128)(2,1)}, u32[]{:S(2)}) copy-start(bf16[768,512]{1,0:T(8,128)(2,1)} %constant.107.clone.low_ref) | copy-start | bytes 2359300
  36.6 33.7 %copy-start.2 = (bf16[768,512]{1,0:T(8,128)(2,1)S(1)}, bf16[768,512]{1,0:T(8,128)(2,1)}, u32[]{:S(2)}) copy-start(bf16[768,512]{1,0:T(8,128)(2,1)} %constant.106.clone.high_ref) | copy-start | bytes 2359300
  36.7 5.6 %collective-permute-start.2 = (bf16[16,32,612]{2,1,0:T(8,128)(2,1)S(1)}, bf16[16,32,612]{2,1,0:T(8,128)(2,1)}, u32[]{:S(2)}, u32[]{:S(2)}) collective-permute-start(bf16[16,32,612]{2,1,0:T(8,128)(2,1)S(1)} %all-to-all-done.1.own_ref), channel_id=1, source_target_pairs={{0,64},{64,0},{128,192},{192,128},{1,65},{65,1},{129,193},{193,129... | collective-permute-start | bytes 1880072 | tf_op jit(solution)/shard_map/ppermute | solution.py:495
  67.4 2.8 %collective-permute-start.3 = (bf16[16,48,256]{2,1,0:T(8,128)(2,1)S(1)}, bf16[16,48,256]{2,1,0:T(8,128)(2,1)S(1)}, u32[]{:S(2)}, u32[]{:S(2)}) collective-permute-start(bf16[16,48,256]{2,1,0:T(8,128)(2,1)S(1)} %all_to_all.15), channel_id=1, source_target_pairs={{0,64},{64,0},{128,192},{192,128},{1,65},{65,1},{129,193},{193,129... | collective-permute-start | bytes 1179656 | tf_op jit(solution)/shard_map/ppermute | solution.py:518

commit v6 on v5

--- a/solution.py
+++ b/solution.py
@@ -318,11 +318,14 @@
     def block(turn, carry):
         fill(2 * turn + 1, rows_b)
         multiply(2 * turn, rows_a)
-        fill(jnp.minimum(2 * turn + 2, steps - 1), rows_a)
+        fill(2 * turn + 2, rows_a)
         multiply(2 * turn + 1, rows_b)
         return carry
 
-    lax.fori_loop(0, steps // 2, block, 0)
+    lax.fori_loop(0, steps // 2 - 1, block, 0)
+    fill(steps - 1, rows_b)
+    multiply(steps - 2, rows_a)
+    multiply(steps - 1, rows_b)
 
     count = GROUP * TILE
     for col in range(WIDE):

time: 72.6 us -> 72.6 us (level)
  no operation moved by 1% of the time
where the time goes in v6:
time: 72.6 us; the launch traced here: 72.1 us
  starting transfers between devices  24.2 us (33%)
  Pallas kernels  18.6 us (26%)
  waiting for transfers between devices  13.7 us (19%)
  blocking collectives  11.9 us (16%)
  local copies, waits for them, and re-layouts  2.2 us (3%)
  other arithmetic  1.06 us (1%)
    pallas_call x1, Pallas kernels, field_sums(): pl.pallas_call(field_kernel, out_shape=jax.ShapeDtypeStruct((2 * GROUP, 2...  13.2 us
    all_to_all x1, blocking collectives, local(): lax.all_to_all(sums, ('half', 'dev'), 0, 0, tiled=True, axis_index_groups...  11.9 us
    all_to_all x1, starting transfers between devices, local(): lax.all_to_all(piece, 'dev', 0, 0, tiled=True, axis_index_groups=groups('...  9.02 us
    all_to_all x1, starting transfers between devices, local(): lax.all_to_all(windows, 'dev', 0, 0, tiled=True, axis_index_groups=groups...  6.75 us
    all_to_all x1, waiting for transfers between devices, local(): lax.all_to_all(piece, 'dev', 0, 0, tiled=True, axis_index_groups=groups('...  6.15 us
    ppermute x1, starting transfers between devices, local(): mate = lax.ppermute(columns, 'half', [(i, i ^ 1) for i in range(HALVES)])  3.63 us
    all_to_all x1, waiting for transfers between devices, local(): lax.all_to_all(windows, 'dev', 0, 0, tiled=True, axis_index_groups=groups...  3.57 us
    ppermute x2, starting transfers between devices, doubled(): other = lax.ppermute(block, axis, [(i, i ^ stride) for i in range(size)])  3.44 us
  transfers between devices with their start and end apart: 6, of which 5 were waited for; matrix products, arithmetic and copies ran while one was open for 5% of the time, Pallas kernels for 0%

profile of v6, /device:TPU:1, one launch (start us, length us, event | category | flops | bytes accessed | tf_op | source)
XLA Modules:
  0.0 72.1 jit_solution(15444902818239776374)
XLA Ops:
  0.0 2.3 %shard_map.100 = bf16[4,8,1280]{2,1,0:T(8,128)(2,1)} custom-call(bf16[16,1024]{1,0:T(8,128)(2,1)} %field_ref.1, bf16[2,1024,256]{2,1,0:T(8,128)(2,1)} %constant.103.clone.table_ref), custom_call_target="tpu_custom_call" | custom-call | tf_op jit(solution)/shard_map/pallas_call | solution.py:154
  2.3 9.0 %all-to-all-start = ((bf16[4,8,1280]{2,1,0:T(8,128)(2,1)}), bf16[4,8,1280]{2,1,0:T(8,128)(2,1)S(1)}, u32[]{:S(2)}, u32[]{:S(2)}) async-start(bf16[4,8,1280]{2,1,0:T(8,128)(2,1)} %shard_map.100), calls=%async_computation | async-start | bytes 163840 | tf_op jit(solution)/shard_map/all_to_all | solution.py:486
  11.4 0.8 %copy.12.spot_ref = s32[16,2]{1,0:T(8,128)S(1)} copy(s32[16,2]{0,1:T(2,128)} %param.14) | data formatting | bytes 256 | tf_op args[4]
  12.2 6.1 %all-to-all-done = bf16[4,8,1280]{2,1,0:T(8,128)(2,1)S(1)} async-done(((bf16[4,8,1280]{2,1,0:T(8,128)(2,1)}), bf16[4,8,1280]{2,1,0:T(8,128)(2,1)S(1)}, u32[]{:S(2)}, u32[]{:S(2)}) %all-to-all-start) | async-done | bytes 81952 | tf_op jit(solution)/shard_map/all_to_all | solution.py:486
  18.3 1.2 %shard_map.101 = bf16[16,32,612]{2,1,0:T(8,128)(2,1)} custom-call(bf16[32,1280]{1,0:T(8,128)(2,1)S(1)} %bitcast.31, s32[16,2]{1,0:T(8,128)S(1)} %copy.12.spot_ref), custom_call_target="tpu_custom_call" | custom-call | tf_op jit(solution)/shard_map/pallas_call | solution.py:188
  19.5 6.8 %all-to-all-start.1 = ((bf16[16,32,612]{2,1,0:T(8,128)(2,1)}), bf16[16,32,612]{2,1,0:T(8,128)(2,1)S(1)}, u32[]{:S(2)}, u32[]{:S(2)}) async-start(bf16[16,32,612]{2,1,0:T(8,128)(2,1)} %shard_map.101), calls=%async_computation.1 | async-start | bytes 1310720 | tf_op jit(solution)/shard_map/all_to_all | solution.py:494
  26.3 2.7 %collective-permute-start = (s32[64,3]{0,1:T(4,128)S(1)}, s32[64,3]{0,1:T(4,128)S(1)}, u32[]{:S(2)}, u32[]{:S(2)}) collective-permute-start(s32[64,3]{0,1:T(4,128)S(1)} %pad_add_fusion), channel_id=1, source_target_pairs={{0,64},{64,0},{128,192},{192,128},{1,65},{65,1},{129,193},{193,129... | collective-permute-start | bytes 2312 | tf_op jit(solution)/shard_map/ppermute | solution.py:457
  29.1 0.7 %collective-permute-done = s32[64,3]{0,1:T(4,128)S(1)} collective-permute-done((s32[64,3]{0,1:T(4,128)S(1)}, s32[64,3]{0,1:T(4,128)S(1)}, u32[]{:S(2)}, u32[]{:S(2)}) %collective-permute-start) | collective-permute-done | bytes 800 | tf_op jit(solution)/shard_map/ppermute | solution.py:457
  29.8 0.1 pad_add_fusion.1
  29.9 0.8 %collective-permute-start.1 = (s32[128,3]{0,1:T(4,128)S(1)}, s32[128,3]{0,1:T(4,128)S(1)}, u32[]{:S(2)}, u32[]{:S(2)}) collective-permute-start(s32[128,3]{0,1:T(4,128)S(1)} %pad_add_fusion.1), channel_id=1, source_target_pairs={{0,128},{64,192},{128,0},{192,64},{1,129},{65,193},{129,1},{193,65... | collective-permute-start | bytes 4616 | tf_op jit(solution)/shard_map/ppermute | solution.py:457
  30.7 1.9 %collective-permute-done.1 = s32[128,3]{0,1:T(4,128)S(1)} collective-permute-done((s32[128,3]{0,1:T(4,128)S(1)}, s32[128,3]{0,1:T(4,128)S(1)}, u32[]{:S(2)}, u32[]{:S(2)}) %collective-permute-start.1) | collective-permute-done | bytes 1568 | tf_op jit(solution)/shard_map/ppermute | solution.py:457
  32.8 0.2 fusion.2
  33.0 3.6 %all-to-all-done.1.own_ref = bf16[16,32,612]{2,1,0:T(8,128)(2,1)S(1)} async-done(((bf16[16,32,612]{2,1,0:T(8,128)(2,1)}), bf16[16,32,612]{2,1,0:T(8,128)(2,1)S(1)}, u32[]{:S(2)}, u32[]{:S(2)}) %all-to-all-start.1) | async-done | bytes 626720 | tf_op jit(solution)/shard_map/all_to_all | solution.py:494
  36.6 0.1 slice.41
  36.7 3.6 %collective-permute-start.2 = (bf16[16,32,612]{2,1,0:T(8,128)(2,1)S(1)}, bf16[16,32,612]{2,1,0:T(8,128)(2,1)}, u32[]{:S(2)}, u32[]{:S(2)}) collective-permute-start(bf16[16,32,612]{2,1,0:T(8,128)(2,1)S(1)} %all-to-all-done.1.own_ref), channel_id=1, source_target_pairs={{0,64},{64,0},{128,192},{192,128},{1,65},{65,1},{129,193},{193,129... | collective-permute-start | bytes 1880072 | tf_op jit(solution)/shard_map/ppermute | solution.py:498
  40.3 0.1 fusion.11
  40.5 0.1 copy.16
  40.6 0.6 negate_convert_fusion
  41.2 1.0 %dynamic-slice_bitcast_fusion.2.back_ref = bf16[768,256]{1,0:T(8,128)(2,1)S(1)} fusion(bf16[8,768,256]{2,1,0:T(8,128)(2,1)} %constant.105.clone, s32[]{:T(128)S(6)} %select_n.72), kind=kLoop, calls=%fused_computation.2 | loop fusion | bytes 786436 | tf_op jit(solution)/shard_map/jit(dynamic_index_in_dim)/squeeze | solution.py:510
  42.3 13.2 %shard_map.102 = bf16[16,48,256]{2,1,0:T(8,128)(2,1)S(1)} custom-call(s32[2,256]{1,0:T(2,128)S(1)} %fusion.8.shift_ref, s32[3]{0:T(128)S(1)} %pad_add_fusion.4.start_ref, bf16[16,32,612]{2,1,0:T(8,128)(2,1)S(1)} %all-to-all-done.1.own_ref, bf16[16,32,612]{2,1,0:T(8,128)(2,1)} %collective-permute-done.2.mate_ref, ...), custom_call_target="tpu_custom_call" | custom-call | tf_op jit(solution)/shard_map/pallas_call | solution.py:368
  55.4 11.9 %all_to_all.15 = bf16[16,48,256]{2,1,0:T(8,128)(2,1)S(1)} all-to-all(bf16[16,48,256]{2,1,0:T(8,128)(2,1)S(1)} %shard_map.102), channel_id=1, replica_groups={{0,1,2,3,4,5,6,7,128,129,130,131,132,133,134,135},{64,65,66,67,68,69,70..., dimensions={0} | all-to-all | bytes 786432 | tf_op jit(solution)/shard_map/all_to_all | solution.py:517
  67.4 1.4 %collective-permute-start.3 = (bf16[16,48,256]{2,1,0:T(8,128)(2,1)S(1)}, bf16[16,48,256]{2,1,0:T(8,128)(2,1)S(1)}, u32[]{:S(2)}, u32[]{:S(2)}) collective-permute-start(bf16[16,48,256]{2,1,0:T(8,128)(2,1)S(1)} %all_to_all.15), channel_id=1, source_target_pairs={{0,64},{64,0},{128,192},{192,128},{1,65},{65,1},{129,193},{193,129... | collective-permute-start | bytes 1179656 | tf_op jit(solution)/shard_map/ppermute | solution.py:521
  68.8 1.3 %collective-permute-done.3 = bf16[16,48,256]{2,1,0:T(8,128)(2,1)S(1)} collective-permute-done((bf16[16,48,256]{2,1,0:T(8,128)(2,1)S(1)}, bf16[16,48,256]{2,1,0:T(8,128)(2,1)S(1)}, u32[]{:S(2)}, u32[]{:S(2)}) %collective-permute-start.3) | collective-permute-done | bytes 393248 | tf_op jit(solution)/shard_map/ppermute | solution.py:521
  70.1 2.0 %shard_map.103 = f32[256,256]{1,0:T(8,128)} custom-call(s32[1]{0:T(128)} %bitcast.half_ref, bf16[2,8,48,256]{3,2,1,0:T(8,128)(2,1)S(1)} %bitcast.29, bf16[2,8,48,256]{3,2,1,0:T(8,128)(2,1)S(1)} %bitcast.30, bf16[768,512]{1,0:T(8,128)(2,1)S(1)} %copy-done.2, bf16[768,512]{1,0:T(8,128)(2,1)S(1)} %copy-done.1), custom_call_target="tpu_custom_call" | custom-call | tf_op jit(solution)/shard_map/pallas_call | solution.py:425
  (27 shorter events, 0.5 us)
Async XLA Ops:
  0.0 32.8 %copy-start = (f32[16,2]{0,1:T(2,128)S(1)}, f32[16,2]{0,1:T(2,128)}, u32[]{:S(2)}) copy-start(f32[16,2]{0,1:T(2,128)} %param.13) | copy-start | bytes 388
  0.0 29.0 %copy-start.3 = (bf16[2,2,256,512]{3,2,1,0:T(8,128)(2,1)S(1)}, bf16[2,2,256,512]{3,2,1,0:T(8,128)(2,1)}, u32[]{:S(2)}) copy-start(bf16[2,2,256,512]{3,2,1,0:T(8,128)(2,1)} %constant.104.clone) | copy-start | bytes 3145732
  0.0 26.3 %copy-start.5 = (s32[64]{0:T(128)S(1)}, s32[64]{0:T(128)}, u32[]{:S(2)}) copy-start(s32[64]{0:T(128)} %param.12) | copy-start | bytes 772
  0.0 26.3 %copy-start.4 = (s32[64,2]{0,1:T(2,128)S(1)}, s32[64,2]{0,1:T(2,128)}, u32[]{:S(2)}) copy-start(s32[64,2]{0,1:T(2,128)} %param.11) | copy-start | bytes 1540
  2.3 16.0 %all-to-all-start = ((bf16[4,8,1280]{2,1,0:T(8,128)(2,1)}), bf16[4,8,1280]{2,1,0:T(8,128)(2,1)S(1)}, u32[]{:S(2)}, u32[]{:S(2)}) async-start(bf16[4,8,1280]{2,1,0:T(8,128)(2,1)} %shard_map.100), calls=%async_computation | async-start | bytes 163840 | tf_op jit(solution)/shard_map/all_to_all | solution.py:486
  19.5 17.1 %all-to-all-start.1 = ((bf16[16,32,612]{2,1,0:T(8,128)(2,1)}), bf16[16,32,612]{2,1,0:T(8,128)(2,1)S(1)}, u32[]{:S(2)}, u32[]{:S(2)}) async-start(bf16[16,32,612]{2,1,0:T(8,128)(2,1)} %shard_map.101), calls=%async_computation.1 | async-start | bytes 1310720 | tf_op jit(solution)/shard_map/all_to_all | solution.py:494
  26.3 3.5 %collective-permute-start = (s32[64,3]{0,1:T(4,128)S(1)}, s32[64,3]{0,1:T(4,128)S(1)}, u32[]{:S(2)}, u32[]{:S(2)}) collective-permute-start(s32[64,3]{0,1:T(4,128)S(1)} %pad_add_fusion), channel_id=1, source_target_pairs={{0,64},{64,0},{128,192},{192,128},{1,65},{65,1},{129,193},{193,129... | collective-permute-start | bytes 2312 | tf_op jit(solution)/shard_map/ppermute | solution.py:457
  29.9 2.8 %collective-permute-start.1 = (s32[128,3]{0,1:T(4,128)S(1)}, s32[128,3]{0,1:T(4,128)S(1)}, u32[]{:S(2)}, u32[]{:S(2)}) collective-permute-start(s32[128,3]{0,1:T(4,128)S(1)} %pad_add_fusion.1), channel_id=1, source_target_pairs={{0,128},{64,192},{128,0},{192,64},{1,129},{65,193},{129,1},{193,65... | collective-permute-start | bytes 4616 | tf_op jit(solution)/shard_map/ppermute | solution.py:457
  36.6 33.6 %copy-start.1 = (bf16[768,512]{1,0:T(8,128)(2,1)S(1)}, bf16[768,512]{1,0:T(8,128)(2,1)}, u32[]{:S(2)}) copy-start(bf16[768,512]{1,0:T(8,128)(2,1)} %constant.107.clone.low_ref) | copy-start | bytes 2359300
  36.6 33.6 %copy-start.2 = (bf16[768,512]{1,0:T(8,128)(2,1)S(1)}, bf16[768,512]{1,0:T(8,128)(2,1)}, u32[]{:S(2)}) copy-start(bf16[768,512]{1,0:T(8,128)(2,1)} %constant.106.clone.high_ref) | copy-start | bytes 2359300
  36.7 5.6 %collective-permute-start.2 = (bf16[16,32,612]{2,1,0:T(8,128)(2,1)S(1)}, bf16[16,32,612]{2,1,0:T(8,128)(2,1)}, u32[]{:S(2)}, u32[]{:S(2)}) collective-permute-start(bf16[16,32,612]{2,1,0:T(8,128)(2,1)S(1)} %all-to-all-done.1.own_ref), channel_id=1, source_target_pairs={{0,64},{64,0},{128,192},{192,128},{1,65},{65,1},{129,193},{193,129... | collective-permute-start | bytes 1880072 | tf_op jit(solution)/shard_map/ppermute | solution.py:498
  67.4 2.7 %collective-permute-start.3 = (bf16[16,48,256]{2,1,0:T(8,128)(2,1)S(1)}, bf16[16,48,256]{2,1,0:T(8,128)(2,1)S(1)}, u32[]{:S(2)}, u32[]{:S(2)}) collective-permute-start(bf16[16,48,256]{2,1,0:T(8,128)(2,1)S(1)} %all_to_all.15), channel_id=1, source_target_pairs={{0,64},{64,0},{128,192},{192,128},{1,65},{65,1},{129,193},{193,129... | collective-permute-start | bytes 1179656 | tf_op jit(solution)/shard_map/ppermute | solution.py:521
